TPU v7x, 256 devices: a whole 4x4x8 slice. The times are simulated.
256 devices in a mesh: shot: 8 (over x, core), rcv: 32 (over y, z).
Axes of the slice: x: 4, y: 4, z: 8, core: 2. Of those that a mesh axis runs over, the one named last changes fastest.
Arguments:
- response: bfloat16 [256, 128, 64], P('shot', 'rcv'), may hold values from -0.0625 to 0.0625
- traces: bfloat16 [128, 256, 512], P('shot', 'rcv'), may hold values from -6 to 6
Outputs:
- multiples: bfloat16 [256, 256, 512], P('shot', 'rcv')
All inputs are finite; a program needn't handle non-finite values.
Results may differ from a plain program's by a relative error of at most 0.001.
Values may be sent and summed in bfloat16 or wider, within the bound.
No kernel may reach another device: no remote copies, remote signals or barrier semaphores. Data moves between devices by JAX's collectives and lax.ppermute only.
A program may use at most 256 MiB of HBM per device.

v0:
```python
import jax
import jax.numpy as jnp
from jax import lax
from jax.sharding import PartitionSpec as P


def banded(resp_piece):
    shots_here = resp_piece.shape[0]
    rows_in = resp_piece.shape[1]
    tap_count = resp_piece.shape[2]
    reversed_taps = jnp.transpose(resp_piece[:, :, ::-1], (2, 0, 1))
    lead = jnp.zeros((1, shots_here, rows_in), resp_piece.dtype)
    trail = jnp.zeros((tap_count, shots_here, rows_in), resp_piece.dtype)
    pattern = jnp.concatenate([lead, reversed_taps, trail], axis=0)
    repeated = jnp.tile(pattern, (tap_count, 1, 1))[: 2 * tap_count * tap_count]
    return repeated.reshape(tap_count, 2 * tap_count, shots_here, rows_in)


def contract(resp_piece, data_piece):
    shots_here = resp_piece.shape[0]
    tap_count = resp_piece.shape[2]
    rows_in = data_piece.shape[0]
    rcv_here = data_piece.shape[1]
    samples = data_piece.shape[2]
    blocks = samples // tap_count
    band = banded(resp_piece)
    padded = jnp.pad(data_piece, ((0, 0), (0, 0), (tap_count, 0)))
    tiles = padded.reshape(rows_in, rcv_here, blocks + 1, tap_count)
    windows = jnp.concatenate([tiles[:, :, :blocks], tiles[:, :, 1:]], axis=3)
    product = jnp.einsum("uvsk,krbv->srbu", band, windows, preferred_element_type=jnp.float32)
    return product.reshape(shots_here, rcv_here * samples)


def shards(response, traces):
    shots_here = response.shape[0]
    rcv_here = traces.shape[1]
    samples = traces.shape[2]
    responses_all = lax.all_gather(response, "rcv", axis=1, tiled=True)
    running = contract(responses_all, lax.all_gather(traces, "shot", axis=0, tiled=True))
    return running.reshape(shots_here, rcv_here, samples).astype(jnp.bfloat16)


def solution(mesh):
    placed = (P("shot", "rcv", None), P("shot", "rcv", None))
    return jax.shard_map(
        shards, mesh=mesh, in_specs=placed, out_specs=P("shot", "rcv", None), check_vma=False
    )
```

profile of v0, /device:TPU:6, one launch (start us, length us, event | category | flops | bytes accessed | tf_op | source)
XLA Modules:
  0.0 341.1 jit_solution(6631717501399990618)
XLA Ops:
  6.5 0.0 all-gather.2.cloned.1.call-start
  6.5 0.7 all-gather.2.cloned.1.call-update
  7.3 0.8 copy.14
  8.0 53.6 %all_gather.7 = bf16[32,128,64]{2,0,1:T(8,128)(2,1)S(1)} all-gather(bf16[32,4,64]{2,0,1:T(8,128)(2,1)S(1)} %copy.14), channel_id=1, replica_groups=mesh['shot'=8,'rcv'=32] {'rcv'}, dimensions={1}, use_global_device_ids=true | all-gather | bytes 540672 | tf_op jit(solution)/shard_map/all_gather | solution.py:38
  61.6 0.8 rev.3
  62.4 0.1 pad.7.clone
  62.5 0.9 maximum_maximum_fusion
  63.4 2.4 copy.15
  65.8 28.0 %tile.4 = bf16[64,129,32,128]{3,2,1,0:T(8,128)(2,1)} broadcast(bf16[129,32,128]{2,1,0:T(8,128)(2,1)S(1)} %copy.15), dimensions={1,2,3} | broadcast | bytes 68689920 | tf_op jit(solution)/shard_map/tile | solution.py:15
  93.8 44.3 %slice.14 = bf16[8192,32,128]{2,1,0:T(8,128)(2,1)} slice(bf16[8256,32,128]{2,1,0:T(8,128)(2,1)} %bitcast.4), slice={[0:8192], [0:32], [0:128]} | slice | bytes 134217728 | tf_op jit(solution)/shard_map/slice | solution.py:15
  138.1 150.2 %copy.20 = bf16[64,128,32,128]{1,0,3,2:T(8,128)(2,1)} copy(bf16[64,128,32,128]{3,2,1,0:T(8,128)(2,1)} %bitcast.5) | data formatting | bytes 134217728 | tf_op jit(solution)/shard_map/reshape | solution.py:16
  288.3 0.0 all-gather.2.cloned.1.call-done
  288.3 1.9 copy.11
  290.3 0.1 pad.4
  290.4 0.5 fusion.14
  290.9 2.0 copy.22
  292.9 0.0 copy-start
  292.9 2.1 copy.21
  295.0 0.0 copy-done
  295.0 38.1 %fusion.10 = bf16[32,8,8,64]{3,2,0,1:T(8,128)(2,1)S(1)} fusion(bf16[64,128,32,128]{1,0,3,2:T(8,128)(2,1)} %copy.20, bf16[128,8,8,64]{3,2,0,1:T(8,128)(2,1)S(1)} %copy-done, bf16[128,8,8,64]{3,2,0,1:T(8,128)(2,1)} %copy.21), kind=kOutput, calls=%fused_computation.8 | convolution fusion | flops 4299292672 | bytes 69468160 | tf_op jit(solution)/shard_map/uvsk,krbv->srbu/dot_general | solution.py:30
  333.1 0.3 convert_element_type.13
  333.4 0.9 copy.17
  (2 shorter events, 0.0 us)
Async XLA Ops:
  6.5 281.8 %all-gather.2.cloned.1.call-start = ((), (), s32[]{:S(2)}) async-start(), calls=%async_computation | async-start | bytes 1179648 | tf_op jit(solution)/shard_map/all_gather | solution.py:39
  292.9 2.1 copy-start
Sparse Core Ops, SparseCore 0:
  9.2 27.2 all-gather.1
where the time goes:
time: 342 us; the launch traced here: 341 us
  local copies, waits for them, and re-layouts  234 us (68%)
  blocking collectives  53.6 us (16%)
  matrix products  38.1 us (11%)
  between operations  13.5 us (4%)
    reshape x1, local copies, waits for them, and re-layouts, banded(): return repeated.reshape(tap_count, 2 * tap_count, shots_here, rows_in)  150 us
    all_gather x1, blocking collectives, shards(): responses_all = lax.all_gather(response, 'rcv', axis=1, tiled=True)  53.6 us
    slice x1, local copies, waits for them, and re-layouts, banded(): repeated = jnp.tile(pattern, (tap_count, 1, 1))[:2 * tap_count * tap_count]  44.3 us
    dot_general x1, matrix products, contract(): jnp.einsum('uvsk,krbv->srbu', band, windows, preferred_element_type=jnp.f...  38.1 us
    another operation x1, local copies, waits for them, and re-layouts, banded(): repeated = jnp.tile(pattern, (tap_count, 1, 1))[:2 * tap_count * tap_count]  28 us
  transfers between devices with their start and end apart: 1, of which 0 were waited for; matrix products, arithmetic and copies ran while one was open for 67% of the time, Pallas kernels for 0%

commit v1 on v0

v1 whole, which is shorter than its diff:
```python
import functools

import jax
import jax.numpy as jnp
from jax import lax
from jax.experimental import pallas as pl
from jax.experimental.pallas import tpu as pltpu
from jax.sharding import PartitionSpec as P

PHASES = 8
RING4 = (0, 1, -1, -2)
RING8 = (0, 1, -1, -2, 3, 2, 4, 5)


def spread(value, axis, partner):
    size = lax.axis_size(axis)
    return lax.ppermute(value, axis, [(i, partner(i)) for i in range(size)])


def sign(coordinate):
    return 1 - 2 * (coordinate % 2)


def gather_response(piece):
    def along_z(step):
        def partner(i):
            y, z = i // 8, i % 8
            return y * 8 + step(z) % 8

        return partner

    def along_y(step):
        def partner(i):
            y, z = i // 8, i % 8
            return (step(y) % 4) * 8 + z

        return partner

    held = piece[None]
    for step in (lambda z: z + sign(z), lambda z: z - sign(z), lambda z: z + 3 * sign(z)):
        held = jnp.concatenate([held, spread(held, "rcv", along_z(step))], axis=0)
    return [held] + [
        spread(held, "rcv", along_y(lambda y, offset=offset: y + offset)) for offset in (1, 3, 2)
    ]


def gather_traces(piece):
    def along_x(offset):
        return lambda i: ((i // 2 + offset) % 4) * 2 + i % 2

    mine = [piece] + [spread(piece, "shot", along_x(offset)) for offset in (1, 3, 2)]
    other = [spread(block, "shot", lambda i: i ^ 1) for block in mine]
    return mine + other


def kernel(slots, r0, r1, r2, r3, t0, t1, t2, t3, t4, t5, t6, t7, out, traces_pad, band, total):
    responses = (r0, r1, r2, r3)
    traces = (t0, t1, t2, t3, t4, t5, t6, t7)
    for slot in range(8):
        block = slots[slot]
        traces_pad[block, :64, :] = jnp.zeros((64, 128), jnp.bfloat16)
        traces_pad[block, 64:, :] = traces[slot][...]
    for y_slot in range(4):
        y_here = slots[8 + y_slot]
        for half in range(2):
            block = y_here * 2 + half
            rows = jnp.concatenate(
                [responses[y_slot][slots[12 + half * 4 + q]].astype(jnp.float32) for q in range(4)],
                axis=0,
            )
            wide = jnp.concatenate([rows, jnp.zeros((16, 384), jnp.float32)], axis=1)
            for shift in range(4):
                band[block, shift * 16 : shift * 16 + 16, :] = pltpu.roll(
                    wide, 128 + 32 * shift, 1
                ).astype(jnp.bfloat16)
    for pair in range(4):
        even_rows, odd_rows, sides = [], [], []
        for group in range(5):
            sides.append(
                jnp.concatenate(
                    [traces_pad[2 * pair + i, 64 - 16 * group : 576 - 16 * group, :] for i in range(2)],
                    axis=1,
                )
            )
            for rows, step in ((even_rows, 2 * group), (odd_rows, 2 * group + 1)):
                if step <= 8:
                    for i in range(2):
                        for late in range(2):
                            first = (2 * step - late + 1) * 128
                            rows.append(band[2 * pair + i, :, first : first + 256])
        even = jnp.dot(
            jnp.concatenate(sides, axis=1),
            jnp.concatenate(even_rows, axis=0),
            preferred_element_type=jnp.float32,
        )
        odd = jnp.dot(
            jnp.concatenate(sides[:4], axis=1),
            jnp.concatenate(odd_rows, axis=0),
            preferred_element_type=jnp.float32,
        )
        if pair == 0:
            total[:512, :] = even
            total[512:520, :] = jnp.zeros((8, 256), jnp.float32)
        else:
            total[:512, :] += even
        total[8:520, :] += odd
    out[...] = total[:512, :]


def shards(response, traces):
    shots_here, _, taps = response.shape
    rcv_here, samples = traces.shape[1:]
    blocks = samples // PHASES
    shot, rcv = lax.axis_index("shot"), lax.axis_index("rcv")
    x, core, y, z = shot // 2, shot % 2, rcv // 8, rcv % 8
    slots = []
    for other in (core, 1 - core):
        slots += [((x - offset) % 4) * 2 + other for offset in (0, 1, 3, 2)]
    slots += [(y - offset) % 4 for offset in (0, 1, 3, 2)]
    where_z = jnp.array([RING8.index(o) if o in RING8 else RING8.index(o - 8) for o in range(8)], jnp.int32)
    slots += [where_z[(sign(z) * (wanted - z)) % 8] for wanted in range(8)]
    slots = jnp.stack([jnp.asarray(s, jnp.int32) for s in slots])

    resp_piece = jnp.transpose(response, (1, 2, 0)).reshape(4, taps * shots_here)
    trace_piece = jnp.transpose(traces.reshape(16, rcv_here, blocks, PHASES), (2, 1, 3, 0)).reshape(
        blocks * rcv_here, PHASES * 16
    )
    responses = gather_response(resp_piece)
    pieces = gather_traces(trace_piece)
    vmem = pl.BlockSpec(memory_space=pltpu.VMEM)
    product = pl.pallas_call(
        kernel,
        out_shape=jax.ShapeDtypeStruct((512, 256), jnp.float32),
        in_specs=[pl.BlockSpec(memory_space=pltpu.SMEM)] + [vmem] * 12,
        out_specs=vmem,
        scratch_shapes=[
            pltpu.VMEM((8, 576, 128), jnp.bfloat16),
            pltpu.VMEM((8, 64, 19 * 128), jnp.bfloat16),
            pltpu.VMEM((520, 256), jnp.float32),
        ],
        compiler_params=pltpu.CompilerParams(vmem_limit_bytes=48 * 2**20),
    )(slots, *responses, *pieces)
    product = product.astype(jnp.bfloat16).reshape(blocks, rcv_here, PHASES, shots_here)
    return jnp.transpose(product, (3, 1, 0, 2)).reshape(shots_here, rcv_here, samples)


def solution(mesh):
    placed = (P("shot", "rcv", None), P("shot", "rcv", None))
    return jax.shard_map(
        shards, mesh=mesh, in_specs=placed, out_specs=P("shot", "rcv", None), check_vma=False
    )
```

time: 342 us -> 47.1 us (0.14)
  the two profiles are of different devices: /device:TPU:6 before, /device:TPU:1 now
where the time goes in v1:
time: 47.1 us; the launch traced here: 47 us
  starting transfers between devices  25.2 us (54%)
  local copies, waits for them, and re-layouts  11 us (23%)
  waiting for transfers between devices  6.7 us (14%)
  Pallas kernels  3.8 us (8%)
    ppermute x13, starting transfers between devices, spread(): return lax.ppermute(value, axis, [(i, partner(i)) for i in range(size)])  25.2 us
    ppermute x13, waiting for transfers between devices, spread(): return lax.ppermute(value, axis, [(i, partner(i)) for i in range(size)])  6.7 us
    another operation x1, local copies, waits for them, and re-layouts, shards(): slots = jnp.stack([jnp.asarray(s, jnp.int32) for s in slots])  5.15 us
    pallas_call x1, Pallas kernels, shards(): pl.pallas_call(kernel, out_shape=jax.ShapeDtypeStruct((512, 256), jnp.flo...  3.8 us
    unnamed x8, local copies, waits for them, and re-layouts  2.09 us
    reshape x2, local copies, waits for them, and re-layouts, shards(): jnp.transpose(product, (3, 1, 0, 2)).reshape(shots_here, rcv_here, samples)  1.43 us
  transfers between devices with their start and end apart: 13, of which 3 were waited for; matrix products, arithmetic and copies ran while one was open for 13% of the time, Pallas kernels for 0%

profile of v1, /device:TPU:1, one launch (start us, length us, event | category | flops | bytes accessed | tf_op | source)
XLA Modules:
  0.0 47.0 jit_solution(10837561015338507561)
XLA Ops:
  0.0 1.4 %copy.8 = bf16[16,8,512]{0,2,1:T(8,128)(2,1)S(1)} copy(bf16[16,8,512]{2,1,0:T(8,128)(2,1)} %param.4) | data formatting | bytes 262144 | tf_op args[1]
  1.4 0.3 copy.9
  1.7 0.0 copy-start
  1.7 0.7 %reshape.13.t0 = bf16[512,128]{1,0:T(8,128)(2,1)S(1)} reshape(bf16[64,8,8,16]{3,2,1,0:T(8,128)(2,1)S(1)} %copy.9) | data formatting | bytes 262144 | tf_op jit(solution)/shard_map/reshape | solution.py:125
  2.4 3.3 %collective-permute-start.9 = (bf16[512,128]{1,0:T(8,128)(2,1)S(1)}, bf16[512,128]{1,0:T(8,128)(2,1)S(1)}, u32[]{:S(2)}, u32[]{:S(2)}) collective-permute-start(bf16[512,128]{1,0:T(8,128)(2,1)S(1)} %reshape.13.t0), channel_id=1, source_target_pairs={{0,32},{32,0},{64,96},{96,64},{128,160},{160,128},{192,224},{224,1... | collective-permute-start | bytes 393224 | tf_op jit(solution)/shard_map/ppermute | solution.py:17
  5.7 1.0 %collective-permute-start.8 = (bf16[512,128]{1,0:T(8,128)(2,1)S(1)}, bf16[512,128]{1,0:T(8,128)(2,1)S(1)}, u32[]{:S(2)}, u32[]{:S(2)}) collective-permute-start(bf16[512,128]{1,0:T(8,128)(2,1)S(1)} %reshape.13.t0), channel_id=1, source_target_pairs={{0,128},{32,160},{64,192},{96,224},{128,0},{160,32},{192,64},{224,... | collective-permute-start | bytes 393224 | tf_op jit(solution)/shard_map/ppermute | solution.py:17
  6.7 0.9 %collective-permute-start.7 = (bf16[512,128]{1,0:T(8,128)(2,1)S(1)}, bf16[512,128]{1,0:T(8,128)(2,1)S(1)}, u32[]{:S(2)}, u32[]{:S(2)}) collective-permute-start(bf16[512,128]{1,0:T(8,128)(2,1)S(1)} %reshape.13.t0), channel_id=1, source_target_pairs={{0,192},{32,224},{64,0},{96,32},{128,64},{160,96},{192,128},{224,1... | collective-permute-start | bytes 393224 | tf_op jit(solution)/shard_map/ppermute | solution.py:17
  7.6 0.6 %collective-permute-start.6 = (bf16[512,128]{1,0:T(8,128)(2,1)S(1)}, bf16[512,128]{1,0:T(8,128)(2,1)S(1)}, u32[]{:S(2)}, u32[]{:S(2)}) collective-permute-start(bf16[512,128]{1,0:T(8,128)(2,1)S(1)} %reshape.13.t0), channel_id=1, source_target_pairs={{0,64},{32,96},{64,128},{96,160},{128,192},{160,224},{192,0},{224,... | collective-permute-start | bytes 393224 | tf_op jit(solution)/shard_map/ppermute | solution.py:17
  8.2 0.1 copy.7
  8.3 0.1 broadcast_in_dim_reshape.3
  8.5 1.7 %collective-permute-start = (bf16[1,4,2048]{2,1,0:T(4,128)(2,1)S(1)}, bf16[1,4,2048]{2,1,0:T(4,128)(2,1)S(1)}, u32[]{:S(2)}, u32[]{:S(2)}) collective-permute-start(bf16[1,4,2048]{2,1,0:T(4,128)(2,1)S(1)} %broadcast_in_dim_reshape.3), channel_id=1, source_target_pairs={{0,1},{1,0},{2,3},{3,2},{4,5},{5,4},{6,7},{7,6},{8,9},{9,8},{10,11... | collective-permute-start | bytes 49160 | tf_op jit(solution)/shard_map/ppermute | solution.py:17
  10.2 1.4 %collective-permute-done = bf16[1,4,2048]{2,1,0:T(4,128)(2,1)S(1)} collective-permute-done((bf16[1,4,2048]{2,1,0:T(4,128)(2,1)S(1)}, bf16[1,4,2048]{2,1,0:T(4,128)(2,1)S(1)}, u32[]{:S(2)}, u32[]{:S(2)}) %collective-permute-start) | collective-permute-done | bytes 16416 | tf_op jit(solution)/shard_map/ppermute | solution.py:17
  11.6 5.5 %collective-permute-start.1 = (bf16[2,4,2048]{2,1,0:T(4,128)(2,1)S(1)}, bf16[2,4,2048]{2,1,0:T(4,128)(2,1)S(1)}, u32[]{:S(2)}, u32[]{:S(2)}) collective-permute-start(bf16[2,4,2048]{2,1,0:T(4,128)(2,1)S(1)} %pad_maximum_fusion.1), channel_id=1, source_target_pairs={{0,7},{1,2},{2,1},{3,4},{4,3},{5,6},{6,5},{7,0},{8,15},{9,10},{10,... | collective-permute-start | bytes 98312 | tf_op jit(solution)/shard_map/ppermute | solution.py:17
  17.1 1.3 %collective-permute-done.1 = bf16[2,4,2048]{2,1,0:T(4,128)(2,1)S(1)} collective-permute-done((bf16[2,4,2048]{2,1,0:T(4,128)(2,1)S(1)}, bf16[2,4,2048]{2,1,0:T(4,128)(2,1)S(1)}, u32[]{:S(2)}, u32[]{:S(2)}) %collective-permute-start.1) | collective-permute-done | bytes 32800 | tf_op jit(solution)/shard_map/ppermute | solution.py:17
  18.4 0.1 pad_maximum_fusion
  18.5 1.7 %collective-permute-start.2 = (bf16[4,4,2048]{2,1,0:T(4,128)(2,1)S(1)}, bf16[4,4,2048]{2,1,0:T(4,128)(2,1)S(1)}, u32[]{:S(2)}, u32[]{:S(2)}) collective-permute-start(bf16[4,4,2048]{2,1,0:T(4,128)(2,1)S(1)} %pad_maximum_fusion), channel_id=1, source_target_pairs={{0,3},{1,6},{2,5},{3,0},{4,7},{5,2},{6,1},{7,4},{8,11},{9,14},{10,... | collective-permute-start | bytes 196616 | tf_op jit(solution)/shard_map/ppermute | solution.py:17
  20.2 4.0 %collective-permute-done.2 = bf16[4,4,2048]{2,1,0:T(4,128)(2,1)S(1)} collective-permute-done((bf16[4,4,2048]{2,1,0:T(4,128)(2,1)S(1)}, bf16[4,4,2048]{2,1,0:T(4,128)(2,1)S(1)}, u32[]{:S(2)}, u32[]{:S(2)}) %collective-permute-start.2) | collective-permute-done | bytes 65568 | tf_op jit(solution)/shard_map/ppermute | solution.py:17
  24.2 3.0 %collective-permute-start.5 = (bf16[8,4,2048]{2,1,0:T(4,128)(2,1)S(1)}, bf16[8,4,2048]{2,1,0:T(4,128)(2,1)S(1)}, u32[]{:S(2)}, u32[]{:S(2)}) collective-permute-start(bf16[8,4,2048]{2,1,0:T(4,128)(2,1)S(1)} %constant_dynamic-update-slice_fusion.r0), channel_id=1, source_target_pairs={{0,16},{1,17},{2,18},{3,19},{4,20},{5,21},{6,22},{7,23},{8,24},{9,... | collective-permute-start | bytes 393224 | tf_op jit(solution)/shard_map/ppermute | solution.py:17
  27.2 0.0 collective-permute-done.9.t4
  27.2 0.8 %collective-permute-start.4 = (bf16[8,4,2048]{2,1,0:T(4,128)(2,1)S(1)}, bf16[8,4,2048]{2,1,0:T(4,128)(2,1)S(1)}, u32[]{:S(2)}, u32[]{:S(2)}) collective-permute-start(bf16[8,4,2048]{2,1,0:T(4,128)(2,1)S(1)} %constant_dynamic-update-slice_fusion.r0), channel_id=1, source_target_pairs={{0,24},{1,25},{2,26},{3,27},{4,28},{5,29},{6,30},{7,31},{8,0},{9,1... | collective-permute-start | bytes 393224 | tf_op jit(solution)/shard_map/ppermute | solution.py:17
  28.0 0.0 collective-permute-done.8.t3
  28.0 0.7 %collective-permute-start.3 = (bf16[8,4,2048]{2,1,0:T(4,128)(2,1)S(1)}, bf16[8,4,2048]{2,1,0:T(4,128)(2,1)S(1)}, u32[]{:S(2)}, u32[]{:S(2)}) collective-permute-start(bf16[8,4,2048]{2,1,0:T(4,128)(2,1)S(1)} %constant_dynamic-update-slice_fusion.r0), channel_id=1, source_target_pairs={{0,8},{1,9},{2,10},{3,11},{4,12},{5,13},{6,14},{7,15},{8,16},{9,17... | collective-permute-start | bytes 393224 | tf_op jit(solution)/shard_map/ppermute | solution.py:17
  28.7 4.6 %collective-permute-start.12 = (bf16[512,128]{1,0:T(8,128)(2,1)S(1)}, bf16[512,128]{1,0:T(8,128)(2,1)S(1)}, u32[]{:S(2)}, u32[]{:S(2)}) collective-permute-start(bf16[512,128]{1,0:T(8,128)(2,1)S(1)} %collective-permute-done.8.t3), channel_id=1, source_target_pairs={{0,32},{32,0},{64,96},{96,64},{128,160},{160,128},{192,224},{224,1... | collective-permute-start | bytes 393224 | tf_op jit(solution)/shard_map/ppermute | solution.py:17
  33.3 0.1 collective-permute-start.11
  33.4 1.3 %collective-permute-start.10 = (bf16[512,128]{1,0:T(8,128)(2,1)S(1)}, bf16[512,128]{1,0:T(8,128)(2,1)S(1)}, u32[]{:S(2)}, u32[]{:S(2)}) collective-permute-start(bf16[512,128]{1,0:T(8,128)(2,1)S(1)} %collective-permute-done.6.t1), channel_id=1, source_target_pairs={{0,32},{32,0},{64,96},{96,64},{128,160},{160,128},{192,224},{224,1... | collective-permute-start | bytes 393224 | tf_op jit(solution)/shard_map/ppermute | solution.py:17
  34.7 0.7 %copy-done.1 = s32[8]{0:T(128)S(1)} copy-done((s32[8]{0:T(128)S(1)}, s32[8]{0:T(128)}, u32[]{:S(2)}) %copy-start.1) | copy-done | bytes 56
  35.3 0.7 %fusion = (s32[1]{0:T(128)}, s32[1]{0:T(128)}, s32[1]{0:T(128)}, s32[1]{0:T(128)}, s32[1]{0:T(128)}, /*index=5*/s32[1]{0:T(128)}, s32[1]{0:T(128)}, s32[1]{0:T(128)}) fusion(s32[8]{0:T(128)S(1)} %copy-done.1, s32[]{:T(128)S(6)} %select_n.160, s32[]{:T(128)S(6)} %select_n.156, s32[]{:T(128)S(6)} %select_n.154, s32[]{:T(128)S(6)} %select_n.152, ...), kind=kLoop, calls=%fused_computation.7 | loop fusion | bytes 96 | tf_op jit(solution)/shard_map/dynamic_slice | solution.py:121
  36.0 5.2 %stack.51.slots = s32[20]{0:T(128)S(1)} concatenate(s32[1]{0:T(128)} %bitcast, s32[1]{0:T(128)} %bitcast.1, s32[1]{0:T(128)} %bitcast.2, s32[1]{0:T(128)} %bitcast.3, s32[1]{0:T(128)} %bitcast.4, s32[1]{0:T(128)} %bitcast.5, s32[1]{0:T(128)} %bitcast.6, s32[1]{0:T(128)} %bitcast.7, s32[1]{0:T(128)} %bitcast.8, s32[1]{0:T(128)} %bitcast.9, s32[1]{0:T(128)} %bitcast.10, ...), dimensions={0} | concatenate | bytes 160 | tf_op jit(solution)/shard_map/stack | solution.py:122
  41.2 3.8 %shard_map.37 = f32[512,256]{1,0:T(8,128)S(1)} custom-call(s32[20]{0:T(128)S(1)} %stack.51.slots, bf16[8,4,2048]{2,1,0:T(4,128)(2,1)S(1)} %constant_dynamic-update-slice_fusion.r0, bf16[8,4,2048]{2,1,0:T(4,128)(2,1)S(1)} %collective-permute-done.3.r1, bf16[8,4,2048]{2,1,0:T(4,128)(2,1)S(1)} %collective-permute-done.4.r2, ...), custom_call_target="tpu_custom_call" | custom-call | tf_op jit(solution)/shard_map/pallas_call | solution.py:131
  45.1 0.4 reshape.14
  45.5 0.2 copy_bitcast_fusion
  45.7 1.2 %copy.11 = bf16[32,8,512]{2,1,0:T(8,128)(2,1)} copy(bf16[32,8,512]{0,2,1:T(8,128)(2,1)S(1)} %copy_bitcast_fusion) | data formatting | bytes 524288 | tf_op jit(solution)/shard_map/reshape | solution.py:144
  (16 shorter events, 0.2 us)
Async XLA Ops:
  1.7 6.5 %copy-start = (bf16[32,4,64]{2,1,0:T(4,128)(2,1)S(1)}, bf16[32,4,64]{2,1,0:T(4,128)(2,1)}, u32[]{:S(2)}) copy-start(bf16[32,4,64]{2,1,0:T(4,128)(2,1)} %param.3) | copy-start | bytes 49156
  2.4 24.8 %collective-permute-start.9 = (bf16[512,128]{1,0:T(8,128)(2,1)S(1)}, bf16[512,128]{1,0:T(8,128)(2,1)S(1)}, u32[]{:S(2)}, u32[]{:S(2)}) collective-permute-start(bf16[512,128]{1,0:T(8,128)(2,1)S(1)} %reshape.13.t0), channel_id=1, source_target_pairs={{0,32},{32,0},{64,96},{96,64},{128,160},{160,128},{192,224},{224,1... | collective-permute-start | bytes 393224 | tf_op jit(solution)/shard_map/ppermute | solution.py:17
  5.7 22.3 %collective-permute-start.8 = (bf16[512,128]{1,0:T(8,128)(2,1)S(1)}, bf16[512,128]{1,0:T(8,128)(2,1)S(1)}, u32[]{:S(2)}, u32[]{:S(2)}) collective-permute-start(bf16[512,128]{1,0:T(8,128)(2,1)S(1)} %reshape.13.t0), channel_id=1, source_target_pairs={{0,128},{32,160},{64,192},{96,224},{128,0},{160,32},{192,64},{224,... | collective-permute-start | bytes 393224 | tf_op jit(solution)/shard_map/ppermute | solution.py:17
  6.7 21.9 %collective-permute-start.7 = (bf16[512,128]{1,0:T(8,128)(2,1)S(1)}, bf16[512,128]{1,0:T(8,128)(2,1)S(1)}, u32[]{:S(2)}, u32[]{:S(2)}) collective-permute-start(bf16[512,128]{1,0:T(8,128)(2,1)S(1)} %reshape.13.t0), channel_id=1, source_target_pairs={{0,192},{32,224},{64,0},{96,32},{128,64},{160,96},{192,128},{224,1... | collective-permute-start | bytes 393224 | tf_op jit(solution)/shard_map/ppermute | solution.py:17
  7.6 25.7 %collective-permute-start.6 = (bf16[512,128]{1,0:T(8,128)(2,1)S(1)}, bf16[512,128]{1,0:T(8,128)(2,1)S(1)}, u32[]{:S(2)}, u32[]{:S(2)}) collective-permute-start(bf16[512,128]{1,0:T(8,128)(2,1)S(1)} %reshape.13.t0), channel_id=1, source_target_pairs={{0,64},{32,96},{64,128},{96,160},{128,192},{160,224},{192,0},{224,... | collective-permute-start | bytes 393224 | tf_op jit(solution)/shard_map/ppermute | solution.py:17
  8.5 3.1 %collective-permute-start = (bf16[1,4,2048]{2,1,0:T(4,128)(2,1)S(1)}, bf16[1,4,2048]{2,1,0:T(4,128)(2,1)S(1)}, u32[]{:S(2)}, u32[]{:S(2)}) collective-permute-start(bf16[1,4,2048]{2,1,0:T(4,128)(2,1)S(1)} %broadcast_in_dim_reshape.3), channel_id=1, source_target_pairs={{0,1},{1,0},{2,3},{3,2},{4,5},{5,4},{6,7},{7,6},{8,9},{9,8},{10,11... | collective-permute-start | bytes 49160 | tf_op jit(solution)/shard_map/ppermute | solution.py:17
  11.6 6.8 %collective-permute-start.1 = (bf16[2,4,2048]{2,1,0:T(4,128)(2,1)S(1)}, bf16[2,4,2048]{2,1,0:T(4,128)(2,1)S(1)}, u32[]{:S(2)}, u32[]{:S(2)}) collective-permute-start(bf16[2,4,2048]{2,1,0:T(4,128)(2,1)S(1)} %pad_maximum_fusion.1), channel_id=1, source_target_pairs={{0,7},{1,2},{2,1},{3,4},{4,3},{5,6},{6,5},{7,0},{8,15},{9,10},{10,... | collective-permute-start | bytes 98312 | tf_op jit(solution)/shard_map/ppermute | solution.py:17
  18.5 5.7 %collective-permute-start.2 = (bf16[4,4,2048]{2,1,0:T(4,128)(2,1)S(1)}, bf16[4,4,2048]{2,1,0:T(4,128)(2,1)S(1)}, u32[]{:S(2)}, u32[]{:S(2)}) collective-permute-start(bf16[4,4,2048]{2,1,0:T(4,128)(2,1)S(1)} %pad_maximum_fusion), channel_id=1, source_target_pairs={{0,3},{1,6},{2,5},{3,0},{4,7},{5,2},{6,1},{7,4},{8,11},{9,14},{10,... | collective-permute-start | bytes 196616 | tf_op jit(solution)/shard_map/ppermute | solution.py:17
  24.2 9.2 %collective-permute-start.5 = (bf16[8,4,2048]{2,1,0:T(4,128)(2,1)S(1)}, bf16[8,4,2048]{2,1,0:T(4,128)(2,1)S(1)}, u32[]{:S(2)}, u32[]{:S(2)}) collective-permute-start(bf16[8,4,2048]{2,1,0:T(4,128)(2,1)S(1)} %constant_dynamic-update-slice_fusion.r0), channel_id=1, source_target_pairs={{0,16},{1,17},{2,18},{3,19},{4,20},{5,21},{6,22},{7,23},{8,24},{9,... | collective-permute-start | bytes 393224 | tf_op jit(solution)/shard_map/ppermute | solution.py:17
  27.2 14.0 %collective-permute-start.4 = (bf16[8,4,2048]{2,1,0:T(4,128)(2,1)S(1)}, bf16[8,4,2048]{2,1,0:T(4,128)(2,1)S(1)}, u32[]{:S(2)}, u32[]{:S(2)}) collective-permute-start(bf16[8,4,2048]{2,1,0:T(4,128)(2,1)S(1)} %constant_dynamic-update-slice_fusion.r0), channel_id=1, source_target_pairs={{0,24},{1,25},{2,26},{3,27},{4,28},{5,29},{6,30},{7,31},{8,0},{9,1... | collective-permute-start | bytes 393224 | tf_op jit(solution)/shard_map/ppermute | solution.py:17
  28.0 13.2 %collective-permute-start.3 = (bf16[8,4,2048]{2,1,0:T(4,128)(2,1)S(1)}, bf16[8,4,2048]{2,1,0:T(4,128)(2,1)S(1)}, u32[]{:S(2)}, u32[]{:S(2)}) collective-permute-start(bf16[8,4,2048]{2,1,0:T(4,128)(2,1)S(1)} %constant_dynamic-update-slice_fusion.r0), channel_id=1, source_target_pairs={{0,8},{1,9},{2,10},{3,11},{4,12},{5,13},{6,14},{7,15},{8,16},{9,17... | collective-permute-start | bytes 393224 | tf_op jit(solution)/shard_map/ppermute | solution.py:17
  28.7 12.5 %collective-permute-start.12 = (bf16[512,128]{1,0:T(8,128)(2,1)S(1)}, bf16[512,128]{1,0:T(8,128)(2,1)S(1)}, u32[]{:S(2)}, u32[]{:S(2)}) collective-permute-start(bf16[512,128]{1,0:T(8,128)(2,1)S(1)} %collective-permute-done.8.t3), channel_id=1, source_target_pairs={{0,32},{32,0},{64,96},{96,64},{128,160},{160,128},{192,224},{224,1... | collective-permute-start | bytes 393224 | tf_op jit(solution)/shard_map/ppermute | solution.py:17
  33.3 7.9 %collective-permute-start.11 = (bf16[512,128]{1,0:T(8,128)(2,1)S(1)}, bf16[512,128]{1,0:T(8,128)(2,1)S(1)}, u32[]{:S(2)}, u32[]{:S(2)}) collective-permute-start(bf16[512,128]{1,0:T(8,128)(2,1)S(1)} %collective-permute-done.7.t2), channel_id=1, source_target_pairs={{0,32},{32,0},{64,96},{96,64},{128,160},{160,128},{192,224},{224,1... | collective-permute-start | bytes 393224 | tf_op jit(solution)/shard_map/ppermute | solution.py:17
  33.4 7.8 %collective-permute-start.10 = (bf16[512,128]{1,0:T(8,128)(2,1)S(1)}, bf16[512,128]{1,0:T(8,128)(2,1)S(1)}, u32[]{:S(2)}, u32[]{:S(2)}) collective-permute-start(bf16[512,128]{1,0:T(8,128)(2,1)S(1)} %collective-permute-done.6.t1), channel_id=1, source_target_pairs={{0,32},{32,0},{64,96},{96,64},{128,160},{160,128},{192,224},{224,1... | collective-permute-start | bytes 393224 | tf_op jit(solution)/shard_map/ppermute | solution.py:17
  34.7 0.7 %copy-start.1 = (s32[8]{0:T(128)S(1)}, s32[8]{0:T(128)}, u32[]{:S(2)}) copy-start(s32[8]{0:T(128)} %constant.165.clone) | copy-start | bytes 100

commit v2 on v0

v2 whole, which is shorter than its diff:
```python
import jax
import jax.numpy as jnp
from jax import lax
from jax.experimental import pallas as pl
from jax.experimental.pallas import tpu as pltpu
from jax.sharding import PartitionSpec as P

RING4 = (0, 1, 3, 2)
RING8 = (0, 1, 7, 6, 3, 2, 4, 5)
VMEM = pl.BlockSpec(memory_space=pltpu.VMEM)
PARAMS = pltpu.CompilerParams(vmem_limit_bytes=40 * 2**20)


def spread(value, axis, partner):
    size = lax.axis_size(axis)
    return lax.ppermute(value, axis, [(i, partner(i)) for i in range(size)])


def sign(coordinate):
    return 1 - 2 * (coordinate % 2)


def prepare_traces(traces, out, rows, turned):
    for part in range(4):
        lanes = traces[:, :, part * 128 : part * 128 + 128]
        rows[part] = lanes.astype(jnp.float32).reshape(128, 128)
    for part in range(4):
        by_receiver = [rows[part, pl.ds(r, 16, stride=8), :] for r in range(8)]
        turned[part * 128 : part * 128 + 128, :] = jnp.concatenate(by_receiver, axis=0).T
    skewed = [pltpu.roll(turned[pl.ds(d, 64, stride=8), :], 16 * d, 1) for d in range(8)]
    lane_block = lax.broadcasted_iota(jnp.int32, (64, 128), 1) // 16
    for r in range(8):
        mixed = skewed[0]
        for d in range(1, 8):
            mixed = jnp.where(lane_block == (r + d) % 8, skewed[d], mixed)
        turned[pl.ds(r, 64, stride=8), :] = pltpu.roll(mixed, (128 - 16 * r) % 128, 1)
    out[...] = turned[...].astype(jnp.bfloat16)


def assemble(mine, other, out):
    shot = lax.axis_index("shot")
    x, core = shot // 2, shot % 2
    for blocks, side in ((mine, core), (other, 1 - core)):
        for slot in range(4):
            place = ((x + 4 - RING4[slot]) % 4) * 2 + side
            out[place, :64, :] = jnp.zeros((64, 128), jnp.bfloat16)
            out[place, 64:, :] = blocks[slot]


def position_of(offset):
    slot = jnp.int32(0)
    for index in range(1, 8):
        slot = jnp.where(offset == RING8[index], index, slot)
    return slot


def add_products(offsets, responses, padded, band, total):
    rcv = lax.axis_index("rcv")
    y, z = rcv // 8, rcv % 8
    slots = [position_of((sign(z) * (wanted - z) + 64) % 8) for wanted in range(8)]
    for response, offset in zip(responses, offsets, strict=True):
        for half in range(2):
            rows = jnp.concatenate(
                [response[slots[half * 4 + q]].astype(jnp.float32) for q in range(4)], axis=0
            )
            wide = jnp.concatenate([rows, jnp.zeros((16, 384), jnp.float32)], axis=1)
            for shift in range(4):
                band[half, shift * 16 : shift * 16 + 16, :] = pltpu.roll(
                    wide, 128 + 32 * shift, 1
                ).astype(jnp.bfloat16)
        place = ((y + 4 - offset) % 4) * 2
        even_rows, odd_rows, sides = [], [], []
        for group in range(5):
            sides += [
                padded[place + half, 64 - 16 * group : 576 - 16 * group, :] for half in range(2)
            ]
            for rows, step in ((even_rows, 2 * group), (odd_rows, 2 * group + 1)):
                if step <= 8:
                    for half in range(2):
                        for late in range(2):
                            first = (2 * step - late + 1) * 128
                            rows.append(band[half, :, first : first + 256])
        total[...] += jnp.dot(
            jnp.concatenate(sides, axis=1),
            jnp.concatenate(even_rows, axis=0),
            preferred_element_type=jnp.float32,
        )
        odd = jnp.dot(
            jnp.concatenate(sides[:8], axis=1),
            jnp.concatenate(odd_rows, axis=0),
            preferred_element_type=jnp.float32,
        )
        total[8:, :] += odd[:504, :]


def first_kernel(own, padded, total, band):
    total[...] = jnp.zeros_like(total)
    add_products((0,), (own,), padded, band, total)


def middle_kernel(before, after, padded, so_far, total, band):
    total[...] = so_far[...]
    add_products((1, 3), (before, after), padded, band, total)


def last_kernel(across, padded, so_far, out, band, total, placed):
    total[...] = so_far[...]
    add_products((2,), (across,), padded, band, total)
    turned = total[...].T
    skewed = [pltpu.roll(turned[u * 32 : u * 32 + 32, :], u, 1) for u in range(8)]
    lane = lax.broadcasted_iota(jnp.int32, (32, 512), 1)
    for r in range(8):
        mixed = skewed[0]
        for u in range(1, 8):
            mixed = jnp.where(lane % 8 == (r + u) % 8, skewed[u], mixed)
        mixed = pltpu.roll(mixed, (512 - r) % 512, 1)
        for part in range(4):
            placed[part, pl.ds(r, 32, stride=8), :] = mixed[:, part * 128 : part * 128 + 128]
    for part in range(4):
        out[:, :, part * 128 : part * 128 + 128] = placed[part].reshape(32, 8, 128).astype(jnp.bfloat16)


def call(body, shape, dtype, operands, scratch, flops=0):
    return pl.pallas_call(
        body,
        out_shape=jax.ShapeDtypeStruct(shape, dtype),
        in_specs=[VMEM] * len(operands),
        out_specs=VMEM,
        scratch_shapes=[pltpu.VMEM(s, d) for s, d in scratch],
        compiler_params=PARAMS,
        cost_estimate=pl.CostEstimate(flops=flops, bytes_accessed=2**20, transcendentals=0),
    )(*operands)


def shards(response, traces):
    f32, bf16 = jnp.float32, jnp.bfloat16
    band = ((2, 64, 19 * 128), bf16)

    def along_z(step):
        return lambda i: (i // 8) * 8 + step(i % 8) % 8

    def along_y(offset):
        return lambda i: (i // 8 + offset) % 4 * 8 + i % 8

    def along_x(offset):
        return lambda i: ((i // 2 + offset) % 4) * 2 + i % 2

    held = jnp.transpose(response, (1, 2, 0)).reshape(1, 4, 2048)
    piece = call(prepare_traces, (512, 128), bf16, (traces,), [((4, 128, 128), f32), ((512, 128), f32)])
    for step in (lambda z: z + sign(z), lambda z: z - sign(z), lambda z: z + 3 * sign(z)):
        held = jnp.concatenate([held, spread(held, "rcv", along_z(step))], axis=0)
    before, after, across = [spread(held, "rcv", along_y(offset)) for offset in (1, 3, 2)]

    mine = jnp.stack([piece] + [spread(piece, "shot", along_x(offset)) for offset in (1, 3, 2)])
    other = spread(mine, "shot", lambda i: i ^ 1)
    padded = call(assemble, (8, 576, 128), bf16, (mine, other), [])
    work = 2 * 512 * 256 * 9 * 256
    total = call(first_kernel, (512, 256), f32, (held, padded), [band], work)
    total = call(middle_kernel, (512, 256), f32, (before, after, padded, total), [band], 2 * work)
    return call(
        last_kernel,
        (32, 8, 512),
        bf16,
        (across, padded, total),
        [band, ((512, 256), f32), ((4, 256, 128), f32)],
        work,
    )


def solution(mesh):
    placed = (P("shot", "rcv", None), P("shot", "rcv", None))
    return jax.shard_map(
        shards, mesh=mesh, in_specs=placed, out_specs=P("shot", "rcv", None), check_vma=False
    )
```

time: 342 us -> 37.1 us (0.11)
  the two profiles are of different devices: /device:TPU:6 before, /device:TPU:8 now
where the time goes in v2:
time: 37.1 us; the launch traced here: 36.9 us
  starting transfers between devices  19.6 us (53%)
  waiting for transfers between devices  9.95 us (27%)
  Pallas kernels  5.11 us (14%)
  local copies, waits for them, and re-layouts  1.97 us (5%)
    ppermute x10, starting transfers between devices, spread(): return lax.ppermute(value, axis, [(i, partner(i)) for i in range(size)])  19.6 us
    ppermute x10, waiting for transfers between devices, spread(): return lax.ppermute(value, axis, [(i, partner(i)) for i in range(size)])  9.95 us
    pallas_call x5, Pallas kernels, call(): pl.pallas_call(body, out_shape=jax.ShapeDtypeStruct(shape, dtype), in_spe...  5.11 us
    unnamed x5, local copies, waits for them, and re-layouts  0.95 us
    transpose x1, local copies, waits for them, and re-layouts, shards(): held = jnp.transpose(response, (1, 2, 0)).reshape(1, 4, 2048)  0.86 us
  transfers between devices with their start and end apart: 10, of which 5 were waited for; matrix products, arithmetic and copies ran while one was open for 3% of the time, Pallas kernels for 7%

profile of v2, /device:TPU:8, one launch (start us, length us, event | category | flops | bytes accessed | tf_op | source)
XLA Modules:
  0.0 36.9 jit_solution(15183514325592453417)
XLA Ops:
  0.0 0.0 copy-start
  0.0 0.9 %copy-done = bf16[16,8,512]{2,1,0:T(8,128)(2,1)S(1)} copy-done((bf16[16,8,512]{2,1,0:T(8,128)(2,1)S(1)}, bf16[16,8,512]{2,1,0:T(8,128)(2,1)}, u32[]{:S(2)}) %copy-start) | copy-done | bytes 131096
  0.9 0.4 %shard_map.28 = bf16[512,128]{1,0:T(8,128)(2,1)S(1)} custom-call(bf16[16,8,512]{2,1,0:T(8,128)(2,1)S(1)} %copy-done), custom_call_target="tpu_custom_call" | custom-call | bytes 1048576 | tf_op jit(solution)/shard_map/pallas_call | solution.py:124
  1.3 1.6 %collective-permute-start.4 = (bf16[512,128]{1,0:T(8,128)(2,1)S(1)}, bf16[512,128]{1,0:T(8,128)(2,1)S(1)}, u32[]{:S(2)}, u32[]{:S(2)}) collective-permute-start(bf16[512,128]{1,0:T(8,128)(2,1)S(1)} %shard_map.28), channel_id=1, source_target_pairs={{0,64},{32,96},{64,128},{96,160},{128,192},{160,224},{192,0},{224,... | collective-permute-start | bytes 393224 | tf_op jit(solution)/shard_map/ppermute | solution.py:16
  2.9 1.7 %collective-permute-start.5 = (bf16[512,128]{1,0:T(8,128)(2,1)S(1)}, bf16[512,128]{1,0:T(8,128)(2,1)S(1)}, u32[]{:S(2)}, u32[]{:S(2)}) collective-permute-start(bf16[512,128]{1,0:T(8,128)(2,1)S(1)} %shard_map.28), channel_id=1, source_target_pairs={{0,192},{32,224},{64,0},{96,32},{128,64},{160,96},{192,128},{224,1... | collective-permute-start | bytes 393224 | tf_op jit(solution)/shard_map/ppermute | solution.py:16
  4.6 1.8 %collective-permute-start.6 = (bf16[512,128]{1,0:T(8,128)(2,1)S(1)}, bf16[512,128]{1,0:T(8,128)(2,1)S(1)}, u32[]{:S(2)}, u32[]{:S(2)}) collective-permute-start(bf16[512,128]{1,0:T(8,128)(2,1)S(1)} %shard_map.28), channel_id=1, source_target_pairs={{0,128},{32,160},{64,192},{96,224},{128,0},{160,32},{192,64},{224,... | collective-permute-start | bytes 393224 | tf_op jit(solution)/shard_map/ppermute | solution.py:16
  6.5 0.9 %copy.4 = bf16[4,64,32]{2,1,0:T(8,128)(2,1)S(1)} copy(bf16[4,64,32]{1,0,2:T(4,128)(2,1)} %bitcast.9) | data formatting | bytes 32768 | tf_op jit(solution)/shard_map/transpose | solution.py:148
  7.3 0.1 reshape.3
  7.4 2.0 %collective-permute-start = (bf16[1,4,2048]{2,1,0:T(4,128)(2,1)S(1)}, bf16[1,4,2048]{2,1,0:T(4,128)(2,1)S(1)}, u32[]{:S(2)}, u32[]{:S(2)}) collective-permute-start(bf16[1,4,2048]{2,1,0:T(4,128)(2,1)S(1)} %reshape.3), channel_id=1, source_target_pairs={{0,1},{1,0},{2,3},{3,2},{4,5},{5,4},{6,7},{7,6},{8,9},{9,8},{10,11... | collective-permute-start | bytes 49160 | tf_op jit(solution)/shard_map/ppermute | solution.py:16
  9.5 1.8 %collective-permute-done = bf16[1,4,2048]{2,1,0:T(4,128)(2,1)S(1)} collective-permute-done((bf16[1,4,2048]{2,1,0:T(4,128)(2,1)S(1)}, bf16[1,4,2048]{2,1,0:T(4,128)(2,1)S(1)}, u32[]{:S(2)}, u32[]{:S(2)}) %collective-permute-start) | collective-permute-done | bytes 16416 | tf_op jit(solution)/shard_map/ppermute | solution.py:16
  11.3 5.9 %collective-permute-start.1 = (bf16[2,4,2048]{2,1,0:T(4,128)(2,1)S(1)}, bf16[2,4,2048]{2,1,0:T(4,128)(2,1)S(1)}, u32[]{:S(2)}, u32[]{:S(2)}) collective-permute-start(bf16[2,4,2048]{2,1,0:T(4,128)(2,1)S(1)} %pad_maximum_fusion.2), channel_id=1, source_target_pairs={{0,7},{1,2},{2,1},{3,4},{4,3},{5,6},{6,5},{7,0},{8,15},{9,10},{10,... | collective-permute-start | bytes 98312 | tf_op jit(solution)/shard_map/ppermute | solution.py:16
  17.3 1.9 %collective-permute-done.1 = bf16[2,4,2048]{2,1,0:T(4,128)(2,1)S(1)} collective-permute-done((bf16[2,4,2048]{2,1,0:T(4,128)(2,1)S(1)}, bf16[2,4,2048]{2,1,0:T(4,128)(2,1)S(1)}, u32[]{:S(2)}, u32[]{:S(2)}) %collective-permute-start.1) | collective-permute-done | bytes 32800 | tf_op jit(solution)/shard_map/ppermute | solution.py:16
  19.1 0.1 pad_maximum_fusion.1
  19.2 2.1 %collective-permute-start.2 = (bf16[4,4,2048]{2,1,0:T(4,128)(2,1)S(1)}, bf16[4,4,2048]{2,1,0:T(4,128)(2,1)S(1)}, u32[]{:S(2)}, u32[]{:S(2)}) collective-permute-start(bf16[4,4,2048]{2,1,0:T(4,128)(2,1)S(1)} %pad_maximum_fusion.1), channel_id=1, source_target_pairs={{0,3},{1,6},{2,5},{3,0},{4,7},{5,2},{6,1},{7,4},{8,11},{9,14},{10,... | collective-permute-start | bytes 196616 | tf_op jit(solution)/shard_map/ppermute | solution.py:16
  21.3 0.0 collective-permute-done.4
  21.3 0.0 collective-permute-done.5
  21.3 0.0 collective-permute-done.6
  21.3 0.1 pad_maximum_fusion.mine
  21.4 0.1 collective-permute-start.7
  21.5 4.6 %collective-permute-done.2 = bf16[4,4,2048]{2,1,0:T(4,128)(2,1)S(1)} collective-permute-done((bf16[4,4,2048]{2,1,0:T(4,128)(2,1)S(1)}, bf16[4,4,2048]{2,1,0:T(4,128)(2,1)S(1)}, u32[]{:S(2)}, u32[]{:S(2)}) %collective-permute-start.2) | collective-permute-done | bytes 65568 | tf_op jit(solution)/shard_map/ppermute | solution.py:16
  26.1 1.7 %collective-permute-start.8 = (bf16[8,4,2048]{2,1,0:T(4,128)(2,1)S(1)}, bf16[8,4,2048]{2,1,0:T(4,128)(2,1)S(1)}, u32[]{:S(2)}, u32[]{:S(2)}) collective-permute-start(bf16[8,4,2048]{2,1,0:T(4,128)(2,1)S(1)} %constant_dynamic-update-slice_fusion.own), channel_id=1, source_target_pairs={{0,8},{1,9},{2,10},{3,11},{4,12},{5,13},{6,14},{7,15},{8,16},{9,17... | collective-permute-start | bytes 393224 | tf_op jit(solution)/shard_map/ppermute | solution.py:16
  27.7 0.5 %collective-permute-start.9 = (bf16[8,4,2048]{2,1,0:T(4,128)(2,1)S(1)}, bf16[8,4,2048]{2,1,0:T(4,128)(2,1)S(1)}, u32[]{:S(2)}, u32[]{:S(2)}) collective-permute-start(bf16[8,4,2048]{2,1,0:T(4,128)(2,1)S(1)} %constant_dynamic-update-slice_fusion.own), channel_id=1, source_target_pairs={{0,24},{1,25},{2,26},{3,27},{4,28},{5,29},{6,30},{7,31},{8,0},{9,1... | collective-permute-start | bytes 393224 | tf_op jit(solution)/shard_map/ppermute | solution.py:16
  28.2 2.3 %collective-permute-start.3 = (bf16[8,4,2048]{2,1,0:T(4,128)(2,1)S(1)}, bf16[8,4,2048]{2,1,0:T(4,128)(2,1)S(1)}, u32[]{:S(2)}, u32[]{:S(2)}) collective-permute-start(bf16[8,4,2048]{2,1,0:T(4,128)(2,1)S(1)} %constant_dynamic-update-slice_fusion.own), channel_id=1, source_target_pairs={{0,16},{1,17},{2,18},{3,19},{4,20},{5,21},{6,22},{7,23},{8,24},{9,... | collective-permute-start | bytes 393224 | tf_op jit(solution)/shard_map/ppermute | solution.py:16
  30.5 0.0 collective-permute-done.7.other
  30.5 0.1 shard_map.29.padded
  30.6 0.9 %shard_map.30.so_far = f32[512,256]{1,0:T(8,128)S(1)} custom-call(bf16[8,4,2048]{2,1,0:T(4,128)(2,1)S(1)} %constant_dynamic-update-slice_fusion.own, bf16[8,576,128]{2,1,0:T(8,128)(2,1)S(1)} %shard_map.29.padded), custom_call_target="tpu_custom_call" | custom-call | flops 603979776 | bytes 1048576 | tf_op jit(solution)/shard_map/pallas_call | solution.py:124
  31.5 0.0 collective-permute-done.8.before
  31.6 1.1 %collective-permute-done.9.after = bf16[8,4,2048]{2,1,0:T(4,128)(2,1)S(1)} collective-permute-done((bf16[8,4,2048]{2,1,0:T(4,128)(2,1)S(1)}, bf16[8,4,2048]{2,1,0:T(4,128)(2,1)S(1)}, u32[]{:S(2)}, u32[]{:S(2)}) %collective-permute-start.9) | collective-permute-done | bytes 131104 | tf_op jit(solution)/shard_map/ppermute | solution.py:16
  32.7 1.6 %shard_map.31.so_far = f32[512,256]{1,0:T(8,128)S(1)} custom-call(bf16[8,4,2048]{2,1,0:T(4,128)(2,1)S(1)} %collective-permute-done.8.before, bf16[8,4,2048]{2,1,0:T(4,128)(2,1)S(1)} %collective-permute-done.9.after, bf16[8,576,128]{2,1,0:T(8,128)(2,1)S(1)} %shard_map.29.padded, f32[512,256]{1,0:T(8,128)S(1)} %shard_map.30.so_far), custom_call_target="tpu_custom_call" | custom-call | flops 1207959552 | bytes 1048576 | tf_op jit(solution)/shard_map/pallas_call | solution.py:124
  34.3 0.5 %collective-permute-done.3.across = bf16[8,4,2048]{2,1,0:T(4,128)(2,1)S(1)} collective-permute-done((bf16[8,4,2048]{2,1,0:T(4,128)(2,1)S(1)}, bf16[8,4,2048]{2,1,0:T(4,128)(2,1)S(1)}, u32[]{:S(2)}, u32[]{:S(2)}) %collective-permute-start.3) | collective-permute-done | bytes 131104 | tf_op jit(solution)/shard_map/ppermute | solution.py:16
  34.8 2.1 %shard_map.32 = bf16[32,8,512]{2,1,0:T(8,128)(2,1)} custom-call(bf16[8,4,2048]{2,1,0:T(4,128)(2,1)S(1)} %collective-permute-done.3.across, bf16[8,576,128]{2,1,0:T(8,128)(2,1)S(1)} %shard_map.29.padded, f32[512,256]{1,0:T(8,128)S(1)} %shard_map.31.so_far), custom_call_target="tpu_custom_call" | custom-call | flops 603979776 | bytes 1048576 | tf_op jit(solution)/shard_map/pallas_call | solution.py:124
  (5 shorter events, 0.1 us)
Async XLA Ops:
  0.0 0.9 %copy-start = (bf16[16,8,512]{2,1,0:T(8,128)(2,1)S(1)}, bf16[16,8,512]{2,1,0:T(8,128)(2,1)}, u32[]{:S(2)}) copy-start(bf16[16,8,512]{2,1,0:T(8,128)(2,1)} %traces.1) | copy-start | bytes 393220
  1.3 20.0 %collective-permute-start.4 = (bf16[512,128]{1,0:T(8,128)(2,1)S(1)}, bf16[512,128]{1,0:T(8,128)(2,1)S(1)}, u32[]{:S(2)}, u32[]{:S(2)}) collective-permute-start(bf16[512,128]{1,0:T(8,128)(2,1)S(1)} %shard_map.28), channel_id=1, source_target_pairs={{0,64},{32,96},{64,128},{96,160},{128,192},{160,224},{192,0},{224,... | collective-permute-start | bytes 393224 | tf_op jit(solution)/shard_map/ppermute | solution.py:16
  2.9 18.4 %collective-permute-start.5 = (bf16[512,128]{1,0:T(8,128)(2,1)S(1)}, bf16[512,128]{1,0:T(8,128)(2,1)S(1)}, u32[]{:S(2)}, u32[]{:S(2)}) collective-permute-start(bf16[512,128]{1,0:T(8,128)(2,1)S(1)} %shard_map.28), channel_id=1, source_target_pairs={{0,192},{32,224},{64,0},{96,32},{128,64},{160,96},{192,128},{224,1... | collective-permute-start | bytes 393224 | tf_op jit(solution)/shard_map/ppermute | solution.py:16
  4.6 16.6 %collective-permute-start.6 = (bf16[512,128]{1,0:T(8,128)(2,1)S(1)}, bf16[512,128]{1,0:T(8,128)(2,1)S(1)}, u32[]{:S(2)}, u32[]{:S(2)}) collective-permute-start(bf16[512,128]{1,0:T(8,128)(2,1)S(1)} %shard_map.28), channel_id=1, source_target_pairs={{0,128},{32,160},{64,192},{96,224},{128,0},{160,32},{192,64},{224,... | collective-permute-start | bytes 393224 | tf_op jit(solution)/shard_map/ppermute | solution.py:16
  7.4 3.8 %collective-permute-start = (bf16[1,4,2048]{2,1,0:T(4,128)(2,1)S(1)}, bf16[1,4,2048]{2,1,0:T(4,128)(2,1)S(1)}, u32[]{:S(2)}, u32[]{:S(2)}) collective-permute-start(bf16[1,4,2048]{2,1,0:T(4,128)(2,1)S(1)} %reshape.3), channel_id=1, source_target_pairs={{0,1},{1,0},{2,3},{3,2},{4,5},{5,4},{6,7},{7,6},{8,9},{9,8},{10,11... | collective-permute-start | bytes 49160 | tf_op jit(solution)/shard_map/ppermute | solution.py:16
  11.3 7.8 %collective-permute-start.1 = (bf16[2,4,2048]{2,1,0:T(4,128)(2,1)S(1)}, bf16[2,4,2048]{2,1,0:T(4,128)(2,1)S(1)}, u32[]{:S(2)}, u32[]{:S(2)}) collective-permute-start(bf16[2,4,2048]{2,1,0:T(4,128)(2,1)S(1)} %pad_maximum_fusion.2), channel_id=1, source_target_pairs={{0,7},{1,2},{2,1},{3,4},{4,3},{5,6},{6,5},{7,0},{8,15},{9,10},{10,... | collective-permute-start | bytes 98312 | tf_op jit(solution)/shard_map/ppermute | solution.py:16
  19.2 6.9 %collective-permute-start.2 = (bf16[4,4,2048]{2,1,0:T(4,128)(2,1)S(1)}, bf16[4,4,2048]{2,1,0:T(4,128)(2,1)S(1)}, u32[]{:S(2)}, u32[]{:S(2)}) collective-permute-start(bf16[4,4,2048]{2,1,0:T(4,128)(2,1)S(1)} %pad_maximum_fusion.1), channel_id=1, source_target_pairs={{0,3},{1,6},{2,5},{3,0},{4,7},{5,2},{6,1},{7,4},{8,11},{9,14},{10,... | collective-permute-start | bytes 196616 | tf_op jit(solution)/shard_map/ppermute | solution.py:16
  21.4 9.1 %collective-permute-start.7 = (bf16[4,512,128]{2,1,0:T(8,128)(2,1)S(1)}, bf16[4,512,128]{2,1,0:T(8,128)(2,1)S(1)}, u32[]{:S(2)}, u32[]{:S(2)}) collective-permute-start(bf16[4,512,128]{2,1,0:T(8,128)(2,1)S(1)} %pad_maximum_fusion.mine), channel_id=1, source_target_pairs={{0,32},{32,0},{64,96},{96,64},{128,160},{160,128},{192,224},{224,1... | collective-permute-start | bytes 1572872 | tf_op jit(solution)/shard_map/ppermute | solution.py:16
  26.1 5.5 %collective-permute-start.8 = (bf16[8,4,2048]{2,1,0:T(4,128)(2,1)S(1)}, bf16[8,4,2048]{2,1,0:T(4,128)(2,1)S(1)}, u32[]{:S(2)}, u32[]{:S(2)}) collective-permute-start(bf16[8,4,2048]{2,1,0:T(4,128)(2,1)S(1)} %constant_dynamic-update-slice_fusion.own), channel_id=1, source_target_pairs={{0,8},{1,9},{2,10},{3,11},{4,12},{5,13},{6,14},{7,15},{8,16},{9,17... | collective-permute-start | bytes 393224 | tf_op jit(solution)/shard_map/ppermute | solution.py:16
  27.7 5.0 %collective-permute-start.9 = (bf16[8,4,2048]{2,1,0:T(4,128)(2,1)S(1)}, bf16[8,4,2048]{2,1,0:T(4,128)(2,1)S(1)}, u32[]{:S(2)}, u32[]{:S(2)}) collective-permute-start(bf16[8,4,2048]{2,1,0:T(4,128)(2,1)S(1)} %constant_dynamic-update-slice_fusion.own), channel_id=1, source_target_pairs={{0,24},{1,25},{2,26},{3,27},{4,28},{5,29},{6,30},{7,31},{8,0},{9,1... | collective-permute-start | bytes 393224 | tf_op jit(solution)/shard_map/ppermute | solution.py:16
  28.2 6.6 %collective-permute-start.3 = (bf16[8,4,2048]{2,1,0:T(4,128)(2,1)S(1)}, bf16[8,4,2048]{2,1,0:T(4,128)(2,1)S(1)}, u32[]{:S(2)}, u32[]{:S(2)}) collective-permute-start(bf16[8,4,2048]{2,1,0:T(4,128)(2,1)S(1)} %constant_dynamic-update-slice_fusion.own), channel_id=1, source_target_pairs={{0,16},{1,17},{2,18},{3,19},{4,20},{5,21},{6,22},{7,23},{8,24},{9,... | collective-permute-start | bytes 393224 | tf_op jit(solution)/shard_map/ppermute | solution.py:16

commit v3 on v2

--- a/solution.py
+++ b/solution.py
@@ -6,7 +6,7 @@
 from jax.sharding import PartitionSpec as P
 
 RING4 = (0, 1, 3, 2)
-RING8 = (0, 1, 7, 6, 3, 2, 4, 5)
+RING8 = (0, 1, 7, 6, 2, 3, 5, 4)
 VMEM = pl.BlockSpec(memory_space=pltpu.VMEM)
 PARAMS = pltpu.CompilerParams(vmem_limit_bytes=40 * 2**20)
 
@@ -20,7 +20,7 @@
     return 1 - 2 * (coordinate % 2)
 
 
-def prepare_traces(traces, out, rows, turned):
+def prepare_traces(traces, _, out, rows, turned):
     for part in range(4):
         lanes = traces[:, :, part * 128 : part * 128 + 128]
         rows[part] = lanes.astype(jnp.float32).reshape(128, 128)
@@ -146,9 +146,10 @@
         return lambda i: ((i // 2 + offset) % 4) * 2 + i % 2
 
     held = jnp.transpose(response, (1, 2, 0)).reshape(1, 4, 2048)
-    piece = call(prepare_traces, (512, 128), bf16, (traces,), [((4, 128, 128), f32), ((512, 128), f32)])
-    for step in (lambda z: z + sign(z), lambda z: z - sign(z), lambda z: z + 3 * sign(z)):
-        held = jnp.concatenate([held, spread(held, "rcv", along_z(step))], axis=0)
+    piece = call(prepare_traces, (512, 128), bf16, (traces, held), [((4, 128, 128), f32), ((512, 128), f32)])
+    held = jnp.concatenate([held, spread(held, "rcv", along_z(lambda z: z + sign(z)))], axis=0)
+    steps = [lambda z: z - sign(z), lambda z: z - 2 * sign(z), lambda z: z - 3 * sign(z)]
+    held = jnp.concatenate([held] + [spread(held, "rcv", along_z(step)) for step in steps], axis=0)
     before, after, across = [spread(held, "rcv", along_y(offset)) for offset in (1, 3, 2)]
 
     mine = jnp.stack([piece] + [spread(piece, "shot", along_x(offset)) for offset in (1, 3, 2)])

time: 37.1 us -> 36.9 us (level)
  the two profiles are of different devices: /device:TPU:8 before, /device:TPU:2 now
where the time goes in v3:
time: 36.9 us; the launch traced here: 36.7 us
  starting transfers between devices  19.1 us (52%)
  waiting for transfers between devices  10.3 us (28%)
  Pallas kernels  5.12 us (14%)
  local copies, waits for them, and re-layouts  1.99 us (5%)
    ppermute x11, starting transfers between devices, spread(): return lax.ppermute(value, axis, [(i, partner(i)) for i in range(size)])  19.1 us
    ppermute x11, waiting for transfers between devices, spread(): return lax.ppermute(value, axis, [(i, partner(i)) for i in range(size)])  10.3 us
    pallas_call x5, Pallas kernels, call(): pl.pallas_call(body, out_shape=jax.ShapeDtypeStruct(shape, dtype), in_spe...  5.12 us
    unnamed x5, local copies, waits for them, and re-layouts  0.96 us
    transpose x1, local copies, waits for them, and re-layouts, shards(): held = jnp.transpose(response, (1, 2, 0)).reshape(1, 4, 2048)  0.86 us
  transfers between devices with their start and end apart: 11, of which 3 were waited for; matrix products, arithmetic and copies ran while one was open for 0% of the time, Pallas kernels for 8%

profile of v3, /device:TPU:2, one launch (start us, length us, event | category | flops | bytes accessed | tf_op | source)
XLA Modules:
  0.0 36.7 jit_solution(7148474458561361440)
XLA Ops:
  0.0 0.9 %copy.4 = bf16[4,64,32]{2,1,0:T(8,128)(2,1)S(1)} copy(bf16[4,64,32]{1,0,2:T(4,128)(2,1)} %bitcast.9) | data formatting | bytes 32768 | tf_op jit(solution)/shard_map/transpose | solution.py:148
  0.9 0.1 reshape.3._
  1.0 2.0 %collective-permute-start = (bf16[1,4,2048]{2,1,0:T(4,128)(2,1)S(1)}, bf16[1,4,2048]{2,1,0:T(4,128)(2,1)S(1)}, u32[]{:S(2)}, u32[]{:S(2)}) collective-permute-start(bf16[1,4,2048]{2,1,0:T(4,128)(2,1)S(1)} %reshape.3._), channel_id=1, source_target_pairs={{0,1},{1,0},{2,3},{3,2},{4,5},{5,4},{6,7},{7,6},{8,9},{9,8},{10,11... | collective-permute-start | bytes 49160 | tf_op jit(solution)/shard_map/ppermute | solution.py:16
  3.0 0.0 copy-start
  3.0 0.9 %copy-done = bf16[16,8,512]{2,1,0:T(8,128)(2,1)S(1)} copy-done((bf16[16,8,512]{2,1,0:T(8,128)(2,1)S(1)}, bf16[16,8,512]{2,1,0:T(8,128)(2,1)}, u32[]{:S(2)}) %copy-start) | copy-done | bytes 131096
  3.9 0.4 %shard_map.28 = bf16[512,128]{1,0:T(8,128)(2,1)S(1)} custom-call(bf16[16,8,512]{2,1,0:T(8,128)(2,1)S(1)} %copy-done, bf16[1,4,2048]{2,1,0:T(4,128)(2,1)S(1)} %reshape.3._), custom_call_target="tpu_custom_call" | custom-call | bytes 1048576 | tf_op jit(solution)/shard_map/pallas_call | solution.py:124
  4.3 1.6 %collective-permute-start.5 = (bf16[512,128]{1,0:T(8,128)(2,1)S(1)}, bf16[512,128]{1,0:T(8,128)(2,1)S(1)}, u32[]{:S(2)}, u32[]{:S(2)}) collective-permute-start(bf16[512,128]{1,0:T(8,128)(2,1)S(1)} %shard_map.28), channel_id=1, source_target_pairs={{0,64},{32,96},{64,128},{96,160},{128,192},{160,224},{192,0},{224,... | collective-permute-start | bytes 393224 | tf_op jit(solution)/shard_map/ppermute | solution.py:16
  5.9 0.5 %collective-permute-start.6 = (bf16[512,128]{1,0:T(8,128)(2,1)S(1)}, bf16[512,128]{1,0:T(8,128)(2,1)S(1)}, u32[]{:S(2)}, u32[]{:S(2)}) collective-permute-start(bf16[512,128]{1,0:T(8,128)(2,1)S(1)} %shard_map.28), channel_id=1, source_target_pairs={{0,192},{32,224},{64,0},{96,32},{128,64},{160,96},{192,128},{224,1... | collective-permute-start | bytes 393224 | tf_op jit(solution)/shard_map/ppermute | solution.py:16
  6.4 2.1 %collective-permute-start.7 = (bf16[512,128]{1,0:T(8,128)(2,1)S(1)}, bf16[512,128]{1,0:T(8,128)(2,1)S(1)}, u32[]{:S(2)}, u32[]{:S(2)}) collective-permute-start(bf16[512,128]{1,0:T(8,128)(2,1)S(1)} %shard_map.28), channel_id=1, source_target_pairs={{0,128},{32,160},{64,192},{96,224},{128,0},{160,32},{192,64},{224,... | collective-permute-start | bytes 393224 | tf_op jit(solution)/shard_map/ppermute | solution.py:16
  8.6 0.0 collective-permute-done
  8.6 5.0 %collective-permute-start.1 = (bf16[2,4,2048]{2,1,0:T(4,128)(2,1)S(1)}, bf16[2,4,2048]{2,1,0:T(4,128)(2,1)S(1)}, u32[]{:S(2)}, u32[]{:S(2)}) collective-permute-start(bf16[2,4,2048]{2,1,0:T(4,128)(2,1)S(1)} %get-tuple-element.5), channel_id=1, source_target_pairs={{0,7},{1,2},{2,1},{3,4},{4,3},{5,6},{6,5},{7,0},{8,15},{9,10},{10,... | collective-permute-start | bytes 98312 | tf_op jit(solution)/shard_map/ppermute | solution.py:16
  13.6 1.5 %collective-permute-start.2 = (bf16[2,4,2048]{2,1,0:T(4,128)(2,1)S(1)}, bf16[2,4,2048]{2,1,0:T(4,128)(2,1)S(1)}, u32[]{:S(2)}, u32[]{:S(2)}) collective-permute-start(bf16[2,4,2048]{2,1,0:T(4,128)(2,1)S(1)} %get-tuple-element.5), channel_id=1, source_target_pairs={{0,6},{1,3},{2,0},{3,5},{4,2},{5,7},{6,4},{7,1},{8,14},{9,11},{10,... | collective-permute-start | bytes 98312 | tf_op jit(solution)/shard_map/ppermute | solution.py:16
  15.1 0.0 collective-permute-done.5
  15.1 1.0 %collective-permute-start.3 = (bf16[2,4,2048]{2,1,0:T(4,128)(2,1)S(1)}, bf16[2,4,2048]{2,1,0:T(4,128)(2,1)S(1)}, u32[]{:S(2)}, u32[]{:S(2)}) collective-permute-start(bf16[2,4,2048]{2,1,0:T(4,128)(2,1)S(1)} %get-tuple-element.5), channel_id=1, source_target_pairs={{0,5},{1,4},{2,7},{3,6},{4,1},{5,0},{6,3},{7,2},{8,13},{9,12},{10,... | collective-permute-start | bytes 98312 | tf_op jit(solution)/shard_map/ppermute | solution.py:16
  16.1 0.0 collective-permute-done.6
  16.1 0.0 collective-permute-done.7
  16.1 0.1 pad_maximum_fusion.mine
  16.2 0.1 collective-permute-start.8
  16.3 0.0 collective-permute-done.1
  16.3 2.1 %collective-permute-done.2 = bf16[2,4,2048]{2,1,0:T(4,128)(2,1)S(1)} collective-permute-done((bf16[2,4,2048]{2,1,0:T(4,128)(2,1)S(1)}, bf16[2,4,2048]{2,1,0:T(4,128)(2,1)S(1)}, u32[]{:S(2)}, u32[]{:S(2)}) %collective-permute-start.2) | collective-permute-done | bytes 32800 | tf_op jit(solution)/shard_map/ppermute | solution.py:16
  18.5 3.9 %collective-permute-done.3 = bf16[2,4,2048]{2,1,0:T(4,128)(2,1)S(1)} collective-permute-done((bf16[2,4,2048]{2,1,0:T(4,128)(2,1)S(1)}, bf16[2,4,2048]{2,1,0:T(4,128)(2,1)S(1)}, u32[]{:S(2)}, u32[]{:S(2)}) %collective-permute-start.3) | collective-permute-done | bytes 32800 | tf_op jit(solution)/shard_map/ppermute | solution.py:16
  22.4 3.1 %collective-permute-start.10 = (bf16[8,4,2048]{2,1,0:T(4,128)(2,1)S(1)}, bf16[8,4,2048]{2,1,0:T(4,128)(2,1)S(1)}, u32[]{:S(2)}, u32[]{:S(2)}) collective-permute-start(bf16[8,4,2048]{2,1,0:T(4,128)(2,1)S(1)} %constant_dynamic-update-slice_fusion.2.own), channel_id=1, source_target_pairs={{0,24},{1,25},{2,26},{3,27},{4,28},{5,29},{6,30},{7,31},{8,0},{9,1... | collective-permute-start | bytes 393224 | tf_op jit(solution)/shard_map/ppermute | solution.py:16
  25.5 0.0 collective-permute-start.9
  25.5 2.2 %collective-permute-start.4 = (bf16[8,4,2048]{2,1,0:T(4,128)(2,1)S(1)}, bf16[8,4,2048]{2,1,0:T(4,128)(2,1)S(1)}, u32[]{:S(2)}, u32[]{:S(2)}) collective-permute-start(bf16[8,4,2048]{2,1,0:T(4,128)(2,1)S(1)} %constant_dynamic-update-slice_fusion.2.own), channel_id=1, source_target_pairs={{0,16},{1,17},{2,18},{3,19},{4,20},{5,21},{6,22},{7,23},{8,24},{9,... | collective-permute-start | bytes 393224 | tf_op jit(solution)/shard_map/ppermute | solution.py:16
  27.7 0.0 collective-permute-done.8.other
  27.7 0.1 shard_map.29.padded
  27.8 0.9 %shard_map.30.so_far = f32[512,256]{1,0:T(8,128)S(1)} custom-call(bf16[8,4,2048]{2,1,0:T(4,128)(2,1)S(1)} %constant_dynamic-update-slice_fusion.2.own, bf16[8,576,128]{2,1,0:T(8,128)(2,1)S(1)} %shard_map.29.padded), custom_call_target="tpu_custom_call" | custom-call | flops 603979776 | bytes 1048576 | tf_op jit(solution)/shard_map/pallas_call | solution.py:124
  28.7 0.0 collective-permute-done.10.after
  28.7 4.3 %collective-permute-done.9.before = bf16[8,4,2048]{2,1,0:T(4,128)(2,1)S(1)} collective-permute-done((bf16[8,4,2048]{2,1,0:T(4,128)(2,1)S(1)}, bf16[8,4,2048]{2,1,0:T(4,128)(2,1)S(1)}, u32[]{:S(2)}, u32[]{:S(2)}) %collective-permute-start.9) | collective-permute-done | bytes 131104 | tf_op jit(solution)/shard_map/ppermute | solution.py:16
  33.0 1.6 %shard_map.31.so_far = f32[512,256]{1,0:T(8,128)S(1)} custom-call(bf16[8,4,2048]{2,1,0:T(4,128)(2,1)S(1)} %collective-permute-done.9.before, bf16[8,4,2048]{2,1,0:T(4,128)(2,1)S(1)} %collective-permute-done.10.after, bf16[8,576,128]{2,1,0:T(8,128)(2,1)S(1)} %shard_map.29.padded, f32[512,256]{1,0:T(8,128)S(1)} %shard_map.30.so_far), custom_call_target="tpu_custom_call" | custom-call | flops 1207959552 | bytes 1048576 | tf_op jit(solution)/shard_map/pallas_call | solution.py:124
  34.6 0.0 collective-permute-done.4.across
  34.6 2.1 %shard_map.32 = bf16[32,8,512]{2,1,0:T(8,128)(2,1)} custom-call(bf16[8,4,2048]{2,1,0:T(4,128)(2,1)S(1)} %collective-permute-done.4.across, bf16[8,576,128]{2,1,0:T(8,128)(2,1)S(1)} %shard_map.29.padded, f32[512,256]{1,0:T(8,128)S(1)} %shard_map.31.so_far), custom_call_target="tpu_custom_call" | custom-call | flops 603979776 | bytes 1048576 | tf_op jit(solution)/shard_map/pallas_call | solution.py:124
  (5 shorter events, 0.1 us)
Async XLA Ops:
  1.0 7.6 %collective-permute-start = (bf16[1,4,2048]{2,1,0:T(4,128)(2,1)S(1)}, bf16[1,4,2048]{2,1,0:T(4,128)(2,1)S(1)}, u32[]{:S(2)}, u32[]{:S(2)}) collective-permute-start(bf16[1,4,2048]{2,1,0:T(4,128)(2,1)S(1)} %reshape.3._), channel_id=1, source_target_pairs={{0,1},{1,0},{2,3},{3,2},{4,5},{5,4},{6,7},{7,6},{8,9},{9,8},{10,11... | collective-permute-start | bytes 49160 | tf_op jit(solution)/shard_map/ppermute | solution.py:16
  3.0 0.9 %copy-start = (bf16[16,8,512]{2,1,0:T(8,128)(2,1)S(1)}, bf16[16,8,512]{2,1,0:T(8,128)(2,1)}, u32[]{:S(2)}) copy-start(bf16[16,8,512]{2,1,0:T(8,128)(2,1)} %traces.1) | copy-start | bytes 393220
  4.3 10.8 %collective-permute-start.5 = (bf16[512,128]{1,0:T(8,128)(2,1)S(1)}, bf16[512,128]{1,0:T(8,128)(2,1)S(1)}, u32[]{:S(2)}, u32[]{:S(2)}) collective-permute-start(bf16[512,128]{1,0:T(8,128)(2,1)S(1)} %shard_map.28), channel_id=1, source_target_pairs={{0,64},{32,96},{64,128},{96,160},{128,192},{160,224},{192,0},{224,... | collective-permute-start | bytes 393224 | tf_op jit(solution)/shard_map/ppermute | solution.py:16
  5.9 10.2 %collective-permute-start.6 = (bf16[512,128]{1,0:T(8,128)(2,1)S(1)}, bf16[512,128]{1,0:T(8,128)(2,1)S(1)}, u32[]{:S(2)}, u32[]{:S(2)}) collective-permute-start(bf16[512,128]{1,0:T(8,128)(2,1)S(1)} %shard_map.28), channel_id=1, source_target_pairs={{0,192},{32,224},{64,0},{96,32},{128,64},{160,96},{192,128},{224,1... | collective-permute-start | bytes 393224 | tf_op jit(solution)/shard_map/ppermute | solution.py:16
  6.4 9.7 %collective-permute-start.7 = (bf16[512,128]{1,0:T(8,128)(2,1)S(1)}, bf16[512,128]{1,0:T(8,128)(2,1)S(1)}, u32[]{:S(2)}, u32[]{:S(2)}) collective-permute-start(bf16[512,128]{1,0:T(8,128)(2,1)S(1)} %shard_map.28), channel_id=1, source_target_pairs={{0,128},{32,160},{64,192},{96,224},{128,0},{160,32},{192,64},{224,... | collective-permute-start | bytes 393224 | tf_op jit(solution)/shard_map/ppermute | solution.py:16
  8.6 7.7 %collective-permute-start.1 = (bf16[2,4,2048]{2,1,0:T(4,128)(2,1)S(1)}, bf16[2,4,2048]{2,1,0:T(4,128)(2,1)S(1)}, u32[]{:S(2)}, u32[]{:S(2)}) collective-permute-start(bf16[2,4,2048]{2,1,0:T(4,128)(2,1)S(1)} %get-tuple-element.5), channel_id=1, source_target_pairs={{0,7},{1,2},{2,1},{3,4},{4,3},{5,6},{6,5},{7,0},{8,15},{9,10},{10,... | collective-permute-start | bytes 98312 | tf_op jit(solution)/shard_map/ppermute | solution.py:16
  13.6 4.8 %collective-permute-start.2 = (bf16[2,4,2048]{2,1,0:T(4,128)(2,1)S(1)}, bf16[2,4,2048]{2,1,0:T(4,128)(2,1)S(1)}, u32[]{:S(2)}, u32[]{:S(2)}) collective-permute-start(bf16[2,4,2048]{2,1,0:T(4,128)(2,1)S(1)} %get-tuple-element.5), channel_id=1, source_target_pairs={{0,6},{1,3},{2,0},{3,5},{4,2},{5,7},{6,4},{7,1},{8,14},{9,11},{10,... | collective-permute-start | bytes 98312 | tf_op jit(solution)/shard_map/ppermute | solution.py:16
  15.1 7.3 %collective-permute-start.3 = (bf16[2,4,2048]{2,1,0:T(4,128)(2,1)S(1)}, bf16[2,4,2048]{2,1,0:T(4,128)(2,1)S(1)}, u32[]{:S(2)}, u32[]{:S(2)}) collective-permute-start(bf16[2,4,2048]{2,1,0:T(4,128)(2,1)S(1)} %get-tuple-element.5), channel_id=1, source_target_pairs={{0,5},{1,4},{2,7},{3,6},{4,1},{5,0},{6,3},{7,2},{8,13},{9,12},{10,... | collective-permute-start | bytes 98312 | tf_op jit(solution)/shard_map/ppermute | solution.py:16
  16.2 11.5 %collective-permute-start.8 = (bf16[4,512,128]{2,1,0:T(8,128)(2,1)S(1)}, bf16[4,512,128]{2,1,0:T(8,128)(2,1)S(1)}, u32[]{:S(2)}, u32[]{:S(2)}) collective-permute-start(bf16[4,512,128]{2,1,0:T(8,128)(2,1)S(1)} %pad_maximum_fusion.mine), channel_id=1, source_target_pairs={{0,32},{32,0},{64,96},{96,64},{128,160},{160,128},{192,224},{224,1... | collective-permute-start | bytes 1572872 | tf_op jit(solution)/shard_map/ppermute | solution.py:16
  22.4 6.4 %collective-permute-start.10 = (bf16[8,4,2048]{2,1,0:T(4,128)(2,1)S(1)}, bf16[8,4,2048]{2,1,0:T(4,128)(2,1)S(1)}, u32[]{:S(2)}, u32[]{:S(2)}) collective-permute-start(bf16[8,4,2048]{2,1,0:T(4,128)(2,1)S(1)} %constant_dynamic-update-slice_fusion.2.own), channel_id=1, source_target_pairs={{0,24},{1,25},{2,26},{3,27},{4,28},{5,29},{6,30},{7,31},{8,0},{9,1... | collective-permute-start | bytes 393224 | tf_op jit(solution)/shard_map/ppermute | solution.py:16
  25.5 7.6 %collective-permute-start.9 = (bf16[8,4,2048]{2,1,0:T(4,128)(2,1)S(1)}, bf16[8,4,2048]{2,1,0:T(4,128)(2,1)S(1)}, u32[]{:S(2)}, u32[]{:S(2)}) collective-permute-start(bf16[8,4,2048]{2,1,0:T(4,128)(2,1)S(1)} %constant_dynamic-update-slice_fusion.2.own), channel_id=1, source_target_pairs={{0,8},{1,9},{2,10},{3,11},{4,12},{5,13},{6,14},{7,15},{8,16},{9,17... | collective-permute-start | bytes 393224 | tf_op jit(solution)/shard_map/ppermute | solution.py:16
  25.5 9.2 %collective-permute-start.4 = (bf16[8,4,2048]{2,1,0:T(4,128)(2,1)S(1)}, bf16[8,4,2048]{2,1,0:T(4,128)(2,1)S(1)}, u32[]{:S(2)}, u32[]{:S(2)}) collective-permute-start(bf16[8,4,2048]{2,1,0:T(4,128)(2,1)S(1)} %constant_dynamic-update-slice_fusion.2.own), channel_id=1, source_target_pairs={{0,16},{1,17},{2,18},{3,19},{4,20},{5,21},{6,22},{7,23},{8,24},{9,... | collective-permute-start | bytes 393224 | tf_op jit(solution)/shard_map/ppermute | solution.py:16

commit v4 on v3

--- a/solution.py
+++ b/solution.py
@@ -6,8 +6,9 @@
 from jax.sharding import PartitionSpec as P
 
 RING4 = (0, 1, 3, 2)
-RING8 = (0, 1, 7, 6, 2, 3, 5, 4)
+RING8 = (0, 1, 2, 3, 7, 6, 5, 4)
 VMEM = pl.BlockSpec(memory_space=pltpu.VMEM)
+JOIN_COST = 2**33
 PARAMS = pltpu.CompilerParams(vmem_limit_bytes=40 * 2**20)
 
 
@@ -18,6 +19,20 @@
 
 def sign(coordinate):
     return 1 - 2 * (coordinate % 2)
+
+
+def prepare_response(response, out, rows, turned):
+    wide = response[...].astype(jnp.float32)
+    rows[...] = jnp.concatenate([wide, jnp.zeros((128, 64), jnp.float32)], axis=1)
+    by_position = jnp.concatenate([rows[pl.ds(k, 32, stride=4), :] for k in range(4)], axis=0)
+    turned[...] = by_position.T[:64, :]
+    skewed = [pltpu.roll(turned[pl.ds(u, 16, stride=4), :], 32 * u, 1) for u in range(4)]
+    lane_block = lax.broadcasted_iota(jnp.int32, (16, 128), 1) // 32
+    for k in range(4):
+        mixed = skewed[0]
+        for u in range(1, 4):
+            mixed = jnp.where(lane_block == (k + u) % 4, skewed[u], mixed)
+        out[k * 16 : k * 16 + 16, :] = pltpu.roll(mixed, (128 - 32 * k) % 128, 1).astype(jnp.bfloat16)
 
 
 def prepare_traces(traces, _, out, rows, turned):
@@ -37,14 +52,22 @@
     out[...] = turned[...].astype(jnp.bfloat16)
 
 
-def assemble(mine, other, out):
+def assemble(own, after, before, across, others, other_across, out):
     shot = lax.axis_index("shot")
     x, core = shot // 2, shot % 2
-    for blocks, side in ((mine, core), (other, 1 - core)):
+    mine = (own, after, before, across)
+    theirs = (others.at[0], others.at[1], others.at[2], other_across)
+    for blocks, side in ((mine, core), (theirs, 1 - core)):
         for slot in range(4):
             place = ((x + 4 - RING4[slot]) % 4) * 2 + side
             out[place, :64, :] = jnp.zeros((64, 128), jnp.bfloat16)
-            out[place, 64:, :] = blocks[slot]
+            out[place, 64:, :] = blocks[slot][...]
+
+
+def join(first, second, out):
+    count = first.shape[0]
+    out[:count] = first[...]
+    out[count:] = second[...]
 
 
 def position_of(offset):
@@ -54,16 +77,20 @@
     return slot
 
 
-def add_products(offsets, responses, padded, band, total):
+def add_products(offsets, responses, padded, band, rows_f32, total):
     rcv = lax.axis_index("rcv")
     y, z = rcv // 8, rcv % 8
     slots = [position_of((sign(z) * (wanted - z) + 64) % 8) for wanted in range(8)]
     for response, offset in zip(responses, offsets, strict=True):
         for half in range(2):
-            rows = jnp.concatenate(
-                [response[slots[half * 4 + q]].astype(jnp.float32) for q in range(4)], axis=0
+            for q in range(4):
+                piece = response[slots[half * 4 + q]]
+                rows_f32[half, q * 64 : q * 64 + 64, :] = piece.astype(jnp.float32)
+            wide = jnp.concatenate(
+                [rows_f32[half, pl.ds(m, 16, stride=16), :] for m in range(16)]
+                + [jnp.zeros((16, 384), jnp.float32)],
+                axis=1,
             )
-            wide = jnp.concatenate([rows, jnp.zeros((16, 384), jnp.float32)], axis=1)
             for shift in range(4):
                 band[half, shift * 16 : shift * 16 + 16, :] = pltpu.roll(
                     wide, 128 + 32 * shift, 1
@@ -93,19 +120,19 @@
         total[8:, :] += odd[:504, :]
 
 
-def first_kernel(own, padded, total, band):
+def first_kernel(own, padded, total, band, rows):
     total[...] = jnp.zeros_like(total)
-    add_products((0,), (own,), padded, band, total)
-
-
-def middle_kernel(before, after, padded, so_far, total, band):
+    add_products((0,), (own,), padded, band, rows, total)
+
+
+def middle_kernel(before, after, padded, so_far, total, band, rows):
     total[...] = so_far[...]
-    add_products((1, 3), (before, after), padded, band, total)
-
-
-def last_kernel(across, padded, so_far, out, band, total, placed):
+    add_products((1, 3), (before, after), padded, band, rows, total)
+
+
+def last_kernel(across, padded, so_far, out, band, rows, total, placed):
     total[...] = so_far[...]
-    add_products((2,), (across,), padded, band, total)
+    add_products((2,), (across,), padded, band, rows, total)
     turned = total[...].T
     skewed = [pltpu.roll(turned[u * 32 : u * 32 + 32, :], u, 1) for u in range(8)]
     lane = lax.broadcasted_iota(jnp.int32, (32, 512), 1)
@@ -134,7 +161,7 @@
 
 def shards(response, traces):
     f32, bf16 = jnp.float32, jnp.bfloat16
-    band = ((2, 64, 19 * 128), bf16)
+    band = [((2, 64, 19 * 128), bf16), ((2, 256, 128), f32)]
 
     def along_z(step):
         return lambda i: (i // 8) * 8 + step(i % 8) % 8
@@ -145,25 +172,38 @@
     def along_x(offset):
         return lambda i: ((i // 2 + offset) % 4) * 2 + i % 2
 
-    held = jnp.transpose(response, (1, 2, 0)).reshape(1, 4, 2048)
+    def swap(value):
+        return spread(value, "shot", lambda i: i ^ 1)
+
+    held = call(
+        prepare_response,
+        (64, 128),
+        bf16,
+        (response.reshape(128, 64),),
+        [((128, 128), f32), ((64, 128), f32)],
+    )
+    held = held[None]
     piece = call(prepare_traces, (512, 128), bf16, (traces, held), [((4, 128, 128), f32), ((512, 128), f32)])
-    held = jnp.concatenate([held, spread(held, "rcv", along_z(lambda z: z + sign(z)))], axis=0)
-    steps = [lambda z: z - sign(z), lambda z: z - 2 * sign(z), lambda z: z - 3 * sign(z)]
-    held = jnp.concatenate([held] + [spread(held, "rcv", along_z(step)) for step in steps], axis=0)
+    for step in (lambda z: z + sign(z), lambda z: z - 2 * sign(z), lambda z: z - sign(z)):
+        arrived = spread(held, "rcv", along_z(step))
+        held = call(join, (2 * held.shape[0], 64, 128), bf16, (held, arrived), [], JOIN_COST)
     before, after, across = [spread(held, "rcv", along_y(offset)) for offset in (1, 3, 2)]
 
-    mine = jnp.stack([piece] + [spread(piece, "shot", along_x(offset)) for offset in (1, 3, 2)])
-    other = spread(mine, "shot", lambda i: i ^ 1)
-    padded = call(assemble, (8, 576, 128), bf16, (mine, other), [])
+    next_piece = spread(piece, "shot", along_x(1))
+    previous_piece = spread(piece, "shot", along_x(3))
+    far_piece = spread(next_piece, "shot", along_x(1))
+    others = swap(jnp.stack([piece, next_piece, previous_piece]))
+    pieces = (piece, next_piece, previous_piece, far_piece, others, swap(far_piece))
+    padded = call(assemble, (8, 576, 128), bf16, pieces, [])
     work = 2 * 512 * 256 * 9 * 256
-    total = call(first_kernel, (512, 256), f32, (held, padded), [band], work)
-    total = call(middle_kernel, (512, 256), f32, (before, after, padded, total), [band], 2 * work)
+    total = call(first_kernel, (512, 256), f32, (held, padded), band, work)
+    total = call(middle_kernel, (512, 256), f32, (before, after, padded, total), band, 2 * work)
     return call(
         last_kernel,
         (32, 8, 512),
         bf16,
         (across, padded, total),
-        [band, ((512, 256), f32), ((4, 256, 128), f32)],
+        band + [((512, 256), f32), ((4, 256, 128), f32)],
         work,
     )
 

time: 36.9 us -> 37.1 us (level)
  the two profiles are of different devices: /device:TPU:2 before, /device:TPU:1 now
where the time goes in v4:
time: 37.1 us; the launch traced here: 36.9 us
  starting transfers between devices  23.2 us (63%)
  waiting for transfers between devices  6.46 us (17%)
  Pallas kernels  5.44 us (15%)
  local copies, waits for them, and re-layouts  1.66 us (4%)
    ppermute x11, starting transfers between devices, spread(): return lax.ppermute(value, axis, [(i, partner(i)) for i in range(size)])  23.2 us
    ppermute x11, waiting for transfers between devices, spread(): return lax.ppermute(value, axis, [(i, partner(i)) for i in range(size)])  6.46 us
    pallas_call x9, Pallas kernels, call(): pl.pallas_call(body, out_shape=jax.ShapeDtypeStruct(shape, dtype), in_spe...  5.44 us
    unnamed x4, local copies, waits for them, and re-layouts  1.66 us
  transfers between devices with their start and end apart: 11, of which 3 were waited for; matrix products, arithmetic and copies ran while one was open for 0% of the time, Pallas kernels for 8%

profile of v4, /device:TPU:1, one launch (start us, length us, event | category | flops | bytes accessed | tf_op | source)
XLA Modules:
  0.0 36.9 jit_solution(11009547878926585944)
XLA Ops:
  0.0 0.0 copy-start.1
  0.0 0.8 %copy-done.1 = bf16[32,4,64]{2,1,0:T(4,128)(2,1)S(1)} copy-done((bf16[32,4,64]{2,1,0:T(4,128)(2,1)S(1)}, bf16[32,4,64]{2,1,0:T(4,128)(2,1)}, u32[]{:S(2)}) %copy-start.1) | copy-done | bytes 16408
  0.8 0.2 shard_map.28
  1.0 2.5 %collective-permute-start = (bf16[1,64,128]{2,1,0:T(8,128)(2,1)S(1)}, bf16[1,64,128]{2,1,0:T(8,128)(2,1)S(1)}, u32[]{:S(2)}, u32[]{:S(2)}) collective-permute-start(bf16[1,64,128]{2,1,0:T(8,128)(2,1)S(1)} %bitcast.8), channel_id=1, source_target_pairs={{0,1},{1,0},{2,3},{3,2},{4,5},{5,4},{6,7},{7,6},{8,9},{9,8},{10,11... | collective-permute-start | bytes 49160 | tf_op jit(solution)/shard_map/ppermute | solution.py:17
  3.5 0.0 copy-start
  3.5 0.9 %copy-done = bf16[16,8,512]{2,1,0:T(8,128)(2,1)S(1)} copy-done((bf16[16,8,512]{2,1,0:T(8,128)(2,1)S(1)}, bf16[16,8,512]{2,1,0:T(8,128)(2,1)}, u32[]{:S(2)}) %copy-start) | copy-done | bytes 131096
  4.4 0.4 %shard_map.32.own = bf16[512,128]{1,0:T(8,128)(2,1)S(1)} custom-call(bf16[16,8,512]{2,1,0:T(8,128)(2,1)S(1)} %copy-done, bf16[1,64,128]{2,1,0:T(8,128)(2,1)S(1)} %bitcast.9), custom_call_target="tpu_custom_call" | custom-call | bytes 1048576 | tf_op jit(solution)/shard_map/pallas_call | solution.py:151
  4.8 1.3 %collective-permute-start.4 = (bf16[512,128]{1,0:T(8,128)(2,1)S(1)}, bf16[512,128]{1,0:T(8,128)(2,1)S(1)}, u32[]{:S(2)}, u32[]{:S(2)}) collective-permute-start(bf16[512,128]{1,0:T(8,128)(2,1)S(1)} %shard_map.32.own), channel_id=1, source_target_pairs={{0,64},{32,96},{64,128},{96,160},{128,192},{160,224},{192,0},{224,... | collective-permute-start | bytes 393224 | tf_op jit(solution)/shard_map/ppermute | solution.py:17
  6.1 0.0 collective-permute-done.second
  6.1 5.1 %collective-permute-start.1 = (bf16[2,64,128]{2,1,0:T(8,128)(2,1)S(1)}, bf16[2,64,128]{2,1,0:T(8,128)(2,1)S(1)}, u32[]{:S(2)}, u32[]{:S(2)}) collective-permute-start(bf16[2,64,128]{2,1,0:T(8,128)(2,1)S(1)} %shard_map.29.first), channel_id=1, source_target_pairs={{0,6},{1,3},{2,0},{3,5},{4,2},{5,7},{6,4},{7,1},{8,14},{9,11},{10,... | collective-permute-start | bytes 98312 | tf_op jit(solution)/shard_map/ppermute | solution.py:17
  11.2 1.7 %collective-permute-start.5 = (bf16[512,128]{1,0:T(8,128)(2,1)S(1)}, bf16[512,128]{1,0:T(8,128)(2,1)S(1)}, u32[]{:S(2)}, u32[]{:S(2)}) collective-permute-start(bf16[512,128]{1,0:T(8,128)(2,1)S(1)} %shard_map.32.own), channel_id=1, source_target_pairs={{0,192},{32,224},{64,0},{96,32},{128,64},{160,96},{192,128},{224,1... | collective-permute-start | bytes 393224 | tf_op jit(solution)/shard_map/ppermute | solution.py:17
  13.0 0.0 collective-permute-done.4.after
  13.0 0.0 collective-permute-start.6
  13.0 0.0 collective-permute-done.1.second
  13.0 1.7 %collective-permute-start.2 = (bf16[4,64,128]{2,1,0:T(8,128)(2,1)S(1)}, bf16[4,64,128]{2,1,0:T(8,128)(2,1)S(1)}, u32[]{:S(2)}, u32[]{:S(2)}) collective-permute-start(bf16[4,64,128]{2,1,0:T(8,128)(2,1)S(1)} %shard_map.30.first), channel_id=1, source_target_pairs={{0,7},{1,2},{2,1},{3,4},{4,3},{5,6},{6,5},{7,0},{8,15},{9,10},{10,... | collective-permute-start | bytes 196616 | tf_op jit(solution)/shard_map/ppermute | solution.py:17
  14.7 0.4 collective-permute-done.5.before
  15.1 2.9 %collective-permute-start.7 = (bf16[3,512,128]{2,1,0:T(8,128)(2,1)S(1)}, bf16[3,512,128]{2,1,0:T(8,128)(2,1)S(1)}, u32[]{:S(2)}, u32[]{:S(2)}) collective-permute-start(bf16[3,512,128]{2,1,0:T(8,128)(2,1)S(1)} %pad_maximum_fusion), channel_id=1, source_target_pairs={{0,32},{32,0},{64,96},{96,64},{128,160},{160,128},{192,224},{224,1... | collective-permute-start | bytes 1179656 | tf_op jit(solution)/shard_map/ppermute | solution.py:17
  18.0 0.0 collective-permute-done.6.across
  18.0 3.5 %collective-permute-start.8 = (bf16[512,128]{1,0:T(8,128)(2,1)S(1)}, bf16[512,128]{1,0:T(8,128)(2,1)S(1)}, u32[]{:S(2)}, u32[]{:S(2)}) collective-permute-start(bf16[512,128]{1,0:T(8,128)(2,1)S(1)} %collective-permute-done.6.across), channel_id=1, source_target_pairs={{0,32},{32,0},{64,96},{96,64},{128,160},{160,128},{192,224},{224,1... | collective-permute-start | bytes 393224 | tf_op jit(solution)/shard_map/ppermute | solution.py:17
  21.5 0.0 collective-permute-done.2.second
  21.5 2.8 %collective-permute-start.10 = (bf16[8,64,128]{2,1,0:T(8,128)(2,1)S(1)}, bf16[8,64,128]{2,1,0:T(8,128)(2,1)S(1)}, u32[]{:S(2)}, u32[]{:S(2)}) collective-permute-start(bf16[8,64,128]{2,1,0:T(8,128)(2,1)S(1)} %shard_map.31.own), channel_id=1, source_target_pairs={{0,24},{1,25},{2,26},{3,27},{4,28},{5,29},{6,30},{7,31},{8,0},{9,1... | collective-permute-start | bytes 393224 | tf_op jit(solution)/shard_map/ppermute | solution.py:17
  24.3 0.0 collective-permute-start.9
  24.4 1.6 %collective-permute-start.3 = (bf16[8,64,128]{2,1,0:T(8,128)(2,1)S(1)}, bf16[8,64,128]{2,1,0:T(8,128)(2,1)S(1)}, u32[]{:S(2)}, u32[]{:S(2)}) collective-permute-start(bf16[8,64,128]{2,1,0:T(8,128)(2,1)S(1)} %shard_map.31.own), channel_id=1, source_target_pairs={{0,16},{1,17},{2,18},{3,19},{4,20},{5,21},{6,22},{7,23},{8,24},{9,... | collective-permute-start | bytes 393224 | tf_op jit(solution)/shard_map/ppermute | solution.py:17
  26.0 0.0 collective-permute-done.8.other_across
  26.0 0.0 collective-permute-done.7.others
  26.0 0.1 shard_map.33.padded
  26.1 1.0 %shard_map.34.so_far = f32[512,256]{1,0:T(8,128)S(1)} custom-call(bf16[8,64,128]{2,1,0:T(8,128)(2,1)S(1)} %shard_map.31.own, bf16[8,576,128]{2,1,0:T(8,128)(2,1)S(1)} %shard_map.33.padded), custom_call_target="tpu_custom_call" | custom-call | flops 603979776 | bytes 1048576 | tf_op jit(solution)/shard_map/pallas_call | solution.py:151
  27.1 0.2 collective-permute-done.10.after
  27.3 5.9 %collective-permute-done.9.before = bf16[8,64,128]{2,1,0:T(8,128)(2,1)S(1)} collective-permute-done((bf16[8,64,128]{2,1,0:T(8,128)(2,1)S(1)}, bf16[8,64,128]{2,1,0:T(8,128)(2,1)S(1)}, u32[]{:S(2)}, u32[]{:S(2)}) %collective-permute-start.9) | collective-permute-done | bytes 131104 | tf_op jit(solution)/shard_map/ppermute | solution.py:17
  33.2 1.6 %shard_map.35.so_far = f32[512,256]{1,0:T(8,128)S(1)} custom-call(bf16[8,64,128]{2,1,0:T(8,128)(2,1)S(1)} %collective-permute-done.9.before, bf16[8,64,128]{2,1,0:T(8,128)(2,1)S(1)} %collective-permute-done.10.after, bf16[8,576,128]{2,1,0:T(8,128)(2,1)S(1)} %shard_map.33.padded, f32[512,256]{1,0:T(8,128)S(1)} %shard_map.34.so_far), custom_call_target="tpu_custom_call" | custom-call | flops 1207959552 | bytes 1048576 | tf_op jit(solution)/shard_map/pallas_call | solution.py:151
  34.8 0.0 collective-permute-done.3.across
  34.8 2.1 %shard_map.36 = bf16[32,8,512]{2,1,0:T(8,128)(2,1)} custom-call(bf16[8,64,128]{2,1,0:T(8,128)(2,1)S(1)} %collective-permute-done.3.across, bf16[8,576,128]{2,1,0:T(8,128)(2,1)S(1)} %shard_map.33.padded, f32[512,256]{1,0:T(8,128)S(1)} %shard_map.35.so_far), custom_call_target="tpu_custom_call" | custom-call | flops 603979776 | bytes 1048576 | tf_op jit(solution)/shard_map/pallas_call | solution.py:151
  (4 shorter events, 0.1 us)
Async XLA Ops:
  0.0 0.8 %copy-start.1 = (bf16[32,4,64]{2,1,0:T(4,128)(2,1)S(1)}, bf16[32,4,64]{2,1,0:T(4,128)(2,1)}, u32[]{:S(2)}) copy-start(bf16[32,4,64]{2,1,0:T(4,128)(2,1)} %param.2) | copy-start | bytes 49156
  1.0 5.1 %collective-permute-start = (bf16[1,64,128]{2,1,0:T(8,128)(2,1)S(1)}, bf16[1,64,128]{2,1,0:T(8,128)(2,1)S(1)}, u32[]{:S(2)}, u32[]{:S(2)}) collective-permute-start(bf16[1,64,128]{2,1,0:T(8,128)(2,1)S(1)} %bitcast.8), channel_id=1, source_target_pairs={{0,1},{1,0},{2,3},{3,2},{4,5},{5,4},{6,7},{7,6},{8,9},{9,8},{10,11... | collective-permute-start | bytes 49160 | tf_op jit(solution)/shard_map/ppermute | solution.py:17
  3.5 0.9 %copy-start = (bf16[16,8,512]{2,1,0:T(8,128)(2,1)S(1)}, bf16[16,8,512]{2,1,0:T(8,128)(2,1)}, u32[]{:S(2)}) copy-start(bf16[16,8,512]{2,1,0:T(8,128)(2,1)} %traces.1) | copy-start | bytes 393220
  4.8 8.1 %collective-permute-start.4 = (bf16[512,128]{1,0:T(8,128)(2,1)S(1)}, bf16[512,128]{1,0:T(8,128)(2,1)S(1)}, u32[]{:S(2)}, u32[]{:S(2)}) collective-permute-start(bf16[512,128]{1,0:T(8,128)(2,1)S(1)} %shard_map.32.own), channel_id=1, source_target_pairs={{0,64},{32,96},{64,128},{96,160},{128,192},{160,224},{192,0},{224,... | collective-permute-start | bytes 393224 | tf_op jit(solution)/shard_map/ppermute | solution.py:17
  6.1 6.8 %collective-permute-start.1 = (bf16[2,64,128]{2,1,0:T(8,128)(2,1)S(1)}, bf16[2,64,128]{2,1,0:T(8,128)(2,1)S(1)}, u32[]{:S(2)}, u32[]{:S(2)}) collective-permute-start(bf16[2,64,128]{2,1,0:T(8,128)(2,1)S(1)} %shard_map.29.first), channel_id=1, source_target_pairs={{0,6},{1,3},{2,0},{3,5},{4,2},{5,7},{6,4},{7,1},{8,14},{9,11},{10,... | collective-permute-start | bytes 98312 | tf_op jit(solution)/shard_map/ppermute | solution.py:17
  11.2 3.8 %collective-permute-start.5 = (bf16[512,128]{1,0:T(8,128)(2,1)S(1)}, bf16[512,128]{1,0:T(8,128)(2,1)S(1)}, u32[]{:S(2)}, u32[]{:S(2)}) collective-permute-start(bf16[512,128]{1,0:T(8,128)(2,1)S(1)} %shard_map.32.own), channel_id=1, source_target_pairs={{0,192},{32,224},{64,0},{96,32},{128,64},{160,96},{192,128},{224,1... | collective-permute-start | bytes 393224 | tf_op jit(solution)/shard_map/ppermute | solution.py:17
  13.0 5.0 %collective-permute-start.6 = (bf16[512,128]{1,0:T(8,128)(2,1)S(1)}, bf16[512,128]{1,0:T(8,128)(2,1)S(1)}, u32[]{:S(2)}, u32[]{:S(2)}) collective-permute-start(bf16[512,128]{1,0:T(8,128)(2,1)S(1)} %collective-permute-done.4.after), channel_id=1, source_target_pairs={{0,64},{32,96},{64,128},{96,160},{128,192},{160,224},{192,0},{224,... | collective-permute-start | bytes 393224 | tf_op jit(solution)/shard_map/ppermute | solution.py:17
  13.0 8.5 %collective-permute-start.2 = (bf16[4,64,128]{2,1,0:T(8,128)(2,1)S(1)}, bf16[4,64,128]{2,1,0:T(8,128)(2,1)S(1)}, u32[]{:S(2)}, u32[]{:S(2)}) collective-permute-start(bf16[4,64,128]{2,1,0:T(8,128)(2,1)S(1)} %shard_map.30.first), channel_id=1, source_target_pairs={{0,7},{1,2},{2,1},{3,4},{4,3},{5,6},{6,5},{7,0},{8,15},{9,10},{10,... | collective-permute-start | bytes 196616 | tf_op jit(solution)/shard_map/ppermute | solution.py:17
  15.1 10.9 %collective-permute-start.7 = (bf16[3,512,128]{2,1,0:T(8,128)(2,1)S(1)}, bf16[3,512,128]{2,1,0:T(8,128)(2,1)S(1)}, u32[]{:S(2)}, u32[]{:S(2)}) collective-permute-start(bf16[3,512,128]{2,1,0:T(8,128)(2,1)S(1)} %pad_maximum_fusion), channel_id=1, source_target_pairs={{0,32},{32,0},{64,96},{96,64},{128,160},{160,128},{192,224},{224,1... | collective-permute-start | bytes 1179656 | tf_op jit(solution)/shard_map/ppermute | solution.py:17
  18.0 8.0 %collective-permute-start.8 = (bf16[512,128]{1,0:T(8,128)(2,1)S(1)}, bf16[512,128]{1,0:T(8,128)(2,1)S(1)}, u32[]{:S(2)}, u32[]{:S(2)}) collective-permute-start(bf16[512,128]{1,0:T(8,128)(2,1)S(1)} %collective-permute-done.6.across), channel_id=1, source_target_pairs={{0,32},{32,0},{64,96},{96,64},{128,160},{160,128},{192,224},{224,1... | collective-permute-start | bytes 393224 | tf_op jit(solution)/shard_map/ppermute | solution.py:17
  21.5 5.7 %collective-permute-start.10 = (bf16[8,64,128]{2,1,0:T(8,128)(2,1)S(1)}, bf16[8,64,128]{2,1,0:T(8,128)(2,1)S(1)}, u32[]{:S(2)}, u32[]{:S(2)}) collective-permute-start(bf16[8,64,128]{2,1,0:T(8,128)(2,1)S(1)} %shard_map.31.own), channel_id=1, source_target_pairs={{0,24},{1,25},{2,26},{3,27},{4,28},{5,29},{6,30},{7,31},{8,0},{9,1... | collective-permute-start | bytes 393224 | tf_op jit(solution)/shard_map/ppermute | solution.py:17
  24.3 8.8 %collective-permute-start.9 = (bf16[8,64,128]{2,1,0:T(8,128)(2,1)S(1)}, bf16[8,64,128]{2,1,0:T(8,128)(2,1)S(1)}, u32[]{:S(2)}, u32[]{:S(2)}) collective-permute-start(bf16[8,64,128]{2,1,0:T(8,128)(2,1)S(1)} %shard_map.31.own), channel_id=1, source_target_pairs={{0,8},{1,9},{2,10},{3,11},{4,12},{5,13},{6,14},{7,15},{8,16},{9,17... | collective-permute-start | bytes 393224 | tf_op jit(solution)/shard_map/ppermute | solution.py:17
  24.4 10.4 %collective-permute-start.3 = (bf16[8,64,128]{2,1,0:T(8,128)(2,1)S(1)}, bf16[8,64,128]{2,1,0:T(8,128)(2,1)S(1)}, u32[]{:S(2)}, u32[]{:S(2)}) collective-permute-start(bf16[8,64,128]{2,1,0:T(8,128)(2,1)S(1)} %shard_map.31.own), channel_id=1, source_target_pairs={{0,16},{1,17},{2,18},{3,19},{4,20},{5,21},{6,22},{7,23},{8,24},{9,... | collective-permute-start | bytes 393224 | tf_op jit(solution)/shard_map/ppermute | solution.py:17

commit v5 on v4

--- a/solution.py
+++ b/solution.py
@@ -1,3 +1,5 @@
+import functools
+
 import jax
 import jax.numpy as jnp
 from jax import lax
@@ -5,7 +7,6 @@
 from jax.experimental.pallas import tpu as pltpu
 from jax.sharding import PartitionSpec as P
 
-RING4 = (0, 1, 3, 2)
 RING8 = (0, 1, 2, 3, 7, 6, 5, 4)
 VMEM = pl.BlockSpec(memory_space=pltpu.VMEM)
 JOIN_COST = 2**33
@@ -35,33 +36,42 @@
         out[k * 16 : k * 16 + 16, :] = pltpu.roll(mixed, (128 - 32 * k) % 128, 1).astype(jnp.bfloat16)
 
 
-def prepare_traces(traces, _, out, rows, turned):
-    for part in range(4):
-        lanes = traces[:, :, part * 128 : part * 128 + 128]
-        rows[part] = lanes.astype(jnp.float32).reshape(128, 128)
-    for part in range(4):
-        by_receiver = [rows[part, pl.ds(r, 16, stride=8), :] for r in range(8)]
-        turned[part * 128 : part * 128 + 128, :] = jnp.concatenate(by_receiver, axis=0).T
-    skewed = [pltpu.roll(turned[pl.ds(d, 64, stride=8), :], 16 * d, 1) for d in range(8)]
+def prepare_traces(own, other, _, out, rows, turned):
     lane_block = lax.broadcasted_iota(jnp.int32, (64, 128), 1) // 16
-    for r in range(8):
-        mixed = skewed[0]
-        for d in range(1, 8):
-            mixed = jnp.where(lane_block == (r + d) % 8, skewed[d], mixed)
-        turned[pl.ds(r, 64, stride=8), :] = pltpu.roll(mixed, (128 - 16 * r) % 128, 1)
-    out[...] = turned[...].astype(jnp.bfloat16)
-
-
-def assemble(own, after, before, across, others, other_across, out):
+    for side, traces in enumerate((own, other)):
+        for part in range(4):
+            lanes = traces[:, :, part * 128 : part * 128 + 128]
+            rows[side, part] = lanes.astype(jnp.float32).reshape(128, 128)
+        for part in range(4):
+            by_receiver = [rows[side, part, pl.ds(r, 16, stride=8), :] for r in range(8)]
+            turned[side, part * 128 : part * 128 + 128, :] = jnp.concatenate(by_receiver, axis=0).T
+        skewed = [pltpu.roll(turned[side, pl.ds(d, 64, stride=8), :], 16 * d, 1) for d in range(8)]
+        for r in range(8):
+            mixed = skewed[0]
+            for d in range(1, 8):
+                mixed = jnp.where(lane_block == (r + d) % 8, skewed[d], mixed)
+            turned[side, pl.ds(r, 64, stride=8), :] = pltpu.roll(mixed, (128 - 16 * r) % 128, 1)
+        out[side] = turned[side].astype(jnp.bfloat16)
+
+
+def assemble(own, near, near_swapped, far, far_swapped, out):
     shot = lax.axis_index("shot")
     x, core = shot // 2, shot % 2
-    mine = (own, after, before, across)
-    theirs = (others.at[0], others.at[1], others.at[2], other_across)
-    for blocks, side in ((mine, core), (theirs, 1 - core)):
-        for slot in range(4):
-            place = ((x + 4 - RING4[slot]) % 4) * 2 + side
-            out[place, :64, :] = jnp.zeros((64, 128), jnp.bfloat16)
-            out[place, 64:, :] = blocks[slot][...]
+    back = 4 - sign(core)
+    blocks = (
+        (own.at[0], x, core),
+        (own.at[1], x, 1 - core),
+        (near.at[0], x + back, core),
+        (near.at[1], x + back, 1 - core),
+        (near_swapped.at[0], x + 8 - back, 1 - core),
+        (near_swapped.at[1], x + 8 - back, core),
+        (far, x + 2, core),
+        (far_swapped, x + 2, 1 - core),
+    )
+    for block, chip, side in blocks:
+        place = (chip % 4) * 2 + side
+        out[place, :64, :] = jnp.zeros((64, 128), jnp.bfloat16)
+        out[place, 64:, :] = block[...]
 
 
 def join(first, second, out):
@@ -125,9 +135,9 @@
     add_products((0,), (own,), padded, band, rows, total)
 
 
-def middle_kernel(before, after, padded, so_far, total, band, rows):
+def middle_kernel(offset, response, padded, so_far, total, band, rows):
     total[...] = so_far[...]
-    add_products((1, 3), (before, after), padded, band, rows, total)
+    add_products((offset,), (response,), padded, band, rows, total)
 
 
 def last_kernel(across, padded, so_far, out, band, rows, total, placed):
@@ -169,8 +179,8 @@
     def along_y(offset):
         return lambda i: (i // 8 + offset) % 4 * 8 + i % 8
 
-    def along_x(offset):
-        return lambda i: ((i // 2 + offset) % 4) * 2 + i % 2
+    def along_x(i):
+        return ((i // 2 + sign(i)) % 4) * 2 + i % 2
 
     def swap(value):
         return spread(value, "shot", lambda i: i ^ 1)
@@ -183,21 +193,27 @@
         [((128, 128), f32), ((64, 128), f32)],
     )
     held = held[None]
-    piece = call(prepare_traces, (512, 128), bf16, (traces, held), [((4, 128, 128), f32), ((512, 128), f32)])
+    both = call(
+        prepare_traces,
+        (2, 512, 128),
+        bf16,
+        (traces, swap(traces), held),
+        [((2, 4, 128, 128), f32), ((2, 512, 128), f32)],
+    )
     for step in (lambda z: z + sign(z), lambda z: z - 2 * sign(z), lambda z: z - sign(z)):
         arrived = spread(held, "rcv", along_z(step))
         held = call(join, (2 * held.shape[0], 64, 128), bf16, (held, arrived), [], JOIN_COST)
     before, after, across = [spread(held, "rcv", along_y(offset)) for offset in (1, 3, 2)]
 
-    next_piece = spread(piece, "shot", along_x(1))
-    previous_piece = spread(piece, "shot", along_x(3))
-    far_piece = spread(next_piece, "shot", along_x(1))
-    others = swap(jnp.stack([piece, next_piece, previous_piece]))
-    pieces = (piece, next_piece, previous_piece, far_piece, others, swap(far_piece))
+    near = spread(both, "shot", along_x)
+    far = spread(near[0], "shot", along_x)
+    pieces = (both, near, swap(near), far, swap(far))
     padded = call(assemble, (8, 576, 128), bf16, pieces, [])
     work = 2 * 512 * 256 * 9 * 256
     total = call(first_kernel, (512, 256), f32, (held, padded), band, work)
-    total = call(middle_kernel, (512, 256), f32, (before, after, padded, total), band, 2 * work)
+    for offset, block in ((3, after), (1, before)):
+        body = functools.partial(middle_kernel, offset)
+        total = call(body, (512, 256), f32, (block, padded, total), band, work)
     return call(
         last_kernel,
         (32, 8, 512),

time: 37.1 us -> 36.1 us (0.973)
  starting transfers between devices: 23.2 us -> 22 us
  Pallas kernels: 5.44 us -> 5.99 us
    ppermute x11, starting transfers between devices: 23.2 us -> 22 us  [spread(): return lax.ppermute(value, axis, [(i, partner(i)) for i in range(size)])]
    pallas_call x9 -> x10, Pallas kernels: 5.44 us -> 5.99 us  [call(): pl.pallas_call(body, out_shape=jax.ShapeDtypeStruct(shape, dtype), in_spe...]
  transfers between devices with their start and end apart: 11 -> 11, of which waited for: 3 -> 3; matrix products, arithmetic and copies ran while one was open for 0% -> 0% of each run, Pallas kernels for 8% -> 11%
where the time goes in v5:
time: 36.1 us; the launch traced here: 35.9 us
  starting transfers between devices  22 us (61%)
  waiting for transfers between devices  6.17 us (17%)
  Pallas kernels  5.99 us (17%)
  local copies, waits for them, and re-layouts  1.67 us (5%)
    ppermute x11, starting transfers between devices, spread(): return lax.ppermute(value, axis, [(i, partner(i)) for i in range(size)])  22 us
    ppermute x11, waiting for transfers between devices, spread(): return lax.ppermute(value, axis, [(i, partner(i)) for i in range(size)])  6.17 us
    pallas_call x10, Pallas kernels, call(): pl.pallas_call(body, out_shape=jax.ShapeDtypeStruct(shape, dtype), in_spe...  5.99 us
    unnamed x4, local copies, waits for them, and re-layouts  1.66 us
  transfers between devices with their start and end apart: 11, of which 3 were waited for; matrix products, arithmetic and copies ran while one was open for 0% of the time, Pallas kernels for 11%

profile of v5, /device:TPU:1, one launch (start us, length us, event | category | flops | bytes accessed | tf_op | source)
XLA Modules:
  0.0 35.9 jit_solution(7062788813287270879)
XLA Ops:
  0.0 3.2 %collective-permute-start.4 = (bf16[16,8,512]{2,1,0:T(8,128)(2,1)}, bf16[16,8,512]{2,1,0:T(8,128)(2,1)S(1)}, u32[]{:S(2)}, u32[]{:S(2)}) collective-permute-start(bf16[16,8,512]{2,1,0:T(8,128)(2,1)} %own.1), channel_id=1, source_target_pairs={{0,32},{32,0},{64,96},{96,64},{128,160},{160,128},{192,224},{224,1... | collective-permute-start | bytes 393224 | tf_op jit(solution)/shard_map/ppermute | solution.py:18
  3.2 0.0 copy-start.1
  3.2 0.8 %copy-done.1 = bf16[32,4,64]{2,1,0:T(4,128)(2,1)S(1)} copy-done((bf16[32,4,64]{2,1,0:T(4,128)(2,1)S(1)}, bf16[32,4,64]{2,1,0:T(4,128)(2,1)}, u32[]{:S(2)}) %copy-start.1) | copy-done | bytes 16408
  4.0 0.2 shard_map.28
  4.2 0.1 collective-permute-start
  4.3 0.2 collective-permute-done.4.other
  4.4 0.9 %copy-done = bf16[16,8,512]{2,1,0:T(8,128)(2,1)S(1)} copy-done((bf16[16,8,512]{2,1,0:T(8,128)(2,1)S(1)}, bf16[16,8,512]{2,1,0:T(8,128)(2,1)}, u32[]{:S(2)}) %copy-start) | copy-done | bytes 131096
  5.3 0.7 %shard_map.32.own = bf16[2,512,128]{2,1,0:T(8,128)(2,1)S(1)} custom-call(bf16[16,8,512]{2,1,0:T(8,128)(2,1)S(1)} %copy-done, bf16[16,8,512]{2,1,0:T(8,128)(2,1)S(1)} %collective-permute-done.4.other, bf16[1,64,128]{2,1,0:T(8,128)(2,1)S(1)} %bitcast.5), custom_call_target="tpu_custom_call" | custom-call | bytes 1048576 | tf_op jit(solution)/shard_map/pallas_call | solution.py:161
  6.0 2.3 %collective-permute-start.5 = (bf16[2,512,128]{2,1,0:T(8,128)(2,1)S(1)}, bf16[2,512,128]{2,1,0:T(8,128)(2,1)S(1)}, u32[]{:S(2)}, u32[]{:S(2)}) collective-permute-start(bf16[2,512,128]{2,1,0:T(8,128)(2,1)S(1)} %shard_map.32.own), channel_id=1, source_target_pairs={{0,64},{32,224},{64,128},{96,32},{128,192},{160,96},{192,0},{224,1... | collective-permute-start | bytes 786440 | tf_op jit(solution)/shard_map/ppermute | solution.py:18
  8.3 0.0 collective-permute-done.second
  8.3 5.1 %collective-permute-start.1 = (bf16[2,64,128]{2,1,0:T(8,128)(2,1)S(1)}, bf16[2,64,128]{2,1,0:T(8,128)(2,1)S(1)}, u32[]{:S(2)}, u32[]{:S(2)}) collective-permute-start(bf16[2,64,128]{2,1,0:T(8,128)(2,1)S(1)} %shard_map.29.first), channel_id=1, source_target_pairs={{0,6},{1,3},{2,0},{3,5},{4,2},{5,7},{6,4},{7,1},{8,14},{9,11},{10,... | collective-permute-start | bytes 98312 | tf_op jit(solution)/shard_map/ppermute | solution.py:18
  13.4 0.0 collective-permute-done.5.near
  13.5 1.4 %collective-permute-start.7 = (bf16[512,128]{1,0:T(8,128)(2,1)S(1)}, bf16[512,128]{1,0:T(8,128)(2,1)S(1)}, u32[]{:S(2)}, u32[]{:S(2)}) collective-permute-start(bf16[512,128]{1,0:T(8,128)(2,1)S(1)} %slice_bitcast_fusion), channel_id=1, source_target_pairs={{0,64},{32,224},{64,128},{96,32},{128,192},{160,96},{192,0},{224,1... | collective-permute-start | bytes 393224 | tf_op jit(solution)/shard_map/ppermute | solution.py:18
  14.8 0.0 collective-permute-done.1.second
  14.8 4.8 %collective-permute-start.2 = (bf16[4,64,128]{2,1,0:T(8,128)(2,1)S(1)}, bf16[4,64,128]{2,1,0:T(8,128)(2,1)S(1)}, u32[]{:S(2)}, u32[]{:S(2)}) collective-permute-start(bf16[4,64,128]{2,1,0:T(8,128)(2,1)S(1)} %shard_map.30.first), channel_id=1, source_target_pairs={{0,7},{1,2},{2,1},{3,4},{4,3},{5,6},{6,5},{7,0},{8,15},{9,10},{10,... | collective-permute-start | bytes 196616 | tf_op jit(solution)/shard_map/ppermute | solution.py:18
  19.6 0.0 collective-permute-start.6
  19.6 0.0 collective-permute-done.7.far
  19.6 0.7 %collective-permute-start.8 = (bf16[512,128]{1,0:T(8,128)(2,1)S(1)}, bf16[512,128]{1,0:T(8,128)(2,1)S(1)}, u32[]{:S(2)}, u32[]{:S(2)}) collective-permute-start(bf16[512,128]{1,0:T(8,128)(2,1)S(1)} %collective-permute-done.7.far), channel_id=1, source_target_pairs={{0,32},{32,0},{64,96},{96,64},{128,160},{160,128},{192,224},{224,1... | collective-permute-start | bytes 393224 | tf_op jit(solution)/shard_map/ppermute | solution.py:18
  20.3 1.1 %collective-permute-done.2.second = bf16[4,64,128]{2,1,0:T(8,128)(2,1)S(1)} collective-permute-done((bf16[4,64,128]{2,1,0:T(8,128)(2,1)S(1)}, bf16[4,64,128]{2,1,0:T(8,128)(2,1)S(1)}, u32[]{:S(2)}, u32[]{:S(2)}) %collective-permute-start.2) | collective-permute-done | bytes 65568 | tf_op jit(solution)/shard_map/ppermute | solution.py:18
  21.4 2.8 %collective-permute-start.10 = (bf16[8,64,128]{2,1,0:T(8,128)(2,1)S(1)}, bf16[8,64,128]{2,1,0:T(8,128)(2,1)S(1)}, u32[]{:S(2)}, u32[]{:S(2)}) collective-permute-start(bf16[8,64,128]{2,1,0:T(8,128)(2,1)S(1)} %shard_map.31.own), channel_id=1, source_target_pairs={{0,24},{1,25},{2,26},{3,27},{4,28},{5,29},{6,30},{7,31},{8,0},{9,1... | collective-permute-start | bytes 393224 | tf_op jit(solution)/shard_map/ppermute | solution.py:18
  24.2 0.0 collective-permute-start.9
  24.2 1.6 %collective-permute-start.3 = (bf16[8,64,128]{2,1,0:T(8,128)(2,1)S(1)}, bf16[8,64,128]{2,1,0:T(8,128)(2,1)S(1)}, u32[]{:S(2)}, u32[]{:S(2)}) collective-permute-start(bf16[8,64,128]{2,1,0:T(8,128)(2,1)S(1)} %shard_map.31.own), channel_id=1, source_target_pairs={{0,16},{1,17},{2,18},{3,19},{4,20},{5,21},{6,22},{7,23},{8,24},{9,... | collective-permute-start | bytes 393224 | tf_op jit(solution)/shard_map/ppermute | solution.py:18
  25.8 0.0 collective-permute-done.8.far_swapped
  25.8 0.0 collective-permute-done.6.near_swapped
  25.9 0.1 shard_map.33.padded
  26.0 1.0 %shard_map.34.so_far = f32[512,256]{1,0:T(8,128)S(1)} custom-call(bf16[8,64,128]{2,1,0:T(8,128)(2,1)S(1)} %shard_map.31.own, bf16[8,576,128]{2,1,0:T(8,128)(2,1)S(1)} %shard_map.33.padded), custom_call_target="tpu_custom_call" | custom-call | flops 603979776 | bytes 1048576 | tf_op jit(solution)/shard_map/pallas_call | solution.py:161
  26.9 0.0 collective-permute-done.10.response
  27.0 1.0 %shard_map.35.so_far = f32[512,256]{1,0:T(8,128)S(1)} custom-call(bf16[8,64,128]{2,1,0:T(8,128)(2,1)S(1)} %collective-permute-done.10.response, bf16[8,576,128]{2,1,0:T(8,128)(2,1)S(1)} %shard_map.33.padded, f32[512,256]{1,0:T(8,128)S(1)} %shard_map.34.so_far), custom_call_target="tpu_custom_call" | custom-call | flops 603979776 | bytes 1048576 | tf_op jit(solution)/shard_map/pallas_call | solution.py:161
  27.9 4.9 %collective-permute-done.9.response = bf16[8,64,128]{2,1,0:T(8,128)(2,1)S(1)} collective-permute-done((bf16[8,64,128]{2,1,0:T(8,128)(2,1)S(1)}, bf16[8,64,128]{2,1,0:T(8,128)(2,1)S(1)}, u32[]{:S(2)}, u32[]{:S(2)}) %collective-permute-start.9) | collective-permute-done | bytes 131104 | tf_op jit(solution)/shard_map/ppermute | solution.py:18
  32.9 0.9 %shard_map.36.so_far = f32[512,256]{1,0:T(8,128)S(1)} custom-call(bf16[8,64,128]{2,1,0:T(8,128)(2,1)S(1)} %collective-permute-done.9.response, bf16[8,576,128]{2,1,0:T(8,128)(2,1)S(1)} %shard_map.33.padded, f32[512,256]{1,0:T(8,128)S(1)} %shard_map.35.so_far), custom_call_target="tpu_custom_call" | custom-call | flops 603979776 | bytes 1048576 | tf_op jit(solution)/shard_map/pallas_call | solution.py:161
  33.8 0.0 collective-permute-done.3.across
  33.8 2.1 %shard_map.37 = bf16[32,8,512]{2,1,0:T(8,128)(2,1)} custom-call(bf16[8,64,128]{2,1,0:T(8,128)(2,1)S(1)} %collective-permute-done.3.across, bf16[8,576,128]{2,1,0:T(8,128)(2,1)S(1)} %shard_map.33.padded, f32[512,256]{1,0:T(8,128)S(1)} %shard_map.36.so_far), custom_call_target="tpu_custom_call" | custom-call | flops 603979776 | bytes 1048576 | tf_op jit(solution)/shard_map/pallas_call | solution.py:161
  (5 shorter events, 0.0 us)
Async XLA Ops:
  0.0 4.4 %collective-permute-start.4 = (bf16[16,8,512]{2,1,0:T(8,128)(2,1)}, bf16[16,8,512]{2,1,0:T(8,128)(2,1)S(1)}, u32[]{:S(2)}, u32[]{:S(2)}) collective-permute-start(bf16[16,8,512]{2,1,0:T(8,128)(2,1)} %own.1), channel_id=1, source_target_pairs={{0,32},{32,0},{64,96},{96,64},{128,160},{160,128},{192,224},{224,1... | collective-permute-start | bytes 393224 | tf_op jit(solution)/shard_map/ppermute | solution.py:18
  3.2 0.8 %copy-start.1 = (bf16[32,4,64]{2,1,0:T(4,128)(2,1)S(1)}, bf16[32,4,64]{2,1,0:T(4,128)(2,1)}, u32[]{:S(2)}) copy-start(bf16[32,4,64]{2,1,0:T(4,128)(2,1)} %param.2) | copy-start | bytes 49156
  4.2 4.1 %collective-permute-start = (bf16[1,64,128]{2,1,0:T(8,128)(2,1)S(1)}, bf16[1,64,128]{2,1,0:T(8,128)(2,1)S(1)}, u32[]{:S(2)}, u32[]{:S(2)}) collective-permute-start(bf16[1,64,128]{2,1,0:T(8,128)(2,1)S(1)} %bitcast.4), channel_id=1, source_target_pairs={{0,1},{1,0},{2,3},{3,2},{4,5},{5,4},{6,7},{7,6},{8,9},{9,8},{10,11... | collective-permute-start | bytes 49160 | tf_op jit(solution)/shard_map/ppermute | solution.py:18
  4.4 0.9 %copy-start = (bf16[16,8,512]{2,1,0:T(8,128)(2,1)S(1)}, bf16[16,8,512]{2,1,0:T(8,128)(2,1)}, u32[]{:S(2)}) copy-start(bf16[16,8,512]{2,1,0:T(8,128)(2,1)} %own.1) | copy-start | bytes 393220
  6.0 7.4 %collective-permute-start.5 = (bf16[2,512,128]{2,1,0:T(8,128)(2,1)S(1)}, bf16[2,512,128]{2,1,0:T(8,128)(2,1)S(1)}, u32[]{:S(2)}, u32[]{:S(2)}) collective-permute-start(bf16[2,512,128]{2,1,0:T(8,128)(2,1)S(1)} %shard_map.32.own), channel_id=1, source_target_pairs={{0,64},{32,224},{64,128},{96,32},{128,192},{160,96},{192,0},{224,1... | collective-permute-start | bytes 786440 | tf_op jit(solution)/shard_map/ppermute | solution.py:18
  8.3 6.5 %collective-permute-start.1 = (bf16[2,64,128]{2,1,0:T(8,128)(2,1)S(1)}, bf16[2,64,128]{2,1,0:T(8,128)(2,1)S(1)}, u32[]{:S(2)}, u32[]{:S(2)}) collective-permute-start(bf16[2,64,128]{2,1,0:T(8,128)(2,1)S(1)} %shard_map.29.first), channel_id=1, source_target_pairs={{0,6},{1,3},{2,0},{3,5},{4,2},{5,7},{6,4},{7,1},{8,14},{9,11},{10,... | collective-permute-start | bytes 98312 | tf_op jit(solution)/shard_map/ppermute | solution.py:18
  13.5 6.1 %collective-permute-start.7 = (bf16[512,128]{1,0:T(8,128)(2,1)S(1)}, bf16[512,128]{1,0:T(8,128)(2,1)S(1)}, u32[]{:S(2)}, u32[]{:S(2)}) collective-permute-start(bf16[512,128]{1,0:T(8,128)(2,1)S(1)} %slice_bitcast_fusion), channel_id=1, source_target_pairs={{0,64},{32,224},{64,128},{96,32},{128,192},{160,96},{192,0},{224,1... | collective-permute-start | bytes 393224 | tf_op jit(solution)/shard_map/ppermute | solution.py:18
  14.8 6.5 %collective-permute-start.2 = (bf16[4,64,128]{2,1,0:T(8,128)(2,1)S(1)}, bf16[4,64,128]{2,1,0:T(8,128)(2,1)S(1)}, u32[]{:S(2)}, u32[]{:S(2)}) collective-permute-start(bf16[4,64,128]{2,1,0:T(8,128)(2,1)S(1)} %shard_map.30.first), channel_id=1, source_target_pairs={{0,7},{1,2},{2,1},{3,4},{4,3},{5,6},{6,5},{7,0},{8,15},{9,10},{10,... | collective-permute-start | bytes 196616 | tf_op jit(solution)/shard_map/ppermute | solution.py:18
  19.6 6.2 %collective-permute-start.6 = (bf16[2,512,128]{2,1,0:T(8,128)(2,1)S(1)}, bf16[2,512,128]{2,1,0:T(8,128)(2,1)S(1)}, u32[]{:S(2)}, u32[]{:S(2)}) collective-permute-start(bf16[2,512,128]{2,1,0:T(8,128)(2,1)S(1)} %collective-permute-done.5.near), channel_id=1, source_target_pairs={{0,32},{32,0},{64,96},{96,64},{128,160},{160,128},{192,224},{224,1... | collective-permute-start | bytes 786440 | tf_op jit(solution)/shard_map/ppermute | solution.py:18
  19.6 6.2 %collective-permute-start.8 = (bf16[512,128]{1,0:T(8,128)(2,1)S(1)}, bf16[512,128]{1,0:T(8,128)(2,1)S(1)}, u32[]{:S(2)}, u32[]{:S(2)}) collective-permute-start(bf16[512,128]{1,0:T(8,128)(2,1)S(1)} %collective-permute-done.7.far), channel_id=1, source_target_pairs={{0,32},{32,0},{64,96},{96,64},{128,160},{160,128},{192,224},{224,1... | collective-permute-start | bytes 393224 | tf_op jit(solution)/shard_map/ppermute | solution.py:18
  21.4 5.6 %collective-permute-start.10 = (bf16[8,64,128]{2,1,0:T(8,128)(2,1)S(1)}, bf16[8,64,128]{2,1,0:T(8,128)(2,1)S(1)}, u32[]{:S(2)}, u32[]{:S(2)}) collective-permute-start(bf16[8,64,128]{2,1,0:T(8,128)(2,1)S(1)} %shard_map.31.own), channel_id=1, source_target_pairs={{0,24},{1,25},{2,26},{3,27},{4,28},{5,29},{6,30},{7,31},{8,0},{9,1... | collective-permute-start | bytes 393224 | tf_op jit(solution)/shard_map/ppermute | solution.py:18
  24.2 8.7 %collective-permute-start.9 = (bf16[8,64,128]{2,1,0:T(8,128)(2,1)S(1)}, bf16[8,64,128]{2,1,0:T(8,128)(2,1)S(1)}, u32[]{:S(2)}, u32[]{:S(2)}) collective-permute-start(bf16[8,64,128]{2,1,0:T(8,128)(2,1)S(1)} %shard_map.31.own), channel_id=1, source_target_pairs={{0,8},{1,9},{2,10},{3,11},{4,12},{5,13},{6,14},{7,15},{8,16},{9,17... | collective-permute-start | bytes 393224 | tf_op jit(solution)/shard_map/ppermute | solution.py:18
  24.2 9.6 %collective-permute-start.3 = (bf16[8,64,128]{2,1,0:T(8,128)(2,1)S(1)}, bf16[8,64,128]{2,1,0:T(8,128)(2,1)S(1)}, u32[]{:S(2)}, u32[]{:S(2)}) collective-permute-start(bf16[8,64,128]{2,1,0:T(8,128)(2,1)S(1)} %shard_map.31.own), channel_id=1, source_target_pairs={{0,16},{1,17},{2,18},{3,19},{4,20},{5,21},{6,22},{7,23},{8,24},{9,... | collective-permute-start | bytes 393224 | tf_op jit(solution)/shard_map/ppermute | solution.py:18

commit v6 on v5

--- a/solution.py
+++ b/solution.py
@@ -7,7 +7,7 @@
 from jax.experimental.pallas import tpu as pltpu
 from jax.sharding import PartitionSpec as P
 
-RING8 = (0, 1, 2, 3, 7, 6, 5, 4)
+RING8 = (0, 1, 5, 4, 2, 3, 7, 6)
 VMEM = pl.BlockSpec(memory_space=pltpu.VMEM)
 JOIN_COST = 2**33
 PARAMS = pltpu.CompilerParams(vmem_limit_bytes=40 * 2**20)
@@ -74,10 +74,11 @@
         out[place, 64:, :] = block[...]
 
 
-def join(first, second, out):
-    count = first.shape[0]
-    out[:count] = first[...]
-    out[count:] = second[...]
+def join(*blocks):
+    out = blocks[-1]
+    count = blocks[0].shape[0]
+    for place, block in enumerate(blocks[:-1]):
+        out[place * count : place * count + count] = block[...]
 
 
 def position_of(offset):
@@ -182,6 +183,9 @@
     def along_x(i):
         return ((i // 2 + sign(i)) % 4) * 2 + i % 2
 
+    def across_x(i):
+        return (i + 4) % 8
+
     def swap(value):
         return spread(value, "shot", lambda i: i ^ 1)
 
@@ -200,13 +204,15 @@
         (traces, swap(traces), held),
         [((2, 4, 128, 128), f32), ((2, 512, 128), f32)],
     )
-    for step in (lambda z: z + sign(z), lambda z: z - 2 * sign(z), lambda z: z - sign(z)):
-        arrived = spread(held, "rcv", along_z(step))
-        held = call(join, (2 * held.shape[0], 64, 128), bf16, (held, arrived), [], JOIN_COST)
+    held = call(join, (2, 64, 128), bf16, (held, spread(held, "rcv", along_z(lambda z: z + sign(z)))), [], JOIN_COST)
+    arrived = [
+        spread(held, "rcv", along_z(lambda z, hops=hops: z - hops * sign(z))) for hops in (3, 2, 1)
+    ]
+    held = call(join, (8, 64, 128), bf16, (held, *arrived), [], JOIN_COST)
     before, after, across = [spread(held, "rcv", along_y(offset)) for offset in (1, 3, 2)]
 
     near = spread(both, "shot", along_x)
-    far = spread(near[0], "shot", along_x)
+    far = spread(both[0], "shot", across_x)
     pieces = (both, near, swap(near), far, swap(far))
     padded = call(assemble, (8, 576, 128), bf16, pieces, [])
     work = 2 * 512 * 256 * 9 * 256

time: 36.1 us -> 34.1 us (0.945)
  the two profiles are of different devices: /device:TPU:1 before, /device:TPU:4 now
where the time goes in v6:
time: 34.1 us; the launch traced here: 34 us
  starting transfers between devices  19.5 us (57%)
  waiting for transfers between devices  6.77 us (20%)
  Pallas kernels  5.99 us (18%)
  local copies, waits for them, and re-layouts  1.67 us (5%)
    ppermute x12, starting transfers between devices, spread(): return lax.ppermute(value, axis, [(i, partner(i)) for i in range(size)])  19.5 us
    ppermute x12, waiting for transfers between devices, spread(): return lax.ppermute(value, axis, [(i, partner(i)) for i in range(size)])  6.77 us
    pallas_call x9, Pallas kernels, call(): pl.pallas_call(body, out_shape=jax.ShapeDtypeStruct(shape, dtype), in_spe...  5.99 us
    unnamed x4, local copies, waits for them, and re-layouts  1.66 us
  transfers between devices with their start and end apart: 12, of which 3 were waited for; matrix products, arithmetic and copies ran while one was open for 0% of the time, Pallas kernels for 11%

profile of v6, /device:TPU:4, one launch (start us, length us, event | category | flops | bytes accessed | tf_op | source)
XLA Modules:
  0.0 34.0 jit_solution(11368985220624068058)
XLA Ops:
  0.0 0.0 collective-permute-start.5
  0.0 0.8 %copy-done.1 = bf16[32,4,64]{2,1,0:T(4,128)(2,1)S(1)} copy-done((bf16[32,4,64]{2,1,0:T(4,128)(2,1)S(1)}, bf16[32,4,64]{2,1,0:T(4,128)(2,1)}, u32[]{:S(2)}) %copy-start.1) | copy-done | bytes 16408
  0.8 0.2 shard_map.28
  1.0 2.0 %collective-permute-start = (bf16[1,64,128]{2,1,0:T(8,128)(2,1)S(1)}, bf16[1,64,128]{2,1,0:T(8,128)(2,1)S(1)}, u32[]{:S(2)}, u32[]{:S(2)}) collective-permute-start(bf16[1,64,128]{2,1,0:T(8,128)(2,1)S(1)} %bitcast.4), channel_id=1, source_target_pairs={{0,1},{1,0},{2,3},{3,2},{4,5},{5,4},{6,7},{7,6},{8,9},{9,8},{10,11... | collective-permute-start | bytes 49160 | tf_op jit(solution)/shard_map/ppermute | solution.py:18
  3.0 0.0 collective-permute-done.5.other
  3.0 0.9 %copy-done = bf16[16,8,512]{2,1,0:T(8,128)(2,1)S(1)} copy-done((bf16[16,8,512]{2,1,0:T(8,128)(2,1)S(1)}, bf16[16,8,512]{2,1,0:T(8,128)(2,1)}, u32[]{:S(2)}) %copy-start) | copy-done | bytes 131096
  3.9 0.7 %shard_map.31.own = bf16[2,512,128]{2,1,0:T(8,128)(2,1)S(1)} custom-call(bf16[16,8,512]{2,1,0:T(8,128)(2,1)S(1)} %copy-done, bf16[16,8,512]{2,1,0:T(8,128)(2,1)S(1)} %collective-permute-done.5.other, bf16[1,64,128]{2,1,0:T(8,128)(2,1)S(1)} %bitcast.5), custom_call_target="tpu_custom_call" | custom-call | bytes 1048576 | tf_op jit(solution)/shard_map/pallas_call | solution.py:162
  4.5 1.3 %collective-permute-start.6 = (bf16[2,512,128]{2,1,0:T(8,128)(2,1)S(1)}, bf16[2,512,128]{2,1,0:T(8,128)(2,1)S(1)}, u32[]{:S(2)}, u32[]{:S(2)}) collective-permute-start(bf16[2,512,128]{2,1,0:T(8,128)(2,1)S(1)} %shard_map.31.own), channel_id=1, source_target_pairs={{0,64},{32,224},{64,128},{96,32},{128,192},{160,96},{192,0},{224,1... | collective-permute-start | bytes 786440 | tf_op jit(solution)/shard_map/ppermute | solution.py:18
  5.8 0.9 %collective-permute-start.8 = (bf16[512,128]{1,0:T(8,128)(2,1)S(1)}, bf16[512,128]{1,0:T(8,128)(2,1)S(1)}, u32[]{:S(2)}, u32[]{:S(2)}) collective-permute-start(bf16[512,128]{1,0:T(8,128)(2,1)S(1)} %slice_bitcast_fusion), channel_id=1, source_target_pairs={{0,128},{32,160},{64,192},{96,224},{128,0},{160,32},{192,64},{224,... | collective-permute-start | bytes 393224 | tf_op jit(solution)/shard_map/ppermute | solution.py:18
  6.7 0.0 collective-permute-done.blocks_1_
  6.7 5.8 %collective-permute-start.1 = (bf16[2,64,128]{2,1,0:T(8,128)(2,1)S(1)}, bf16[2,64,128]{2,1,0:T(8,128)(2,1)S(1)}, u32[]{:S(2)}, u32[]{:S(2)}) collective-permute-start(bf16[2,64,128]{2,1,0:T(8,128)(2,1)S(1)} %shard_map.29.blocks_0_), channel_id=1, source_target_pairs={{0,5},{1,4},{2,7},{3,6},{4,1},{5,0},{6,3},{7,2},{8,13},{9,12},{10,... | collective-permute-start | bytes 98312 | tf_op jit(solution)/shard_map/ppermute | solution.py:18
  12.6 0.1 collective-permute-start.2
  12.6 3.6 %collective-permute-start.3 = (bf16[2,64,128]{2,1,0:T(8,128)(2,1)S(1)}, bf16[2,64,128]{2,1,0:T(8,128)(2,1)S(1)}, u32[]{:S(2)}, u32[]{:S(2)}) collective-permute-start(bf16[2,64,128]{2,1,0:T(8,128)(2,1)S(1)} %shard_map.29.blocks_0_), channel_id=1, source_target_pairs={{0,7},{1,2},{2,1},{3,4},{4,3},{5,6},{6,5},{7,0},{8,15},{9,10},{10,... | collective-permute-start | bytes 98312 | tf_op jit(solution)/shard_map/ppermute | solution.py:18
  16.3 0.0 collective-permute-done.8.far
  16.3 0.1 collective-permute-start.9
  16.3 0.0 collective-permute-done.6.near
  16.3 0.4 %collective-permute-start.7 = (bf16[2,512,128]{2,1,0:T(8,128)(2,1)S(1)}, bf16[2,512,128]{2,1,0:T(8,128)(2,1)S(1)}, u32[]{:S(2)}, u32[]{:S(2)}) collective-permute-start(bf16[2,512,128]{2,1,0:T(8,128)(2,1)S(1)} %collective-permute-done.6.near), channel_id=1, source_target_pairs={{0,32},{32,0},{64,96},{96,64},{128,160},{160,128},{192,224},{224,1... | collective-permute-start | bytes 786440 | tf_op jit(solution)/shard_map/ppermute | solution.py:18
  16.8 0.0 collective-permute-done.1.blocks_1_
  16.8 0.6 %collective-permute-done.2.blocks_2_ = bf16[2,64,128]{2,1,0:T(8,128)(2,1)S(1)} collective-permute-done((bf16[2,64,128]{2,1,0:T(8,128)(2,1)S(1)}, bf16[2,64,128]{2,1,0:T(8,128)(2,1)S(1)}, u32[]{:S(2)}, u32[]{:S(2)}) %collective-permute-start.2) | collective-permute-done | bytes 32800 | tf_op jit(solution)/shard_map/ppermute | solution.py:18
  17.4 1.5 %collective-permute-done.3.blocks_3_ = bf16[2,64,128]{2,1,0:T(8,128)(2,1)S(1)} collective-permute-done((bf16[2,64,128]{2,1,0:T(8,128)(2,1)S(1)}, bf16[2,64,128]{2,1,0:T(8,128)(2,1)S(1)}, u32[]{:S(2)}, u32[]{:S(2)}) %collective-permute-start.3) | collective-permute-done | bytes 32800 | tf_op jit(solution)/shard_map/ppermute | solution.py:18
  18.9 3.1 %collective-permute-start.11 = (bf16[8,64,128]{2,1,0:T(8,128)(2,1)S(1)}, bf16[8,64,128]{2,1,0:T(8,128)(2,1)S(1)}, u32[]{:S(2)}, u32[]{:S(2)}) collective-permute-start(bf16[8,64,128]{2,1,0:T(8,128)(2,1)S(1)} %shard_map.30.own), channel_id=1, source_target_pairs={{0,24},{1,25},{2,26},{3,27},{4,28},{5,29},{6,30},{7,31},{8,0},{9,1... | collective-permute-start | bytes 393224 | tf_op jit(solution)/shard_map/ppermute | solution.py:18
  22.0 0.0 collective-permute-start.10
  22.0 2.2 %collective-permute-start.4 = (bf16[8,64,128]{2,1,0:T(8,128)(2,1)S(1)}, bf16[8,64,128]{2,1,0:T(8,128)(2,1)S(1)}, u32[]{:S(2)}, u32[]{:S(2)}) collective-permute-start(bf16[8,64,128]{2,1,0:T(8,128)(2,1)S(1)} %shard_map.30.own), channel_id=1, source_target_pairs={{0,16},{1,17},{2,18},{3,19},{4,20},{5,21},{6,22},{7,23},{8,24},{9,... | collective-permute-start | bytes 393224 | tf_op jit(solution)/shard_map/ppermute | solution.py:18
  24.2 0.0 collective-permute-done.9.far_swapped
  24.2 0.0 collective-permute-done.7.near_swapped
  24.2 0.1 shard_map.32.padded
  24.3 1.0 %shard_map.33.so_far = f32[512,256]{1,0:T(8,128)S(1)} custom-call(bf16[8,64,128]{2,1,0:T(8,128)(2,1)S(1)} %shard_map.30.own, bf16[8,576,128]{2,1,0:T(8,128)(2,1)S(1)} %shard_map.32.padded), custom_call_target="tpu_custom_call" | custom-call | flops 603979776 | bytes 1048576 | tf_op jit(solution)/shard_map/pallas_call | solution.py:162
  25.3 1.0 %shard_map.34.so_far = f32[512,256]{1,0:T(8,128)S(1)} custom-call(bf16[8,64,128]{2,1,0:T(8,128)(2,1)S(1)} %collective-permute-done.11.response, bf16[8,576,128]{2,1,0:T(8,128)(2,1)S(1)} %shard_map.32.padded, f32[512,256]{1,0:T(8,128)S(1)} %shard_map.33.so_far), custom_call_target="tpu_custom_call" | custom-call | flops 603979776 | bytes 1048576 | tf_op jit(solution)/shard_map/pallas_call | solution.py:162
  26.3 4.7 %collective-permute-done.10.response = bf16[8,64,128]{2,1,0:T(8,128)(2,1)S(1)} collective-permute-done((bf16[8,64,128]{2,1,0:T(8,128)(2,1)S(1)}, bf16[8,64,128]{2,1,0:T(8,128)(2,1)S(1)}, u32[]{:S(2)}, u32[]{:S(2)}) %collective-permute-start.10) | collective-permute-done | bytes 131104 | tf_op jit(solution)/shard_map/ppermute | solution.py:18
  30.9 0.9 %shard_map.35.so_far = f32[512,256]{1,0:T(8,128)S(1)} custom-call(bf16[8,64,128]{2,1,0:T(8,128)(2,1)S(1)} %collective-permute-done.10.response, bf16[8,576,128]{2,1,0:T(8,128)(2,1)S(1)} %shard_map.32.padded, f32[512,256]{1,0:T(8,128)S(1)} %shard_map.34.so_far), custom_call_target="tpu_custom_call" | custom-call | flops 603979776 | bytes 1048576 | tf_op jit(solution)/shard_map/pallas_call | solution.py:162
  31.9 0.0 collective-permute-done.4.across
  31.9 2.1 %shard_map.36 = bf16[32,8,512]{2,1,0:T(8,128)(2,1)} custom-call(bf16[8,64,128]{2,1,0:T(8,128)(2,1)S(1)} %collective-permute-done.4.across, bf16[8,576,128]{2,1,0:T(8,128)(2,1)S(1)} %shard_map.32.padded, f32[512,256]{1,0:T(8,128)S(1)} %shard_map.35.so_far), custom_call_target="tpu_custom_call" | custom-call | flops 603979776 | bytes 1048576 | tf_op jit(solution)/shard_map/pallas_call | solution.py:162
  (6 shorter events, 0.0 us)
Async XLA Ops:
  0.0 3.0 %collective-permute-start.5 = (bf16[16,8,512]{2,1,0:T(8,128)(2,1)}, bf16[16,8,512]{2,1,0:T(8,128)(2,1)S(1)}, u32[]{:S(2)}, u32[]{:S(2)}) collective-permute-start(bf16[16,8,512]{2,1,0:T(8,128)(2,1)} %own.1), channel_id=1, source_target_pairs={{0,32},{32,0},{64,96},{96,64},{128,160},{160,128},{192,224},{224,1... | collective-permute-start | bytes 393224 | tf_op jit(solution)/shard_map/ppermute | solution.py:18
  0.0 0.8 %copy-start.1 = (bf16[32,4,64]{2,1,0:T(4,128)(2,1)S(1)}, bf16[32,4,64]{2,1,0:T(4,128)(2,1)}, u32[]{:S(2)}) copy-start(bf16[32,4,64]{2,1,0:T(4,128)(2,1)} %param.2) | copy-start | bytes 49156
  1.0 5.7 %collective-permute-start = (bf16[1,64,128]{2,1,0:T(8,128)(2,1)S(1)}, bf16[1,64,128]{2,1,0:T(8,128)(2,1)S(1)}, u32[]{:S(2)}, u32[]{:S(2)}) collective-permute-start(bf16[1,64,128]{2,1,0:T(8,128)(2,1)S(1)} %bitcast.4), channel_id=1, source_target_pairs={{0,1},{1,0},{2,3},{3,2},{4,5},{5,4},{6,7},{7,6},{8,9},{9,8},{10,11... | collective-permute-start | bytes 49160 | tf_op jit(solution)/shard_map/ppermute | solution.py:18
  3.0 0.9 %copy-start = (bf16[16,8,512]{2,1,0:T(8,128)(2,1)S(1)}, bf16[16,8,512]{2,1,0:T(8,128)(2,1)}, u32[]{:S(2)}) copy-start(bf16[16,8,512]{2,1,0:T(8,128)(2,1)} %own.1) | copy-start | bytes 393220
  4.5 11.8 %collective-permute-start.6 = (bf16[2,512,128]{2,1,0:T(8,128)(2,1)S(1)}, bf16[2,512,128]{2,1,0:T(8,128)(2,1)S(1)}, u32[]{:S(2)}, u32[]{:S(2)}) collective-permute-start(bf16[2,512,128]{2,1,0:T(8,128)(2,1)S(1)} %shard_map.31.own), channel_id=1, source_target_pairs={{0,64},{32,224},{64,128},{96,32},{128,192},{160,96},{192,0},{224,1... | collective-permute-start | bytes 786440 | tf_op jit(solution)/shard_map/ppermute | solution.py:18
  5.8 10.4 %collective-permute-start.8 = (bf16[512,128]{1,0:T(8,128)(2,1)S(1)}, bf16[512,128]{1,0:T(8,128)(2,1)S(1)}, u32[]{:S(2)}, u32[]{:S(2)}) collective-permute-start(bf16[512,128]{1,0:T(8,128)(2,1)S(1)} %slice_bitcast_fusion), channel_id=1, source_target_pairs={{0,128},{32,160},{64,192},{96,224},{128,0},{160,32},{192,64},{224,... | collective-permute-start | bytes 393224 | tf_op jit(solution)/shard_map/ppermute | solution.py:18
  6.7 10.1 %collective-permute-start.1 = (bf16[2,64,128]{2,1,0:T(8,128)(2,1)S(1)}, bf16[2,64,128]{2,1,0:T(8,128)(2,1)S(1)}, u32[]{:S(2)}, u32[]{:S(2)}) collective-permute-start(bf16[2,64,128]{2,1,0:T(8,128)(2,1)S(1)} %shard_map.29.blocks_0_), channel_id=1, source_target_pairs={{0,5},{1,4},{2,7},{3,6},{4,1},{5,0},{6,3},{7,2},{8,13},{9,12},{10,... | collective-permute-start | bytes 98312 | tf_op jit(solution)/shard_map/ppermute | solution.py:18
  12.6 4.8 %collective-permute-start.2 = (bf16[2,64,128]{2,1,0:T(8,128)(2,1)S(1)}, bf16[2,64,128]{2,1,0:T(8,128)(2,1)S(1)}, u32[]{:S(2)}, u32[]{:S(2)}) collective-permute-start(bf16[2,64,128]{2,1,0:T(8,128)(2,1)S(1)} %shard_map.29.blocks_0_), channel_id=1, source_target_pairs={{0,6},{1,3},{2,0},{3,5},{4,2},{5,7},{6,4},{7,1},{8,14},{9,11},{10,... | collective-permute-start | bytes 98312 | tf_op jit(solution)/shard_map/ppermute | solution.py:18
  12.6 6.3 %collective-permute-start.3 = (bf16[2,64,128]{2,1,0:T(8,128)(2,1)S(1)}, bf16[2,64,128]{2,1,0:T(8,128)(2,1)S(1)}, u32[]{:S(2)}, u32[]{:S(2)}) collective-permute-start(bf16[2,64,128]{2,1,0:T(8,128)(2,1)S(1)} %shard_map.29.blocks_0_), channel_id=1, source_target_pairs={{0,7},{1,2},{2,1},{3,4},{4,3},{5,6},{6,5},{7,0},{8,15},{9,10},{10,... | collective-permute-start | bytes 98312 | tf_op jit(solution)/shard_map/ppermute | solution.py:18
  16.3 7.9 %collective-permute-start.9 = (bf16[512,128]{1,0:T(8,128)(2,1)S(1)}, bf16[512,128]{1,0:T(8,128)(2,1)S(1)}, u32[]{:S(2)}, u32[]{:S(2)}) collective-permute-start(bf16[512,128]{1,0:T(8,128)(2,1)S(1)} %collective-permute-done.8.far), channel_id=1, source_target_pairs={{0,32},{32,0},{64,96},{96,64},{128,160},{160,128},{192,224},{224,1... | collective-permute-start | bytes 393224 | tf_op jit(solution)/shard_map/ppermute | solution.py:18
  16.3 7.8 %collective-permute-start.7 = (bf16[2,512,128]{2,1,0:T(8,128)(2,1)S(1)}, bf16[2,512,128]{2,1,0:T(8,128)(2,1)S(1)}, u32[]{:S(2)}, u32[]{:S(2)}) collective-permute-start(bf16[2,512,128]{2,1,0:T(8,128)(2,1)S(1)} %collective-permute-done.6.near), channel_id=1, source_target_pairs={{0,32},{32,0},{64,96},{96,64},{128,160},{160,128},{192,224},{224,1... | collective-permute-start | bytes 786440 | tf_op jit(solution)/shard_map/ppermute | solution.py:18
  18.9 6.4 %collective-permute-start.11 = (bf16[8,64,128]{2,1,0:T(8,128)(2,1)S(1)}, bf16[8,64,128]{2,1,0:T(8,128)(2,1)S(1)}, u32[]{:S(2)}, u32[]{:S(2)}) collective-permute-start(bf16[8,64,128]{2,1,0:T(8,128)(2,1)S(1)} %shard_map.30.own), channel_id=1, source_target_pairs={{0,24},{1,25},{2,26},{3,27},{4,28},{5,29},{6,30},{7,31},{8,0},{9,1... | collective-permute-start | bytes 393224 | tf_op jit(solution)/shard_map/ppermute | solution.py:18
  22.0 8.9 %collective-permute-start.10 = (bf16[8,64,128]{2,1,0:T(8,128)(2,1)S(1)}, bf16[8,64,128]{2,1,0:T(8,128)(2,1)S(1)}, u32[]{:S(2)}, u32[]{:S(2)}) collective-permute-start(bf16[8,64,128]{2,1,0:T(8,128)(2,1)S(1)} %shard_map.30.own), channel_id=1, source_target_pairs={{0,8},{1,9},{2,10},{3,11},{4,12},{5,13},{6,14},{7,15},{8,16},{9,17... | collective-permute-start | bytes 393224 | tf_op jit(solution)/shard_map/ppermute | solution.py:18
  22.0 9.9 %collective-permute-start.4 = (bf16[8,64,128]{2,1,0:T(8,128)(2,1)S(1)}, bf16[8,64,128]{2,1,0:T(8,128)(2,1)S(1)}, u32[]{:S(2)}, u32[]{:S(2)}) collective-permute-start(bf16[8,64,128]{2,1,0:T(8,128)(2,1)S(1)} %shard_map.30.own), channel_id=1, source_target_pairs={{0,16},{1,17},{2,18},{3,19},{4,20},{5,21},{6,22},{7,23},{8,24},{9,... | collective-permute-start | bytes 393224 | tf_op jit(solution)/shard_map/ppermute | solution.py:18

commit v7 on v6

--- a/solution.py
+++ b/solution.py
@@ -54,7 +54,7 @@
         out[side] = turned[side].astype(jnp.bfloat16)
 
 
-def assemble(own, near, near_swapped, far, far_swapped, out):
+def assemble(own, near, near_swapped, far, out):
     shot = lax.axis_index("shot")
     x, core = shot // 2, shot % 2
     back = 4 - sign(core)
@@ -65,8 +65,8 @@
         (near.at[1], x + back, 1 - core),
         (near_swapped.at[0], x + 8 - back, 1 - core),
         (near_swapped.at[1], x + 8 - back, core),
-        (far, x + 2, core),
-        (far_swapped, x + 2, 1 - core),
+        (far.at[0], x + 2, core),
+        (far.at[1], x + 2, 1 - core),
     )
     for block, chip, side in blocks:
         place = (chip % 4) * 2 + side
@@ -212,8 +212,8 @@
     before, after, across = [spread(held, "rcv", along_y(offset)) for offset in (1, 3, 2)]
 
     near = spread(both, "shot", along_x)
-    far = spread(both[0], "shot", across_x)
-    pieces = (both, near, swap(near), far, swap(far))
+    far = spread(both, "shot", across_x)
+    pieces = (both, near, swap(near), far)
     padded = call(assemble, (8, 576, 128), bf16, pieces, [])
     work = 2 * 512 * 256 * 9 * 256
     total = call(first_kernel, (512, 256), f32, (held, padded), band, work)

time: 34.1 us -> 34.6 us (1.015)
  the two profiles are of different devices: /device:TPU:4 before, /device:TPU:1 now
where the time goes in v7:
time: 34.6 us; the launch traced here: 34.4 us
  starting transfers between devices  21.6 us (62%)
  Pallas kernels  5.99 us (17%)
  waiting for transfers between devices  5.11 us (15%)
  local copies, waits for them, and re-layouts  1.66 us (5%)
    ppermute x11, starting transfers between devices, spread(): return lax.ppermute(value, axis, [(i, partner(i)) for i in range(size)])  21.6 us
    pallas_call x9, Pallas kernels, call(): pl.pallas_call(body, out_shape=jax.ShapeDtypeStruct(shape, dtype), in_spe...  5.99 us
    ppermute x11, waiting for transfers between devices, spread(): return lax.ppermute(value, axis, [(i, partner(i)) for i in range(size)])  5.11 us
    unnamed x4, local copies, waits for them, and re-layouts  1.66 us
  transfers between devices with their start and end apart: 11, of which 3 were waited for; matrix products, arithmetic and copies ran while one was open for 0% of the time, Pallas kernels for 11%

profile of v7, /device:TPU:1, one launch (start us, length us, event | category | flops | bytes accessed | tf_op | source)
XLA Modules:
  0.0 34.4 jit_solution(325508750898135038)
XLA Ops:
  0.0 3.2 %collective-permute-start.5 = (bf16[16,8,512]{2,1,0:T(8,128)(2,1)}, bf16[16,8,512]{2,1,0:T(8,128)(2,1)S(1)}, u32[]{:S(2)}, u32[]{:S(2)}) collective-permute-start(bf16[16,8,512]{2,1,0:T(8,128)(2,1)} %own.1), channel_id=1, source_target_pairs={{0,32},{32,0},{64,96},{96,64},{128,160},{160,128},{192,224},{224,1... | collective-permute-start | bytes 393224 | tf_op jit(solution)/shard_map/ppermute | solution.py:18
  3.2 0.0 copy-start.1
  3.2 0.8 %copy-done.1 = bf16[32,4,64]{2,1,0:T(4,128)(2,1)S(1)} copy-done((bf16[32,4,64]{2,1,0:T(4,128)(2,1)S(1)}, bf16[32,4,64]{2,1,0:T(4,128)(2,1)}, u32[]{:S(2)}) %copy-start.1) | copy-done | bytes 16408
  4.0 0.2 shard_map.28
  4.2 0.1 collective-permute-start
  4.3 0.2 collective-permute-done.5.other
  4.4 0.9 %copy-done = bf16[16,8,512]{2,1,0:T(8,128)(2,1)S(1)} copy-done((bf16[16,8,512]{2,1,0:T(8,128)(2,1)S(1)}, bf16[16,8,512]{2,1,0:T(8,128)(2,1)}, u32[]{:S(2)}) %copy-start) | copy-done | bytes 131096
  5.3 0.7 %shard_map.31.own = bf16[2,512,128]{2,1,0:T(8,128)(2,1)S(1)} custom-call(bf16[16,8,512]{2,1,0:T(8,128)(2,1)S(1)} %copy-done, bf16[16,8,512]{2,1,0:T(8,128)(2,1)S(1)} %collective-permute-done.5.other, bf16[1,64,128]{2,1,0:T(8,128)(2,1)S(1)} %bitcast.3), custom_call_target="tpu_custom_call" | custom-call | bytes 1048576 | tf_op jit(solution)/shard_map/pallas_call | solution.py:162
  6.0 2.3 %collective-permute-start.6 = (bf16[2,512,128]{2,1,0:T(8,128)(2,1)S(1)}, bf16[2,512,128]{2,1,0:T(8,128)(2,1)S(1)}, u32[]{:S(2)}, u32[]{:S(2)}) collective-permute-start(bf16[2,512,128]{2,1,0:T(8,128)(2,1)S(1)} %shard_map.31.own), channel_id=1, source_target_pairs={{0,64},{32,224},{64,128},{96,32},{128,192},{160,96},{192,0},{224,1... | collective-permute-start | bytes 786440 | tf_op jit(solution)/shard_map/ppermute | solution.py:18
  8.3 0.0 collective-permute-done.blocks_1_
  8.3 5.6 %collective-permute-start.1 = (bf16[2,64,128]{2,1,0:T(8,128)(2,1)S(1)}, bf16[2,64,128]{2,1,0:T(8,128)(2,1)S(1)}, u32[]{:S(2)}, u32[]{:S(2)}) collective-permute-start(bf16[2,64,128]{2,1,0:T(8,128)(2,1)S(1)} %shard_map.29.blocks_0_), channel_id=1, source_target_pairs={{0,5},{1,4},{2,7},{3,6},{4,1},{5,0},{6,3},{7,2},{8,13},{9,12},{10,... | collective-permute-start | bytes 98312 | tf_op jit(solution)/shard_map/ppermute | solution.py:18
  13.9 0.0 collective-permute-start.2
  13.9 3.1 %collective-permute-start.3 = (bf16[2,64,128]{2,1,0:T(8,128)(2,1)S(1)}, bf16[2,64,128]{2,1,0:T(8,128)(2,1)S(1)}, u32[]{:S(2)}, u32[]{:S(2)}) collective-permute-start(bf16[2,64,128]{2,1,0:T(8,128)(2,1)S(1)} %shard_map.29.blocks_0_), channel_id=1, source_target_pairs={{0,7},{1,2},{2,1},{3,4},{4,3},{5,6},{6,5},{7,0},{8,15},{9,10},{10,... | collective-permute-start | bytes 98312 | tf_op jit(solution)/shard_map/ppermute | solution.py:18
  17.0 0.5 %collective-permute-start.8 = (bf16[2,512,128]{2,1,0:T(8,128)(2,1)S(1)}, bf16[2,512,128]{2,1,0:T(8,128)(2,1)S(1)}, u32[]{:S(2)}, u32[]{:S(2)}) collective-permute-start(bf16[2,512,128]{2,1,0:T(8,128)(2,1)S(1)} %shard_map.31.own), channel_id=1, source_target_pairs={{0,128},{32,160},{64,192},{96,224},{128,0},{160,32},{192,64},{224,... | collective-permute-start | bytes 786440 | tf_op jit(solution)/shard_map/ppermute | solution.py:18
  17.5 0.0 collective-permute-done.6.near
  17.5 2.3 %collective-permute-start.7 = (bf16[2,512,128]{2,1,0:T(8,128)(2,1)S(1)}, bf16[2,512,128]{2,1,0:T(8,128)(2,1)S(1)}, u32[]{:S(2)}, u32[]{:S(2)}) collective-permute-start(bf16[2,512,128]{2,1,0:T(8,128)(2,1)S(1)} %collective-permute-done.6.near), channel_id=1, source_target_pairs={{0,32},{32,0},{64,96},{96,64},{128,160},{160,128},{192,224},{224,1... | collective-permute-start | bytes 786440 | tf_op jit(solution)/shard_map/ppermute | solution.py:18
  19.9 0.0 collective-permute-done.1.blocks_1_
  19.9 0.0 collective-permute-done.2.blocks_2_
  19.9 0.0 collective-permute-done.3.blocks_3_
  19.9 2.8 %collective-permute-start.10 = (bf16[8,64,128]{2,1,0:T(8,128)(2,1)S(1)}, bf16[8,64,128]{2,1,0:T(8,128)(2,1)S(1)}, u32[]{:S(2)}, u32[]{:S(2)}) collective-permute-start(bf16[8,64,128]{2,1,0:T(8,128)(2,1)S(1)} %shard_map.30.own), channel_id=1, source_target_pairs={{0,24},{1,25},{2,26},{3,27},{4,28},{5,29},{6,30},{7,31},{8,0},{9,1... | collective-permute-start | bytes 393224 | tf_op jit(solution)/shard_map/ppermute | solution.py:18
  22.7 0.0 collective-permute-start.9
  22.7 1.6 %collective-permute-start.4 = (bf16[8,64,128]{2,1,0:T(8,128)(2,1)S(1)}, bf16[8,64,128]{2,1,0:T(8,128)(2,1)S(1)}, u32[]{:S(2)}, u32[]{:S(2)}) collective-permute-start(bf16[8,64,128]{2,1,0:T(8,128)(2,1)S(1)} %shard_map.30.own), channel_id=1, source_target_pairs={{0,16},{1,17},{2,18},{3,19},{4,20},{5,21},{6,22},{7,23},{8,24},{9,... | collective-permute-start | bytes 393224 | tf_op jit(solution)/shard_map/ppermute | solution.py:18
  24.4 1.9 %collective-permute-done.8.far = bf16[2,512,128]{2,1,0:T(8,128)(2,1)S(1)} collective-permute-done((bf16[2,512,128]{2,1,0:T(8,128)(2,1)S(1)}, bf16[2,512,128]{2,1,0:T(8,128)(2,1)S(1)}, u32[]{:S(2)}, u32[]{:S(2)}) %collective-permute-start.8) | collective-permute-done | bytes 262176 | tf_op jit(solution)/shard_map/ppermute | solution.py:18
  26.3 0.0 collective-permute-done.7.near_swapped
  26.3 0.1 shard_map.32.padded
  26.4 1.0 %shard_map.33.so_far = f32[512,256]{1,0:T(8,128)S(1)} custom-call(bf16[8,64,128]{2,1,0:T(8,128)(2,1)S(1)} %shard_map.30.own, bf16[8,576,128]{2,1,0:T(8,128)(2,1)S(1)} %shard_map.32.padded), custom_call_target="tpu_custom_call" | custom-call | flops 603979776 | bytes 1048576 | tf_op jit(solution)/shard_map/pallas_call | solution.py:162
  27.4 0.0 collective-permute-done.10.response
  27.4 1.0 %shard_map.34.so_far = f32[512,256]{1,0:T(8,128)S(1)} custom-call(bf16[8,64,128]{2,1,0:T(8,128)(2,1)S(1)} %collective-permute-done.10.response, bf16[8,576,128]{2,1,0:T(8,128)(2,1)S(1)} %shard_map.32.padded, f32[512,256]{1,0:T(8,128)S(1)} %shard_map.33.so_far), custom_call_target="tpu_custom_call" | custom-call | flops 603979776 | bytes 1048576 | tf_op jit(solution)/shard_map/pallas_call | solution.py:162
  28.4 3.0 %collective-permute-done.9.response = bf16[8,64,128]{2,1,0:T(8,128)(2,1)S(1)} collective-permute-done((bf16[8,64,128]{2,1,0:T(8,128)(2,1)S(1)}, bf16[8,64,128]{2,1,0:T(8,128)(2,1)S(1)}, u32[]{:S(2)}, u32[]{:S(2)}) %collective-permute-start.9) | collective-permute-done | bytes 131104 | tf_op jit(solution)/shard_map/ppermute | solution.py:18
  31.4 0.9 %shard_map.35.so_far = f32[512,256]{1,0:T(8,128)S(1)} custom-call(bf16[8,64,128]{2,1,0:T(8,128)(2,1)S(1)} %collective-permute-done.9.response, bf16[8,576,128]{2,1,0:T(8,128)(2,1)S(1)} %shard_map.32.padded, f32[512,256]{1,0:T(8,128)S(1)} %shard_map.34.so_far), custom_call_target="tpu_custom_call" | custom-call | flops 603979776 | bytes 1048576 | tf_op jit(solution)/shard_map/pallas_call | solution.py:162
  32.3 0.0 collective-permute-done.4.across
  32.3 2.1 %shard_map.36 = bf16[32,8,512]{2,1,0:T(8,128)(2,1)} custom-call(bf16[8,64,128]{2,1,0:T(8,128)(2,1)S(1)} %collective-permute-done.4.across, bf16[8,576,128]{2,1,0:T(8,128)(2,1)S(1)} %shard_map.32.padded, f32[512,256]{1,0:T(8,128)S(1)} %shard_map.35.so_far), custom_call_target="tpu_custom_call" | custom-call | flops 603979776 | bytes 1048576 | tf_op jit(solution)/shard_map/pallas_call | solution.py:162
  (3 shorter events, 0.0 us)
Async XLA Ops:
  0.0 4.4 %collective-permute-start.5 = (bf16[16,8,512]{2,1,0:T(8,128)(2,1)}, bf16[16,8,512]{2,1,0:T(8,128)(2,1)S(1)}, u32[]{:S(2)}, u32[]{:S(2)}) collective-permute-start(bf16[16,8,512]{2,1,0:T(8,128)(2,1)} %own.1), channel_id=1, source_target_pairs={{0,32},{32,0},{64,96},{96,64},{128,160},{160,128},{192,224},{224,1... | collective-permute-start | bytes 393224 | tf_op jit(solution)/shard_map/ppermute | solution.py:18
  3.2 0.8 %copy-start.1 = (bf16[32,4,64]{2,1,0:T(4,128)(2,1)S(1)}, bf16[32,4,64]{2,1,0:T(4,128)(2,1)}, u32[]{:S(2)}) copy-start(bf16[32,4,64]{2,1,0:T(4,128)(2,1)} %param.2) | copy-start | bytes 49156
  4.2 4.1 %collective-permute-start = (bf16[1,64,128]{2,1,0:T(8,128)(2,1)S(1)}, bf16[1,64,128]{2,1,0:T(8,128)(2,1)S(1)}, u32[]{:S(2)}, u32[]{:S(2)}) collective-permute-start(bf16[1,64,128]{2,1,0:T(8,128)(2,1)S(1)} %bitcast.2), channel_id=1, source_target_pairs={{0,1},{1,0},{2,3},{3,2},{4,5},{5,4},{6,7},{7,6},{8,9},{9,8},{10,11... | collective-permute-start | bytes 49160 | tf_op jit(solution)/shard_map/ppermute | solution.py:18
  4.4 0.9 %copy-start = (bf16[16,8,512]{2,1,0:T(8,128)(2,1)S(1)}, bf16[16,8,512]{2,1,0:T(8,128)(2,1)}, u32[]{:S(2)}) copy-start(bf16[16,8,512]{2,1,0:T(8,128)(2,1)} %own.1) | copy-start | bytes 393220
  6.0 11.5 %collective-permute-start.6 = (bf16[2,512,128]{2,1,0:T(8,128)(2,1)S(1)}, bf16[2,512,128]{2,1,0:T(8,128)(2,1)S(1)}, u32[]{:S(2)}, u32[]{:S(2)}) collective-permute-start(bf16[2,512,128]{2,1,0:T(8,128)(2,1)S(1)} %shard_map.31.own), channel_id=1, source_target_pairs={{0,64},{32,224},{64,128},{96,32},{128,192},{160,96},{192,0},{224,1... | collective-permute-start | bytes 786440 | tf_op jit(solution)/shard_map/ppermute | solution.py:18
  8.3 11.6 %collective-permute-start.1 = (bf16[2,64,128]{2,1,0:T(8,128)(2,1)S(1)}, bf16[2,64,128]{2,1,0:T(8,128)(2,1)S(1)}, u32[]{:S(2)}, u32[]{:S(2)}) collective-permute-start(bf16[2,64,128]{2,1,0:T(8,128)(2,1)S(1)} %shard_map.29.blocks_0_), channel_id=1, source_target_pairs={{0,5},{1,4},{2,7},{3,6},{4,1},{5,0},{6,3},{7,2},{8,13},{9,12},{10,... | collective-permute-start | bytes 98312 | tf_op jit(solution)/shard_map/ppermute | solution.py:18
  13.9 6.0 %collective-permute-start.2 = (bf16[2,64,128]{2,1,0:T(8,128)(2,1)S(1)}, bf16[2,64,128]{2,1,0:T(8,128)(2,1)S(1)}, u32[]{:S(2)}, u32[]{:S(2)}) collective-permute-start(bf16[2,64,128]{2,1,0:T(8,128)(2,1)S(1)} %shard_map.29.blocks_0_), channel_id=1, source_target_pairs={{0,6},{1,3},{2,0},{3,5},{4,2},{5,7},{6,4},{7,1},{8,14},{9,11},{10,... | collective-permute-start | bytes 98312 | tf_op jit(solution)/shard_map/ppermute | solution.py:18
  13.9 6.0 %collective-permute-start.3 = (bf16[2,64,128]{2,1,0:T(8,128)(2,1)S(1)}, bf16[2,64,128]{2,1,0:T(8,128)(2,1)S(1)}, u32[]{:S(2)}, u32[]{:S(2)}) collective-permute-start(bf16[2,64,128]{2,1,0:T(8,128)(2,1)S(1)} %shard_map.29.blocks_0_), channel_id=1, source_target_pairs={{0,7},{1,2},{2,1},{3,4},{4,3},{5,6},{6,5},{7,0},{8,15},{9,10},{10,... | collective-permute-start | bytes 98312 | tf_op jit(solution)/shard_map/ppermute | solution.py:18
  17.0 9.3 %collective-permute-start.8 = (bf16[2,512,128]{2,1,0:T(8,128)(2,1)S(1)}, bf16[2,512,128]{2,1,0:T(8,128)(2,1)S(1)}, u32[]{:S(2)}, u32[]{:S(2)}) collective-permute-start(bf16[2,512,128]{2,1,0:T(8,128)(2,1)S(1)} %shard_map.31.own), channel_id=1, source_target_pairs={{0,128},{32,160},{64,192},{96,224},{128,0},{160,32},{192,64},{224,... | collective-permute-start | bytes 786440 | tf_op jit(solution)/shard_map/ppermute | solution.py:18
  17.5 8.8 %collective-permute-start.7 = (bf16[2,512,128]{2,1,0:T(8,128)(2,1)S(1)}, bf16[2,512,128]{2,1,0:T(8,128)(2,1)S(1)}, u32[]{:S(2)}, u32[]{:S(2)}) collective-permute-start(bf16[2,512,128]{2,1,0:T(8,128)(2,1)S(1)} %collective-permute-done.6.near), channel_id=1, source_target_pairs={{0,32},{32,0},{64,96},{96,64},{128,160},{160,128},{192,224},{224,1... | collective-permute-start | bytes 786440 | tf_op jit(solution)/shard_map/ppermute | solution.py:18
  19.9 7.5 %collective-permute-start.10 = (bf16[8,64,128]{2,1,0:T(8,128)(2,1)S(1)}, bf16[8,64,128]{2,1,0:T(8,128)(2,1)S(1)}, u32[]{:S(2)}, u32[]{:S(2)}) collective-permute-start(bf16[8,64,128]{2,1,0:T(8,128)(2,1)S(1)} %shard_map.30.own), channel_id=1, source_target_pairs={{0,24},{1,25},{2,26},{3,27},{4,28},{5,29},{6,30},{7,31},{8,0},{9,1... | collective-permute-start | bytes 393224 | tf_op jit(solution)/shard_map/ppermute | solution.py:18
  22.7 8.7 %collective-permute-start.9 = (bf16[8,64,128]{2,1,0:T(8,128)(2,1)S(1)}, bf16[8,64,128]{2,1,0:T(8,128)(2,1)S(1)}, u32[]{:S(2)}, u32[]{:S(2)}) collective-permute-start(bf16[8,64,128]{2,1,0:T(8,128)(2,1)S(1)} %shard_map.30.own), channel_id=1, source_target_pairs={{0,8},{1,9},{2,10},{3,11},{4,12},{5,13},{6,14},{7,15},{8,16},{9,17... | collective-permute-start | bytes 393224 | tf_op jit(solution)/shard_map/ppermute | solution.py:18
  22.7 9.6 %collective-permute-start.4 = (bf16[8,64,128]{2,1,0:T(8,128)(2,1)S(1)}, bf16[8,64,128]{2,1,0:T(8,128)(2,1)S(1)}, u32[]{:S(2)}, u32[]{:S(2)}) collective-permute-start(bf16[8,64,128]{2,1,0:T(8,128)(2,1)S(1)} %shard_map.30.own), channel_id=1, source_target_pairs={{0,16},{1,17},{2,18},{3,19},{4,20},{5,21},{6,22},{7,23},{8,24},{9,... | collective-permute-start | bytes 393224 | tf_op jit(solution)/shard_map/ppermute | solution.py:18

commit v8 on v7

--- a/solution.py
+++ b/solution.py
@@ -141,9 +141,9 @@
     add_products((offset,), (response,), padded, band, rows, total)
 
 
-def last_kernel(across, padded, so_far, out, band, rows, total, placed):
+def last_kernel(before, padded, so_far, out, band, rows, total, placed):
     total[...] = so_far[...]
-    add_products((2,), (across,), padded, band, rows, total)
+    add_products((1,), (before,), padded, band, rows, total)
     turned = total[...].T
     skewed = [pltpu.roll(turned[u * 32 : u * 32 + 32, :], u, 1) for u in range(8)]
     lane = lax.broadcasted_iota(jnp.int32, (32, 512), 1)
@@ -217,14 +217,14 @@
     padded = call(assemble, (8, 576, 128), bf16, pieces, [])
     work = 2 * 512 * 256 * 9 * 256
     total = call(first_kernel, (512, 256), f32, (held, padded), band, work)
-    for offset, block in ((3, after), (1, before)):
+    for offset, block in ((2, across), (3, after)):
         body = functools.partial(middle_kernel, offset)
         total = call(body, (512, 256), f32, (block, padded, total), band, work)
     return call(
         last_kernel,
         (32, 8, 512),
         bf16,
-        (across, padded, total),
+        (before, padded, total),
         band + [((512, 256), f32), ((4, 256, 128), f32)],
         work,
     )

time: 34.6 us -> 32.8 us (0.948)
  waiting for transfers between devices: 5.11 us -> 3.33 us
    ppermute x11, waiting for transfers between devices: 5.11 us -> 3.33 us  [spread(): return lax.ppermute(value, axis, [(i, partner(i)) for i in range(size)])]
  transfers between devices with their start and end apart: 11 -> 11, of which waited for: 3 -> 3; matrix products, arithmetic and copies ran while one was open for 0% -> 0% of each run, Pallas kernels for 11% -> 12%
where the time goes in v8:
time: 32.8 us; the launch traced here: 32.7 us
  starting transfers between devices  21.6 us (66%)
  Pallas kernels  5.99 us (18%)
  waiting for transfers between devices  3.33 us (10%)
  local copies, waits for them, and re-layouts  1.66 us (5%)
    ppermute x11, starting transfers between devices, spread(): return lax.ppermute(value, axis, [(i, partner(i)) for i in range(size)])  21.6 us
    pallas_call x9, Pallas kernels, call(): pl.pallas_call(body, out_shape=jax.ShapeDtypeStruct(shape, dtype), in_spe...  5.99 us
    ppermute x11, waiting for transfers between devices, spread(): return lax.ppermute(value, axis, [(i, partner(i)) for i in range(size)])  3.33 us
    unnamed x4, local copies, waits for them, and re-layouts  1.66 us
  transfers between devices with their start and end apart: 11, of which 3 were waited for; matrix products, arithmetic and copies ran while one was open for 0% of the time, Pallas kernels for 12%

profile of v8, /device:TPU:1, one launch (start us, length us, event | category | flops | bytes accessed | tf_op | source)
XLA Modules:
  0.0 32.7 jit_solution(17015557059770719194)
XLA Ops:
  0.0 3.2 %collective-permute-start.5 = (bf16[16,8,512]{2,1,0:T(8,128)(2,1)}, bf16[16,8,512]{2,1,0:T(8,128)(2,1)S(1)}, u32[]{:S(2)}, u32[]{:S(2)}) collective-permute-start(bf16[16,8,512]{2,1,0:T(8,128)(2,1)} %own.1), channel_id=1, source_target_pairs={{0,32},{32,0},{64,96},{96,64},{128,160},{160,128},{192,224},{224,1... | collective-permute-start | bytes 393224 | tf_op jit(solution)/shard_map/ppermute | solution.py:18
  3.2 0.8 %copy-done.1 = bf16[32,4,64]{2,1,0:T(4,128)(2,1)S(1)} copy-done((bf16[32,4,64]{2,1,0:T(4,128)(2,1)S(1)}, bf16[32,4,64]{2,1,0:T(4,128)(2,1)}, u32[]{:S(2)}) %copy-start.1) | copy-done | bytes 16408
  4.0 0.2 shard_map.28
  4.2 0.1 collective-permute-start
  4.3 0.2 collective-permute-done.5.other
  4.4 0.0 copy-start
  4.4 0.9 %copy-done = bf16[16,8,512]{2,1,0:T(8,128)(2,1)S(1)} copy-done((bf16[16,8,512]{2,1,0:T(8,128)(2,1)S(1)}, bf16[16,8,512]{2,1,0:T(8,128)(2,1)}, u32[]{:S(2)}) %copy-start) | copy-done | bytes 131096
  5.3 0.7 %shard_map.31.own = bf16[2,512,128]{2,1,0:T(8,128)(2,1)S(1)} custom-call(bf16[16,8,512]{2,1,0:T(8,128)(2,1)S(1)} %copy-done, bf16[16,8,512]{2,1,0:T(8,128)(2,1)S(1)} %collective-permute-done.5.other, bf16[1,64,128]{2,1,0:T(8,128)(2,1)S(1)} %bitcast.3), custom_call_target="tpu_custom_call" | custom-call | bytes 1048576 | tf_op jit(solution)/shard_map/pallas_call | solution.py:162
  6.0 2.3 %collective-permute-start.6 = (bf16[2,512,128]{2,1,0:T(8,128)(2,1)S(1)}, bf16[2,512,128]{2,1,0:T(8,128)(2,1)S(1)}, u32[]{:S(2)}, u32[]{:S(2)}) collective-permute-start(bf16[2,512,128]{2,1,0:T(8,128)(2,1)S(1)} %shard_map.31.own), channel_id=1, source_target_pairs={{0,64},{32,224},{64,128},{96,32},{128,192},{160,96},{192,0},{224,1... | collective-permute-start | bytes 786440 | tf_op jit(solution)/shard_map/ppermute | solution.py:18
  8.3 0.0 collective-permute-done.blocks_1_
  8.3 5.6 %collective-permute-start.1 = (bf16[2,64,128]{2,1,0:T(8,128)(2,1)S(1)}, bf16[2,64,128]{2,1,0:T(8,128)(2,1)S(1)}, u32[]{:S(2)}, u32[]{:S(2)}) collective-permute-start(bf16[2,64,128]{2,1,0:T(8,128)(2,1)S(1)} %shard_map.29.blocks_0_), channel_id=1, source_target_pairs={{0,5},{1,4},{2,7},{3,6},{4,1},{5,0},{6,3},{7,2},{8,13},{9,12},{10,... | collective-permute-start | bytes 98312 | tf_op jit(solution)/shard_map/ppermute | solution.py:18
  13.9 0.0 collective-permute-start.2
  13.9 3.1 %collective-permute-start.3 = (bf16[2,64,128]{2,1,0:T(8,128)(2,1)S(1)}, bf16[2,64,128]{2,1,0:T(8,128)(2,1)S(1)}, u32[]{:S(2)}, u32[]{:S(2)}) collective-permute-start(bf16[2,64,128]{2,1,0:T(8,128)(2,1)S(1)} %shard_map.29.blocks_0_), channel_id=1, source_target_pairs={{0,7},{1,2},{2,1},{3,4},{4,3},{5,6},{6,5},{7,0},{8,15},{9,10},{10,... | collective-permute-start | bytes 98312 | tf_op jit(solution)/shard_map/ppermute | solution.py:18
  17.0 0.5 %collective-permute-start.8 = (bf16[2,512,128]{2,1,0:T(8,128)(2,1)S(1)}, bf16[2,512,128]{2,1,0:T(8,128)(2,1)S(1)}, u32[]{:S(2)}, u32[]{:S(2)}) collective-permute-start(bf16[2,512,128]{2,1,0:T(8,128)(2,1)S(1)} %shard_map.31.own), channel_id=1, source_target_pairs={{0,128},{32,160},{64,192},{96,224},{128,0},{160,32},{192,64},{224,... | collective-permute-start | bytes 786440 | tf_op jit(solution)/shard_map/ppermute | solution.py:18
  17.5 0.0 collective-permute-done.6.near
  17.5 2.3 %collective-permute-start.7 = (bf16[2,512,128]{2,1,0:T(8,128)(2,1)S(1)}, bf16[2,512,128]{2,1,0:T(8,128)(2,1)S(1)}, u32[]{:S(2)}, u32[]{:S(2)}) collective-permute-start(bf16[2,512,128]{2,1,0:T(8,128)(2,1)S(1)} %collective-permute-done.6.near), channel_id=1, source_target_pairs={{0,32},{32,0},{64,96},{96,64},{128,160},{160,128},{192,224},{224,1... | collective-permute-start | bytes 786440 | tf_op jit(solution)/shard_map/ppermute | solution.py:18
  19.9 0.0 collective-permute-done.1.blocks_1_
  19.9 0.0 collective-permute-done.2.blocks_2_
  19.9 0.0 collective-permute-done.3.blocks_3_
  19.9 3.0 %collective-permute-start.10 = (bf16[8,64,128]{2,1,0:T(8,128)(2,1)S(1)}, bf16[8,64,128]{2,1,0:T(8,128)(2,1)S(1)}, u32[]{:S(2)}, u32[]{:S(2)}) collective-permute-start(bf16[8,64,128]{2,1,0:T(8,128)(2,1)S(1)} %shard_map.30.own), channel_id=1, source_target_pairs={{0,16},{1,17},{2,18},{3,19},{4,20},{5,21},{6,22},{7,23},{8,24},{9,... | collective-permute-start | bytes 393224 | tf_op jit(solution)/shard_map/ppermute | solution.py:18
  22.9 0.8 %collective-permute-start.9 = (bf16[8,64,128]{2,1,0:T(8,128)(2,1)S(1)}, bf16[8,64,128]{2,1,0:T(8,128)(2,1)S(1)}, u32[]{:S(2)}, u32[]{:S(2)}) collective-permute-start(bf16[8,64,128]{2,1,0:T(8,128)(2,1)S(1)} %shard_map.30.own), channel_id=1, source_target_pairs={{0,24},{1,25},{2,26},{3,27},{4,28},{5,29},{6,30},{7,31},{8,0},{9,1... | collective-permute-start | bytes 393224 | tf_op jit(solution)/shard_map/ppermute | solution.py:18
  23.7 0.7 %collective-permute-start.4 = (bf16[8,64,128]{2,1,0:T(8,128)(2,1)S(1)}, bf16[8,64,128]{2,1,0:T(8,128)(2,1)S(1)}, u32[]{:S(2)}, u32[]{:S(2)}) collective-permute-start(bf16[8,64,128]{2,1,0:T(8,128)(2,1)S(1)} %shard_map.30.own), channel_id=1, source_target_pairs={{0,8},{1,9},{2,10},{3,11},{4,12},{5,13},{6,14},{7,15},{8,16},{9,17... | collective-permute-start | bytes 393224 | tf_op jit(solution)/shard_map/ppermute | solution.py:18
  24.4 1.9 %collective-permute-done.8.far = bf16[2,512,128]{2,1,0:T(8,128)(2,1)S(1)} collective-permute-done((bf16[2,512,128]{2,1,0:T(8,128)(2,1)S(1)}, bf16[2,512,128]{2,1,0:T(8,128)(2,1)S(1)}, u32[]{:S(2)}, u32[]{:S(2)}) %collective-permute-start.8) | collective-permute-done | bytes 262176 | tf_op jit(solution)/shard_map/ppermute | solution.py:18
  26.3 0.0 collective-permute-done.7.near_swapped
  26.3 0.1 shard_map.32.padded
  26.4 1.0 %shard_map.33.so_far = f32[512,256]{1,0:T(8,128)S(1)} custom-call(bf16[8,64,128]{2,1,0:T(8,128)(2,1)S(1)} %shard_map.30.own, bf16[8,576,128]{2,1,0:T(8,128)(2,1)S(1)} %shard_map.32.padded), custom_call_target="tpu_custom_call" | custom-call | flops 603979776 | bytes 1048576 | tf_op jit(solution)/shard_map/pallas_call | solution.py:162
  27.4 0.0 collective-permute-done.10.response
  27.4 1.0 %shard_map.34.so_far = f32[512,256]{1,0:T(8,128)S(1)} custom-call(bf16[8,64,128]{2,1,0:T(8,128)(2,1)S(1)} %collective-permute-done.10.response, bf16[8,576,128]{2,1,0:T(8,128)(2,1)S(1)} %shard_map.32.padded, f32[512,256]{1,0:T(8,128)S(1)} %shard_map.33.so_far), custom_call_target="tpu_custom_call" | custom-call | flops 603979776 | bytes 1048576 | tf_op jit(solution)/shard_map/pallas_call | solution.py:162
  28.4 1.2 %collective-permute-done.9.response = bf16[8,64,128]{2,1,0:T(8,128)(2,1)S(1)} collective-permute-done((bf16[8,64,128]{2,1,0:T(8,128)(2,1)S(1)}, bf16[8,64,128]{2,1,0:T(8,128)(2,1)S(1)}, u32[]{:S(2)}, u32[]{:S(2)}) %collective-permute-start.9) | collective-permute-done | bytes 131104 | tf_op jit(solution)/shard_map/ppermute | solution.py:18
  29.6 0.9 %shard_map.35.so_far = f32[512,256]{1,0:T(8,128)S(1)} custom-call(bf16[8,64,128]{2,1,0:T(8,128)(2,1)S(1)} %collective-permute-done.9.response, bf16[8,576,128]{2,1,0:T(8,128)(2,1)S(1)} %shard_map.32.padded, f32[512,256]{1,0:T(8,128)S(1)} %shard_map.34.so_far), custom_call_target="tpu_custom_call" | custom-call | flops 603979776 | bytes 1048576 | tf_op jit(solution)/shard_map/pallas_call | solution.py:162
  30.5 0.0 collective-permute-done.4.before
  30.6 2.1 %shard_map.36 = bf16[32,8,512]{2,1,0:T(8,128)(2,1)} custom-call(bf16[8,64,128]{2,1,0:T(8,128)(2,1)S(1)} %collective-permute-done.4.before, bf16[8,576,128]{2,1,0:T(8,128)(2,1)S(1)} %shard_map.32.padded, f32[512,256]{1,0:T(8,128)S(1)} %shard_map.35.so_far), custom_call_target="tpu_custom_call" | custom-call | flops 603979776 | bytes 1048576 | tf_op jit(solution)/shard_map/pallas_call | solution.py:162
  (3 shorter events, 0.0 us)
Async XLA Ops:
  0.0 4.4 %collective-permute-start.5 = (bf16[16,8,512]{2,1,0:T(8,128)(2,1)}, bf16[16,8,512]{2,1,0:T(8,128)(2,1)S(1)}, u32[]{:S(2)}, u32[]{:S(2)}) collective-permute-start(bf16[16,8,512]{2,1,0:T(8,128)(2,1)} %own.1), channel_id=1, source_target_pairs={{0,32},{32,0},{64,96},{96,64},{128,160},{160,128},{192,224},{224,1... | collective-permute-start | bytes 393224 | tf_op jit(solution)/shard_map/ppermute | solution.py:18
  3.2 0.8 %copy-start.1 = (bf16[32,4,64]{2,1,0:T(4,128)(2,1)S(1)}, bf16[32,4,64]{2,1,0:T(4,128)(2,1)}, u32[]{:S(2)}) copy-start(bf16[32,4,64]{2,1,0:T(4,128)(2,1)} %param.2) | copy-start | bytes 49156
  4.2 4.1 %collective-permute-start = (bf16[1,64,128]{2,1,0:T(8,128)(2,1)S(1)}, bf16[1,64,128]{2,1,0:T(8,128)(2,1)S(1)}, u32[]{:S(2)}, u32[]{:S(2)}) collective-permute-start(bf16[1,64,128]{2,1,0:T(8,128)(2,1)S(1)} %bitcast.2), channel_id=1, source_target_pairs={{0,1},{1,0},{2,3},{3,2},{4,5},{5,4},{6,7},{7,6},{8,9},{9,8},{10,11... | collective-permute-start | bytes 49160 | tf_op jit(solution)/shard_map/ppermute | solution.py:18
  4.4 0.9 %copy-start = (bf16[16,8,512]{2,1,0:T(8,128)(2,1)S(1)}, bf16[16,8,512]{2,1,0:T(8,128)(2,1)}, u32[]{:S(2)}) copy-start(bf16[16,8,512]{2,1,0:T(8,128)(2,1)} %own.1) | copy-start | bytes 393220
  6.0 11.5 %collective-permute-start.6 = (bf16[2,512,128]{2,1,0:T(8,128)(2,1)S(1)}, bf16[2,512,128]{2,1,0:T(8,128)(2,1)S(1)}, u32[]{:S(2)}, u32[]{:S(2)}) collective-permute-start(bf16[2,512,128]{2,1,0:T(8,128)(2,1)S(1)} %shard_map.31.own), channel_id=1, source_target_pairs={{0,64},{32,224},{64,128},{96,32},{128,192},{160,96},{192,0},{224,1... | collective-permute-start | bytes 786440 | tf_op jit(solution)/shard_map/ppermute | solution.py:18
  8.3 11.6 %collective-permute-start.1 = (bf16[2,64,128]{2,1,0:T(8,128)(2,1)S(1)}, bf16[2,64,128]{2,1,0:T(8,128)(2,1)S(1)}, u32[]{:S(2)}, u32[]{:S(2)}) collective-permute-start(bf16[2,64,128]{2,1,0:T(8,128)(2,1)S(1)} %shard_map.29.blocks_0_), channel_id=1, source_target_pairs={{0,5},{1,4},{2,7},{3,6},{4,1},{5,0},{6,3},{7,2},{8,13},{9,12},{10,... | collective-permute-start | bytes 98312 | tf_op jit(solution)/shard_map/ppermute | solution.py:18
  13.9 6.0 %collective-permute-start.2 = (bf16[2,64,128]{2,1,0:T(8,128)(2,1)S(1)}, bf16[2,64,128]{2,1,0:T(8,128)(2,1)S(1)}, u32[]{:S(2)}, u32[]{:S(2)}) collective-permute-start(bf16[2,64,128]{2,1,0:T(8,128)(2,1)S(1)} %shard_map.29.blocks_0_), channel_id=1, source_target_pairs={{0,6},{1,3},{2,0},{3,5},{4,2},{5,7},{6,4},{7,1},{8,14},{9,11},{10,... | collective-permute-start | bytes 98312 | tf_op jit(solution)/shard_map/ppermute | solution.py:18
  13.9 6.0 %collective-permute-start.3 = (bf16[2,64,128]{2,1,0:T(8,128)(2,1)S(1)}, bf16[2,64,128]{2,1,0:T(8,128)(2,1)S(1)}, u32[]{:S(2)}, u32[]{:S(2)}) collective-permute-start(bf16[2,64,128]{2,1,0:T(8,128)(2,1)S(1)} %shard_map.29.blocks_0_), channel_id=1, source_target_pairs={{0,7},{1,2},{2,1},{3,4},{4,3},{5,6},{6,5},{7,0},{8,15},{9,10},{10,... | collective-permute-start | bytes 98312 | tf_op jit(solution)/shard_map/ppermute | solution.py:18
  17.0 9.3 %collective-permute-start.8 = (bf16[2,512,128]{2,1,0:T(8,128)(2,1)S(1)}, bf16[2,512,128]{2,1,0:T(8,128)(2,1)S(1)}, u32[]{:S(2)}, u32[]{:S(2)}) collective-permute-start(bf16[2,512,128]{2,1,0:T(8,128)(2,1)S(1)} %shard_map.31.own), channel_id=1, source_target_pairs={{0,128},{32,160},{64,192},{96,224},{128,0},{160,32},{192,64},{224,... | collective-permute-start | bytes 786440 | tf_op jit(solution)/shard_map/ppermute | solution.py:18
  17.5 8.8 %collective-permute-start.7 = (bf16[2,512,128]{2,1,0:T(8,128)(2,1)S(1)}, bf16[2,512,128]{2,1,0:T(8,128)(2,1)S(1)}, u32[]{:S(2)}, u32[]{:S(2)}) collective-permute-start(bf16[2,512,128]{2,1,0:T(8,128)(2,1)S(1)} %collective-permute-done.6.near), channel_id=1, source_target_pairs={{0,32},{32,0},{64,96},{96,64},{128,160},{160,128},{192,224},{224,1... | collective-permute-start | bytes 786440 | tf_op jit(solution)/shard_map/ppermute | solution.py:18
  19.9 7.5 %collective-permute-start.10 = (bf16[8,64,128]{2,1,0:T(8,128)(2,1)S(1)}, bf16[8,64,128]{2,1,0:T(8,128)(2,1)S(1)}, u32[]{:S(2)}, u32[]{:S(2)}) collective-permute-start(bf16[8,64,128]{2,1,0:T(8,128)(2,1)S(1)} %shard_map.30.own), channel_id=1, source_target_pairs={{0,16},{1,17},{2,18},{3,19},{4,20},{5,21},{6,22},{7,23},{8,24},{9,... | collective-permute-start | bytes 393224 | tf_op jit(solution)/shard_map/ppermute | solution.py:18
  22.9 6.7 %collective-permute-start.9 = (bf16[8,64,128]{2,1,0:T(8,128)(2,1)S(1)}, bf16[8,64,128]{2,1,0:T(8,128)(2,1)S(1)}, u32[]{:S(2)}, u32[]{:S(2)}) collective-permute-start(bf16[8,64,128]{2,1,0:T(8,128)(2,1)S(1)} %shard_map.30.own), channel_id=1, source_target_pairs={{0,24},{1,25},{2,26},{3,27},{4,28},{5,29},{6,30},{7,31},{8,0},{9,1... | collective-permute-start | bytes 393224 | tf_op jit(solution)/shard_map/ppermute | solution.py:18
  23.7 6.9 %collective-permute-start.4 = (bf16[8,64,128]{2,1,0:T(8,128)(2,1)S(1)}, bf16[8,64,128]{2,1,0:T(8,128)(2,1)S(1)}, u32[]{:S(2)}, u32[]{:S(2)}) collective-permute-start(bf16[8,64,128]{2,1,0:T(8,128)(2,1)S(1)} %shard_map.30.own), channel_id=1, source_target_pairs={{0,8},{1,9},{2,10},{3,11},{4,12},{5,13},{6,14},{7,15},{8,16},{9,17... | collective-permute-start | bytes 393224 | tf_op jit(solution)/shard_map/ppermute | solution.py:18

commit v9 on v8

--- a/solution.py
+++ b/solution.py
@@ -7,7 +7,7 @@
 from jax.experimental.pallas import tpu as pltpu
 from jax.sharding import PartitionSpec as P
 
-RING8 = (0, 1, 5, 4, 2, 3, 7, 6)
+RING8 = (0, 1, 2, 3, 7, 6, 5, 4)
 VMEM = pl.BlockSpec(memory_space=pltpu.VMEM)
 JOIN_COST = 2**33
 PARAMS = pltpu.CompilerParams(vmem_limit_bytes=40 * 2**20)
@@ -88,63 +88,65 @@
     return slot
 
 
-def add_products(offsets, responses, padded, band, rows_f32, total):
+def add_products(offset, response, padded, band, rows_f32, so_far, total):
     rcv = lax.axis_index("rcv")
     y, z = rcv // 8, rcv % 8
     slots = [position_of((sign(z) * (wanted - z) + 64) % 8) for wanted in range(8)]
-    for response, offset in zip(responses, offsets, strict=True):
-        for half in range(2):
-            for q in range(4):
-                piece = response[slots[half * 4 + q]]
-                rows_f32[half, q * 64 : q * 64 + 64, :] = piece.astype(jnp.float32)
-            wide = jnp.concatenate(
-                [rows_f32[half, pl.ds(m, 16, stride=16), :] for m in range(16)]
-                + [jnp.zeros((16, 384), jnp.float32)],
-                axis=1,
-            )
-            for shift in range(4):
-                band[half, shift * 16 : shift * 16 + 16, :] = pltpu.roll(
-                    wide, 128 + 32 * shift, 1
-                ).astype(jnp.bfloat16)
-        place = ((y + 4 - offset) % 4) * 2
-        even_rows, odd_rows, sides = [], [], []
-        for group in range(5):
-            sides += [
-                padded[place + half, 64 - 16 * group : 576 - 16 * group, :] for half in range(2)
-            ]
-            for rows, step in ((even_rows, 2 * group), (odd_rows, 2 * group + 1)):
-                if step <= 8:
-                    for half in range(2):
-                        for late in range(2):
-                            first = (2 * step - late + 1) * 128
-                            rows.append(band[half, :, first : first + 256])
-        total[...] += jnp.dot(
-            jnp.concatenate(sides, axis=1),
-            jnp.concatenate(even_rows, axis=0),
-            preferred_element_type=jnp.float32,
+    for half in range(2):
+        for q in range(4):
+            piece = response[slots[half * 4 + q]]
+            rows_f32[half, q * 64 : q * 64 + 64, :] = piece.astype(jnp.float32)
+        wide = jnp.concatenate(
+            [rows_f32[half, pl.ds(m, 16, stride=16), :] for m in range(16)]
+            + [jnp.zeros((16, 384), jnp.float32)],
+            axis=1,
         )
-        odd = jnp.dot(
-            jnp.concatenate(sides[:8], axis=1),
-            jnp.concatenate(odd_rows, axis=0),
-            preferred_element_type=jnp.float32,
-        )
-        total[8:, :] += odd[:504, :]
+        for shift in range(4):
+            band[half, shift * 16 : shift * 16 + 16, :] = pltpu.roll(
+                wide, 128 + 32 * shift, 1
+            ).astype(jnp.bfloat16)
+    place = ((y + 4 - offset) % 4) * 2
+    even_rows, odd_rows, sides = [], [], []
+    for group in range(5):
+        sides += [
+            padded[place + half, 64 - 16 * group : 576 - 16 * group, :] for half in range(2)
+        ]
+        for rows, step in ((even_rows, 2 * group), (odd_rows, 2 * group + 1)):
+            if step <= 8:
+                for half in range(2):
+                    for late in range(2):
+                        first = (2 * step - late + 1) * 128
+                        rows.append(band[half, :, first : first + 256])
+    even = jnp.dot(
+        jnp.concatenate(sides, axis=1),
+        jnp.concatenate(even_rows, axis=0),
+        preferred_element_type=jnp.float32,
+    )
+    odd = jnp.dot(
+        jnp.concatenate(sides[:8], axis=1),
+        jnp.concatenate(odd_rows, axis=0),
+        preferred_element_type=jnp.float32,
+    )
+    if so_far is None:
+        total[:8, :] = even[:8, :]
+        total[8:, :] = even[8:, :] + odd[:504, :]
+    else:
+        total[:8, :] = so_far[:8, :] + even[:8, :]
+        total[8:, :] = so_far[8:, :] + even[8:, :] + odd[:504, :]
 
 
 def first_kernel(own, padded, total, band, rows):
-    total[...] = jnp.zeros_like(total)
-    add_products((0,), (own,), padded, band, rows, total)
+    add_products(0, own, padded, band, rows, None, total)
 
 
 def middle_kernel(offset, response, padded, so_far, total, band, rows):
-    total[...] = so_far[...]
-    add_products((offset,), (response,), padded, band, rows, total)
+    add_products(offset, response, padded, band, rows, so_far, total)
 
 
 def last_kernel(before, padded, so_far, out, band, rows, total, placed):
-    total[...] = so_far[...]
-    add_products((1,), (before,), padded, band, rows, total)
-    turned = total[...].T
+    add_products(1, before, padded, band, rows, so_far, total)
+    turned = total[...].astype(jnp.bfloat16).T
+    turned = turned.astype(jnp.bfloat16)
     skewed = [pltpu.roll(turned[u * 32 : u * 32 + 32, :], u, 1) for u in range(8)]
     lane = lax.broadcasted_iota(jnp.int32, (32, 512), 1)
     for r in range(8):
@@ -153,7 +155,7 @@
             mixed = jnp.where(lane % 8 == (r + u) % 8, skewed[u], mixed)
         mixed = pltpu.roll(mixed, (512 - r) % 512, 1)
         for part in range(4):
-            placed[part, pl.ds(r, 32, stride=8), :] = mixed[:, part * 128 : part * 128 + 128]
+            placed[part, pl.ds(r, 32, stride=8), :] = mixed[:, part * 128 : part * 128 + 128].astype(jnp.float32)
     for part in range(4):
         out[:, :, part * 128 : part * 128 + 128] = placed[part].reshape(32, 8, 128).astype(jnp.bfloat16)
 
@@ -204,11 +206,9 @@
         (traces, swap(traces), held),
         [((2, 4, 128, 128), f32), ((2, 512, 128), f32)],
     )
-    held = call(join, (2, 64, 128), bf16, (held, spread(held, "rcv", along_z(lambda z: z + sign(z)))), [], JOIN_COST)
-    arrived = [
-        spread(held, "rcv", along_z(lambda z, hops=hops: z - hops * sign(z))) for hops in (3, 2, 1)
-    ]
-    held = call(join, (8, 64, 128), bf16, (held, *arrived), [], JOIN_COST)
+    for step in (lambda z: z + sign(z), lambda z: z - 2 * sign(z), lambda z: z - sign(z)):
+        arrived = spread(held, "rcv", along_z(step))
+        held = call(join, (2 * held.shape[0], 64, 128), bf16, (held, arrived), [], JOIN_COST)
     before, after, across = [spread(held, "rcv", along_y(offset)) for offset in (1, 3, 2)]
 
     near = spread(both, "shot", along_x)

time: 32.8 us -> 36.7 us (1.12)
  starting transfers between devices: 21.6 us -> 25.8 us
  local copies, waits for them, and re-layouts: 1.66 us -> 0.76 us
  waiting for transfers between devices: 3.33 us -> 4.16 us
    ppermute x11 -> x10, starting transfers between devices: 21.6 us -> 25.8 us  [spread(): return lax.ppermute(value, axis, [(i, partner(i)) for i in range(size)])]
    unnamed x4, local copies, waits for them, and re-layouts: 1.66 us -> 0.76 us
    ppermute x11 -> x10, waiting for transfers between devices: 3.33 us -> 4.16 us  [spread(): return lax.ppermute(value, axis, [(i, partner(i)) for i in range(size)])]
    pallas_call x9 -> x10, Pallas kernels: 5.99 us -> 5.84 us  [call(): pl.pallas_call(body, out_shape=jax.ShapeDtypeStruct(shape, dtype), in_spe...]
  transfers between devices with their start and end apart: 11 -> 10, of which waited for: 3 -> 4; matrix products, arithmetic and copies ran while one was open for 0% -> 0% of each run, Pallas kernels for 12% -> 10%
where the time goes in v9:
time: 36.7 us; the launch traced here: 36.6 us
  starting transfers between devices  25.8 us (70%)
  Pallas kernels  5.84 us (16%)
  waiting for transfers between devices  4.16 us (11%)
  local copies, waits for them, and re-layouts  0.76 us (2%)
    ppermute x10, starting transfers between devices, spread(): return lax.ppermute(value, axis, [(i, partner(i)) for i in range(size)])  25.8 us
    pallas_call x10, Pallas kernels, call(): pl.pallas_call(body, out_shape=jax.ShapeDtypeStruct(shape, dtype), in_spe...  5.84 us
    ppermute x10, waiting for transfers between devices, spread(): return lax.ppermute(value, axis, [(i, partner(i)) for i in range(size)])  4.16 us
    unnamed x4, local copies, waits for them, and re-layouts  0.76 us
  transfers between devices with their start and end apart: 10, of which 4 were waited for; matrix products, arithmetic and copies ran while one was open for 0% of the time, Pallas kernels for 10%

profile of v9, /device:TPU:1, one launch (start us, length us, event | category | flops | bytes accessed | tf_op | source)
XLA Modules:
  0.0 36.6 jit_solution(4485841982911410064)
XLA Ops:
  0.0 0.0 copy-start.1
  0.0 0.8 %copy-done.1 = bf16[32,4,64]{2,1,0:T(4,128)(2,1)S(1)} copy-done((bf16[32,4,64]{2,1,0:T(4,128)(2,1)S(1)}, bf16[32,4,64]{2,1,0:T(4,128)(2,1)}, u32[]{:S(2)}) %copy-start.1) | copy-done | bytes 16408
  0.8 0.2 shard_map.28
  1.0 0.0 copy-start
  1.0 2.5 %collective-permute-start = (bf16[1,64,128]{2,1,0:T(8,128)(2,1)S(1)}, bf16[1,64,128]{2,1,0:T(8,128)(2,1)S(1)}, u32[]{:S(2)}, u32[]{:S(2)}) collective-permute-start(bf16[1,64,128]{2,1,0:T(8,128)(2,1)S(1)} %bitcast.2), channel_id=1, source_target_pairs={{0,1},{1,0},{2,3},{3,2},{4,5},{5,4},{6,7},{7,6},{8,9},{9,8},{10,11... | collective-permute-start | bytes 49160 | tf_op jit(solution)/shard_map/ppermute | solution.py:18
  3.5 1.0 %collective-permute-start.4 = (bf16[16,8,512]{2,1,0:T(8,128)(2,1)}, bf16[16,8,512]{2,1,0:T(8,128)(2,1)S(1)}, u32[]{:S(2)}, u32[]{:S(2)}) collective-permute-start(bf16[16,8,512]{2,1,0:T(8,128)(2,1)} %own.1), channel_id=1, source_target_pairs={{0,32},{32,0},{64,96},{96,64},{128,160},{160,128},{192,224},{224,1... | collective-permute-start | bytes 393224 | tf_op jit(solution)/shard_map/ppermute | solution.py:18
  4.5 0.2 collective-permute-done.blocks_1_
  4.6 5.8 %collective-permute-start.1 = (bf16[2,64,128]{2,1,0:T(8,128)(2,1)S(1)}, bf16[2,64,128]{2,1,0:T(8,128)(2,1)S(1)}, u32[]{:S(2)}, u32[]{:S(2)}) collective-permute-start(bf16[2,64,128]{2,1,0:T(8,128)(2,1)S(1)} %shard_map.29.blocks_0_), channel_id=1, source_target_pairs={{0,6},{1,3},{2,0},{3,5},{4,2},{5,7},{6,4},{7,1},{8,14},{9,11},{10,... | collective-permute-start | bytes 98312 | tf_op jit(solution)/shard_map/ppermute | solution.py:18
  10.5 0.0 collective-permute-done.4.other
  10.5 0.0 copy-done
  10.5 0.7 %shard_map.32.own = bf16[2,512,128]{2,1,0:T(8,128)(2,1)S(1)} custom-call(bf16[16,8,512]{2,1,0:T(8,128)(2,1)S(1)} %copy-done, bf16[16,8,512]{2,1,0:T(8,128)(2,1)S(1)} %collective-permute-done.4.other, bf16[1,64,128]{2,1,0:T(8,128)(2,1)S(1)} %bitcast.4), custom_call_target="tpu_custom_call" | custom-call | bytes 1048576 | tf_op jit(solution)/shard_map/pallas_call | solution.py:164
  11.2 2.6 %collective-permute-start.5 = (bf16[2,512,128]{2,1,0:T(8,128)(2,1)S(1)}, bf16[2,512,128]{2,1,0:T(8,128)(2,1)S(1)}, u32[]{:S(2)}, u32[]{:S(2)}) collective-permute-start(bf16[2,512,128]{2,1,0:T(8,128)(2,1)S(1)} %shard_map.32.own), channel_id=1, source_target_pairs={{0,64},{32,224},{64,128},{96,32},{128,192},{160,96},{192,0},{224,1... | collective-permute-start | bytes 786440 | tf_op jit(solution)/shard_map/ppermute | solution.py:18
  13.7 0.0 collective-permute-done.1.blocks_1_
  13.7 0.1 collective-permute-start.2
  13.8 2.6 %collective-permute-start.7 = (bf16[2,512,128]{2,1,0:T(8,128)(2,1)S(1)}, bf16[2,512,128]{2,1,0:T(8,128)(2,1)S(1)}, u32[]{:S(2)}, u32[]{:S(2)}) collective-permute-start(bf16[2,512,128]{2,1,0:T(8,128)(2,1)S(1)} %shard_map.32.own), channel_id=1, source_target_pairs={{0,128},{32,160},{64,192},{96,224},{128,0},{160,32},{192,64},{224,... | collective-permute-start | bytes 786440 | tf_op jit(solution)/shard_map/ppermute | solution.py:18
  16.5 0.6 %collective-permute-done.5.near = bf16[2,512,128]{2,1,0:T(8,128)(2,1)S(1)} collective-permute-done((bf16[2,512,128]{2,1,0:T(8,128)(2,1)S(1)}, bf16[2,512,128]{2,1,0:T(8,128)(2,1)S(1)}, u32[]{:S(2)}, u32[]{:S(2)}) %collective-permute-start.5) | collective-permute-done | bytes 262176 | tf_op jit(solution)/shard_map/ppermute | solution.py:18
  17.0 6.7 %collective-permute-start.6 = (bf16[2,512,128]{2,1,0:T(8,128)(2,1)S(1)}, bf16[2,512,128]{2,1,0:T(8,128)(2,1)S(1)}, u32[]{:S(2)}, u32[]{:S(2)}) collective-permute-start(bf16[2,512,128]{2,1,0:T(8,128)(2,1)S(1)} %collective-permute-done.5.near), channel_id=1, source_target_pairs={{0,32},{32,0},{64,96},{96,64},{128,160},{160,128},{192,224},{224,1... | collective-permute-start | bytes 786440 | tf_op jit(solution)/shard_map/ppermute | solution.py:18
  23.7 0.0 collective-permute-done.2.blocks_1_
  23.8 3.0 %collective-permute-start.9 = (bf16[8,64,128]{2,1,0:T(8,128)(2,1)S(1)}, bf16[8,64,128]{2,1,0:T(8,128)(2,1)S(1)}, u32[]{:S(2)}, u32[]{:S(2)}) collective-permute-start(bf16[8,64,128]{2,1,0:T(8,128)(2,1)S(1)} %shard_map.31.own), channel_id=1, source_target_pairs={{0,16},{1,17},{2,18},{3,19},{4,20},{5,21},{6,22},{7,23},{8,24},{9,... | collective-permute-start | bytes 393224 | tf_op jit(solution)/shard_map/ppermute | solution.py:18
  26.8 0.8 %collective-permute-start.8 = (bf16[8,64,128]{2,1,0:T(8,128)(2,1)S(1)}, bf16[8,64,128]{2,1,0:T(8,128)(2,1)S(1)}, u32[]{:S(2)}, u32[]{:S(2)}) collective-permute-start(bf16[8,64,128]{2,1,0:T(8,128)(2,1)S(1)} %shard_map.31.own), channel_id=1, source_target_pairs={{0,24},{1,25},{2,26},{3,27},{4,28},{5,29},{6,30},{7,31},{8,0},{9,1... | collective-permute-start | bytes 393224 | tf_op jit(solution)/shard_map/ppermute | solution.py:18
  27.5 0.7 %collective-permute-start.3 = (bf16[8,64,128]{2,1,0:T(8,128)(2,1)S(1)}, bf16[8,64,128]{2,1,0:T(8,128)(2,1)S(1)}, u32[]{:S(2)}, u32[]{:S(2)}) collective-permute-start(bf16[8,64,128]{2,1,0:T(8,128)(2,1)S(1)} %shard_map.31.own), channel_id=1, source_target_pairs={{0,8},{1,9},{2,10},{3,11},{4,12},{5,13},{6,14},{7,15},{8,16},{9,17... | collective-permute-start | bytes 393224 | tf_op jit(solution)/shard_map/ppermute | solution.py:18
  28.2 0.0 collective-permute-done.7.far
  28.2 0.0 collective-permute-done.6.near_swapped
  28.2 0.1 shard_map.33.padded
  28.4 1.0 %shard_map.34.so_far = f32[512,256]{1,0:T(8,128)S(1)} custom-call(bf16[8,64,128]{2,1,0:T(8,128)(2,1)S(1)} %shard_map.31.own, bf16[8,576,128]{2,1,0:T(8,128)(2,1)S(1)} %shard_map.33.padded), custom_call_target="tpu_custom_call" | custom-call | flops 603979776 | bytes 1048576 | tf_op jit(solution)/shard_map/pallas_call | solution.py:164
  29.3 1.1 %collective-permute-done.9.response = bf16[8,64,128]{2,1,0:T(8,128)(2,1)S(1)} collective-permute-done((bf16[8,64,128]{2,1,0:T(8,128)(2,1)S(1)}, bf16[8,64,128]{2,1,0:T(8,128)(2,1)S(1)}, u32[]{:S(2)}, u32[]{:S(2)}) %collective-permute-start.9) | collective-permute-done | bytes 131104 | tf_op jit(solution)/shard_map/ppermute | solution.py:18
  30.5 0.9 %shard_map.35.so_far = f32[512,256]{1,0:T(8,128)S(1)} custom-call(bf16[8,64,128]{2,1,0:T(8,128)(2,1)S(1)} %collective-permute-done.9.response, bf16[8,576,128]{2,1,0:T(8,128)(2,1)S(1)} %shard_map.33.padded, f32[512,256]{1,0:T(8,128)S(1)} %shard_map.34.so_far), custom_call_target="tpu_custom_call" | custom-call | flops 603979776 | bytes 1048576 | tf_op jit(solution)/shard_map/pallas_call | solution.py:164
  31.4 2.2 %collective-permute-done.8.response = bf16[8,64,128]{2,1,0:T(8,128)(2,1)S(1)} collective-permute-done((bf16[8,64,128]{2,1,0:T(8,128)(2,1)S(1)}, bf16[8,64,128]{2,1,0:T(8,128)(2,1)S(1)}, u32[]{:S(2)}, u32[]{:S(2)}) %collective-permute-start.8) | collective-permute-done | bytes 131104 | tf_op jit(solution)/shard_map/ppermute | solution.py:18
  33.7 0.9 %shard_map.36.so_far = f32[512,256]{1,0:T(8,128)S(1)} custom-call(bf16[8,64,128]{2,1,0:T(8,128)(2,1)S(1)} %collective-permute-done.8.response, bf16[8,576,128]{2,1,0:T(8,128)(2,1)S(1)} %shard_map.33.padded, f32[512,256]{1,0:T(8,128)S(1)} %shard_map.35.so_far), custom_call_target="tpu_custom_call" | custom-call | flops 603979776 | bytes 1048576 | tf_op jit(solution)/shard_map/pallas_call | solution.py:164
  34.6 0.0 collective-permute-done.3.before
  34.6 2.0 %shard_map.37 = bf16[32,8,512]{2,1,0:T(8,128)(2,1)} custom-call(bf16[8,64,128]{2,1,0:T(8,128)(2,1)S(1)} %collective-permute-done.3.before, bf16[8,576,128]{2,1,0:T(8,128)(2,1)S(1)} %shard_map.33.padded, f32[512,256]{1,0:T(8,128)S(1)} %shard_map.36.so_far), custom_call_target="tpu_custom_call" | custom-call | flops 603979776 | bytes 1048576 | tf_op jit(solution)/shard_map/pallas_call | solution.py:164
  (3 shorter events, 0.0 us)
Async XLA Ops:
  0.0 0.8 %copy-start.1 = (bf16[32,4,64]{2,1,0:T(4,128)(2,1)S(1)}, bf16[32,4,64]{2,1,0:T(4,128)(2,1)}, u32[]{:S(2)}) copy-start(bf16[32,4,64]{2,1,0:T(4,128)(2,1)} %param.2) | copy-start | bytes 49156
  1.0 9.5 %copy-start = (bf16[16,8,512]{2,1,0:T(8,128)(2,1)S(1)}, bf16[16,8,512]{2,1,0:T(8,128)(2,1)}, u32[]{:S(2)}) copy-start(bf16[16,8,512]{2,1,0:T(8,128)(2,1)} %own.1) | copy-start | bytes 393220
  1.0 3.7 %collective-permute-start = (bf16[1,64,128]{2,1,0:T(8,128)(2,1)S(1)}, bf16[1,64,128]{2,1,0:T(8,128)(2,1)S(1)}, u32[]{:S(2)}, u32[]{:S(2)}) collective-permute-start(bf16[1,64,128]{2,1,0:T(8,128)(2,1)S(1)} %bitcast.2), channel_id=1, source_target_pairs={{0,1},{1,0},{2,3},{3,2},{4,5},{5,4},{6,7},{7,6},{8,9},{9,8},{10,11... | collective-permute-start | bytes 49160 | tf_op jit(solution)/shard_map/ppermute | solution.py:18
  3.5 7.0 %collective-permute-start.4 = (bf16[16,8,512]{2,1,0:T(8,128)(2,1)}, bf16[16,8,512]{2,1,0:T(8,128)(2,1)S(1)}, u32[]{:S(2)}, u32[]{:S(2)}) collective-permute-start(bf16[16,8,512]{2,1,0:T(8,128)(2,1)} %own.1), channel_id=1, source_target_pairs={{0,32},{32,0},{64,96},{96,64},{128,160},{160,128},{192,224},{224,1... | collective-permute-start | bytes 393224 | tf_op jit(solution)/shard_map/ppermute | solution.py:18
  4.6 9.1 %collective-permute-start.1 = (bf16[2,64,128]{2,1,0:T(8,128)(2,1)S(1)}, bf16[2,64,128]{2,1,0:T(8,128)(2,1)S(1)}, u32[]{:S(2)}, u32[]{:S(2)}) collective-permute-start(bf16[2,64,128]{2,1,0:T(8,128)(2,1)S(1)} %shard_map.29.blocks_0_), channel_id=1, source_target_pairs={{0,6},{1,3},{2,0},{3,5},{4,2},{5,7},{6,4},{7,1},{8,14},{9,11},{10,... | collective-permute-start | bytes 98312 | tf_op jit(solution)/shard_map/ppermute | solution.py:18
  11.2 5.9 %collective-permute-start.5 = (bf16[2,512,128]{2,1,0:T(8,128)(2,1)S(1)}, bf16[2,512,128]{2,1,0:T(8,128)(2,1)S(1)}, u32[]{:S(2)}, u32[]{:S(2)}) collective-permute-start(bf16[2,512,128]{2,1,0:T(8,128)(2,1)S(1)} %shard_map.32.own), channel_id=1, source_target_pairs={{0,64},{32,224},{64,128},{96,32},{128,192},{160,96},{192,0},{224,1... | collective-permute-start | bytes 786440 | tf_op jit(solution)/shard_map/ppermute | solution.py:18
  13.7 10.0 %collective-permute-start.2 = (bf16[4,64,128]{2,1,0:T(8,128)(2,1)S(1)}, bf16[4,64,128]{2,1,0:T(8,128)(2,1)S(1)}, u32[]{:S(2)}, u32[]{:S(2)}) collective-permute-start(bf16[4,64,128]{2,1,0:T(8,128)(2,1)S(1)} %shard_map.30.blocks_0_), channel_id=1, source_target_pairs={{0,7},{1,2},{2,1},{3,4},{4,3},{5,6},{6,5},{7,0},{8,15},{9,10},{10,... | collective-permute-start | bytes 196616 | tf_op jit(solution)/shard_map/ppermute | solution.py:18
  13.8 14.4 %collective-permute-start.7 = (bf16[2,512,128]{2,1,0:T(8,128)(2,1)S(1)}, bf16[2,512,128]{2,1,0:T(8,128)(2,1)S(1)}, u32[]{:S(2)}, u32[]{:S(2)}) collective-permute-start(bf16[2,512,128]{2,1,0:T(8,128)(2,1)S(1)} %shard_map.32.own), channel_id=1, source_target_pairs={{0,128},{32,160},{64,192},{96,224},{128,0},{160,32},{192,64},{224,... | collective-permute-start | bytes 786440 | tf_op jit(solution)/shard_map/ppermute | solution.py:18
  17.0 11.2 %collective-permute-start.6 = (bf16[2,512,128]{2,1,0:T(8,128)(2,1)S(1)}, bf16[2,512,128]{2,1,0:T(8,128)(2,1)S(1)}, u32[]{:S(2)}, u32[]{:S(2)}) collective-permute-start(bf16[2,512,128]{2,1,0:T(8,128)(2,1)S(1)} %collective-permute-done.5.near), channel_id=1, source_target_pairs={{0,32},{32,0},{64,96},{96,64},{128,160},{160,128},{192,224},{224,1... | collective-permute-start | bytes 786440 | tf_op jit(solution)/shard_map/ppermute | solution.py:18
  23.8 6.7 %collective-permute-start.9 = (bf16[8,64,128]{2,1,0:T(8,128)(2,1)S(1)}, bf16[8,64,128]{2,1,0:T(8,128)(2,1)S(1)}, u32[]{:S(2)}, u32[]{:S(2)}) collective-permute-start(bf16[8,64,128]{2,1,0:T(8,128)(2,1)S(1)} %shard_map.31.own), channel_id=1, source_target_pairs={{0,16},{1,17},{2,18},{3,19},{4,20},{5,21},{6,22},{7,23},{8,24},{9,... | collective-permute-start | bytes 393224 | tf_op jit(solution)/shard_map/ppermute | solution.py:18
  26.8 6.9 %collective-permute-start.8 = (bf16[8,64,128]{2,1,0:T(8,128)(2,1)S(1)}, bf16[8,64,128]{2,1,0:T(8,128)(2,1)S(1)}, u32[]{:S(2)}, u32[]{:S(2)}) collective-permute-start(bf16[8,64,128]{2,1,0:T(8,128)(2,1)S(1)} %shard_map.31.own), channel_id=1, source_target_pairs={{0,24},{1,25},{2,26},{3,27},{4,28},{5,29},{6,30},{7,31},{8,0},{9,1... | collective-permute-start | bytes 393224 | tf_op jit(solution)/shard_map/ppermute | solution.py:18
  27.5 7.1 %collective-permute-start.3 = (bf16[8,64,128]{2,1,0:T(8,128)(2,1)S(1)}, bf16[8,64,128]{2,1,0:T(8,128)(2,1)S(1)}, u32[]{:S(2)}, u32[]{:S(2)}) collective-permute-start(bf16[8,64,128]{2,1,0:T(8,128)(2,1)S(1)} %shard_map.31.own), channel_id=1, source_target_pairs={{0,8},{1,9},{2,10},{3,11},{4,12},{5,13},{6,14},{7,15},{8,16},{9,17... | collective-permute-start | bytes 393224 | tf_op jit(solution)/shard_map/ppermute | solution.py:18

commit v10 on v9

--- a/solution.py
+++ b/solution.py
@@ -7,7 +7,7 @@
 from jax.experimental.pallas import tpu as pltpu
 from jax.sharding import PartitionSpec as P
 
-RING8 = (0, 1, 2, 3, 7, 6, 5, 4)
+RING8 = (0, 1, 5, 4, 2, 3, 7, 6)
 VMEM = pl.BlockSpec(memory_space=pltpu.VMEM)
 JOIN_COST = 2**33
 PARAMS = pltpu.CompilerParams(vmem_limit_bytes=40 * 2**20)
@@ -22,21 +22,23 @@
     return 1 - 2 * (coordinate % 2)
 
 
-def prepare_response(response, out, rows, turned):
-    wide = response[...].astype(jnp.float32)
-    rows[...] = jnp.concatenate([wide, jnp.zeros((128, 64), jnp.float32)], axis=1)
-    by_position = jnp.concatenate([rows[pl.ds(k, 32, stride=4), :] for k in range(4)], axis=0)
-    turned[...] = by_position.T[:64, :]
-    skewed = [pltpu.roll(turned[pl.ds(u, 16, stride=4), :], 32 * u, 1) for u in range(4)]
+def prepare_responses(own, neighbour, out, rows, turned):
     lane_block = lax.broadcasted_iota(jnp.int32, (16, 128), 1) // 32
-    for k in range(4):
-        mixed = skewed[0]
-        for u in range(1, 4):
-            mixed = jnp.where(lane_block == (k + u) % 4, skewed[u], mixed)
-        out[k * 16 : k * 16 + 16, :] = pltpu.roll(mixed, (128 - 32 * k) % 128, 1).astype(jnp.bfloat16)
-
-
-def prepare_traces(own, other, _, out, rows, turned):
+    for side, response in enumerate((own, neighbour)):
+        wide = response[...].astype(jnp.float32)
+        rows[side] = jnp.concatenate([wide, jnp.zeros((128, 64), jnp.float32)], axis=1)
+        by_position = [rows[side, pl.ds(k, 32, stride=4), :] for k in range(4)]
+        turned[side] = jnp.concatenate(by_position, axis=0).T[:64, :]
+        skewed = [pltpu.roll(turned[side, pl.ds(u, 16, stride=4), :], 32 * u, 1) for u in range(4)]
+        for k in range(4):
+            mixed = skewed[0]
+            for u in range(1, 4):
+                mixed = jnp.where(lane_block == (k + u) % 4, skewed[u], mixed)
+            mixed = pltpu.roll(mixed, (128 - 32 * k) % 128, 1)
+            out[side, k * 16 : k * 16 + 16, :] = mixed.astype(jnp.bfloat16)
+
+
+def prepare_traces(own, other, out, rows, turned):
     lane_block = lax.broadcasted_iota(jnp.int32, (64, 128), 1) // 16
     for side, traces in enumerate((own, other)):
         for part in range(4):
@@ -191,24 +193,26 @@
     def swap(value):
         return spread(value, "shot", lambda i: i ^ 1)
 
+    response = response.reshape(128, 64)
     held = call(
-        prepare_response,
-        (64, 128),
+        prepare_responses,
+        (2, 64, 128),
         bf16,
-        (response.reshape(128, 64),),
-        [((128, 128), f32), ((64, 128), f32)],
-    )
-    held = held[None]
+        (spread(response, "shot", lambda i: i), spread(response, "rcv", along_z(lambda z: z + sign(z)))),
+        [((2, 128, 128), f32), ((2, 64, 128), f32)],
+        JOIN_COST,
+    )
     both = call(
         prepare_traces,
         (2, 512, 128),
         bf16,
-        (traces, swap(traces), held),
+        (spread(traces, "shot", lambda i: i), swap(traces)),
         [((2, 4, 128, 128), f32), ((2, 512, 128), f32)],
     )
-    for step in (lambda z: z + sign(z), lambda z: z - 2 * sign(z), lambda z: z - sign(z)):
-        arrived = spread(held, "rcv", along_z(step))
-        held = call(join, (2 * held.shape[0], 64, 128), bf16, (held, arrived), [], JOIN_COST)
+    arrived = [
+        spread(held, "rcv", along_z(lambda z, hops=hops: z - hops * sign(z))) for hops in (3, 2, 1)
+    ]
+    held = call(join, (8, 64, 128), bf16, (held, *arrived), [], JOIN_COST)
     before, after, across = [spread(held, "rcv", along_y(offset)) for offset in (1, 3, 2)]
 
     near = spread(both, "shot", along_x)

time: 36.7 us -> 34.1 us (0.929)
  starting transfers between devices: 25.8 us -> 24.2 us
  local copies, waits for them, and re-layouts: 0.76 us -> 0 us
    ppermute x10 -> x13, starting transfers between devices: 25.8 us -> 24.2 us  [spread(): return lax.ppermute(value, axis, [(i, partner(i)) for i in range(size)])]
    unnamed x4 -> x0, local copies, waits for them, and re-layouts: 0.76 us -> none
    ppermute x10 -> x13, waiting for transfers between devices: 4.16 us -> 3.83 us  [spread(): return lax.ppermute(value, axis, [(i, partner(i)) for i in range(size)])]
    pallas_call x10 -> x8, Pallas kernels: 5.84 us -> 5.86 us  [call(): pl.pallas_call(body, out_shape=jax.ShapeDtypeStruct(shape, dtype), in_spe...]
  transfers between devices with their start and end apart: 10 -> 13, of which waited for: 4 -> 3; matrix products, arithmetic and copies ran while one was open for 0% -> 0% of each run, Pallas kernels for 10% -> 11%
where the time goes in v10:
time: 34.1 us; the launch traced here: 34 us
  starting transfers between devices  24.2 us (71%)
  Pallas kernels  5.86 us (17%)
  waiting for transfers between devices  3.83 us (11%)
    ppermute x13, starting transfers between devices, spread(): return lax.ppermute(value, axis, [(i, partner(i)) for i in range(size)])  24.2 us
    pallas_call x8, Pallas kernels, call(): pl.pallas_call(body, out_shape=jax.ShapeDtypeStruct(shape, dtype), in_spe...  5.86 us
    ppermute x13, waiting for transfers between devices, spread(): return lax.ppermute(value, axis, [(i, partner(i)) for i in range(size)])  3.83 us
  transfers between devices with their start and end apart: 13, of which 3 were waited for; matrix products, arithmetic and copies ran while one was open for 0% of the time, Pallas kernels for 11%

profile of v10, /device:TPU:1, one launch (start us, length us, event | category | flops | bytes accessed | tf_op | source)
XLA Modules:
  0.0 34.0 jit_solution(2350983127533487139)
XLA Ops:
  0.0 0.9 %collective-permute-start.6 = (bf16[16,8,512]{2,1,0:T(8,128)(2,1)}, bf16[16,8,512]{2,1,0:T(8,128)(2,1)S(1)}, u32[]{:S(2)}, u32[]{:S(2)}) collective-permute-start(bf16[16,8,512]{2,1,0:T(8,128)(2,1)} %param.3), channel_id=1, source_target_pairs={{0,0},{32,32},{64,64},{96,96},{128,128},{160,160},{192,192},{224,2... | collective-permute-start | bytes 393224 | tf_op jit(solution)/shard_map/ppermute | solution.py:18
  0.9 3.2 %collective-permute-start.7 = (bf16[16,8,512]{2,1,0:T(8,128)(2,1)}, bf16[16,8,512]{2,1,0:T(8,128)(2,1)S(1)}, u32[]{:S(2)}, u32[]{:S(2)}) collective-permute-start(bf16[16,8,512]{2,1,0:T(8,128)(2,1)} %param.3), channel_id=1, source_target_pairs={{0,32},{32,0},{64,96},{96,64},{128,160},{160,128},{192,224},{224,1... | collective-permute-start | bytes 393224 | tf_op jit(solution)/shard_map/ppermute | solution.py:18
  4.1 0.8 %collective-permute-start = (bf16[128,64]{1,0:T(8,128)(2,1)}, bf16[128,64]{1,0:T(8,128)(2,1)S(1)}, u32[]{:S(2)}, u32[]{:S(2)}) collective-permute-start(bf16[128,64]{1,0:T(8,128)(2,1)} %bitcast.1), channel_id=1, source_target_pairs={{0,0},{32,32},{64,64},{96,96},{128,128},{160,160},{192,192},{224,2... | collective-permute-start | bytes 49160 | tf_op jit(solution)/shard_map/ppermute | solution.py:18
  4.9 0.0 collective-permute-start.1
  4.9 0.0 collective-permute-done.6.own
  4.9 0.4 %collective-permute-done.7.other = bf16[16,8,512]{2,1,0:T(8,128)(2,1)S(1)} collective-permute-done((bf16[16,8,512]{2,1,0:T(8,128)(2,1)}, bf16[16,8,512]{2,1,0:T(8,128)(2,1)S(1)}, u32[]{:S(2)}, u32[]{:S(2)}) %collective-permute-start.7) | collective-permute-done | bytes 131104 | tf_op jit(solution)/shard_map/ppermute | solution.py:18
  5.3 0.7 %shard_map.30.own = bf16[2,512,128]{2,1,0:T(8,128)(2,1)S(1)} custom-call(bf16[16,8,512]{2,1,0:T(8,128)(2,1)S(1)} %collective-permute-done.6.own, bf16[16,8,512]{2,1,0:T(8,128)(2,1)S(1)} %collective-permute-done.7.other), custom_call_target="tpu_custom_call" | custom-call | bytes 1048576 | tf_op jit(solution)/shard_map/pallas_call | solution.py:166
  6.0 2.0 %collective-permute-start.8 = (bf16[2,512,128]{2,1,0:T(8,128)(2,1)S(1)}, bf16[2,512,128]{2,1,0:T(8,128)(2,1)S(1)}, u32[]{:S(2)}, u32[]{:S(2)}) collective-permute-start(bf16[2,512,128]{2,1,0:T(8,128)(2,1)S(1)} %shard_map.30.own), channel_id=1, source_target_pairs={{0,64},{32,224},{64,128},{96,32},{128,192},{160,96},{192,0},{224,1... | collective-permute-start | bytes 786440 | tf_op jit(solution)/shard_map/ppermute | solution.py:18
  8.0 0.0 collective-permute-done.own
  8.1 0.0 collective-permute-done.1.neighbour
  8.1 0.3 shard_map.28.blocks_0_
  8.3 5.6 %collective-permute-start.2 = (bf16[2,64,128]{2,1,0:T(8,128)(2,1)S(1)}, bf16[2,64,128]{2,1,0:T(8,128)(2,1)S(1)}, u32[]{:S(2)}, u32[]{:S(2)}) collective-permute-start(bf16[2,64,128]{2,1,0:T(8,128)(2,1)S(1)} %shard_map.28.blocks_0_), channel_id=1, source_target_pairs={{0,5},{1,4},{2,7},{3,6},{4,1},{5,0},{6,3},{7,2},{8,13},{9,12},{10,... | collective-permute-start | bytes 98312 | tf_op jit(solution)/shard_map/ppermute | solution.py:18
  14.0 0.0 collective-permute-start.3
  14.0 3.1 %collective-permute-start.4 = (bf16[2,64,128]{2,1,0:T(8,128)(2,1)S(1)}, bf16[2,64,128]{2,1,0:T(8,128)(2,1)S(1)}, u32[]{:S(2)}, u32[]{:S(2)}) collective-permute-start(bf16[2,64,128]{2,1,0:T(8,128)(2,1)S(1)} %shard_map.28.blocks_0_), channel_id=1, source_target_pairs={{0,7},{1,2},{2,1},{3,4},{4,3},{5,6},{6,5},{7,0},{8,15},{9,10},{10,... | collective-permute-start | bytes 98312 | tf_op jit(solution)/shard_map/ppermute | solution.py:18
  17.1 1.7 %collective-permute-start.10 = (bf16[2,512,128]{2,1,0:T(8,128)(2,1)S(1)}, bf16[2,512,128]{2,1,0:T(8,128)(2,1)S(1)}, u32[]{:S(2)}, u32[]{:S(2)}) collective-permute-start(bf16[2,512,128]{2,1,0:T(8,128)(2,1)S(1)} %shard_map.30.own), channel_id=1, source_target_pairs={{0,128},{32,160},{64,192},{96,224},{128,0},{160,32},{192,64},{224,... | collective-permute-start | bytes 786440 | tf_op jit(solution)/shard_map/ppermute | solution.py:18
  18.8 0.0 collective-permute-done.8.near
  18.8 2.3 %collective-permute-start.9 = (bf16[2,512,128]{2,1,0:T(8,128)(2,1)S(1)}, bf16[2,512,128]{2,1,0:T(8,128)(2,1)S(1)}, u32[]{:S(2)}, u32[]{:S(2)}) collective-permute-start(bf16[2,512,128]{2,1,0:T(8,128)(2,1)S(1)} %collective-permute-done.8.near), channel_id=1, source_target_pairs={{0,32},{32,0},{64,96},{96,64},{128,160},{160,128},{192,224},{224,1... | collective-permute-start | bytes 786440 | tf_op jit(solution)/shard_map/ppermute | solution.py:18
  21.1 0.0 collective-permute-done.2.blocks_1_
  21.1 0.0 collective-permute-done.3.blocks_2_
  21.1 0.0 collective-permute-done.4.blocks_3_
  21.1 3.0 %collective-permute-start.12 = (bf16[8,64,128]{2,1,0:T(8,128)(2,1)S(1)}, bf16[8,64,128]{2,1,0:T(8,128)(2,1)S(1)}, u32[]{:S(2)}, u32[]{:S(2)}) collective-permute-start(bf16[8,64,128]{2,1,0:T(8,128)(2,1)S(1)} %shard_map.29.own), channel_id=1, source_target_pairs={{0,16},{1,17},{2,18},{3,19},{4,20},{5,21},{6,22},{7,23},{8,24},{9,... | collective-permute-start | bytes 393224 | tf_op jit(solution)/shard_map/ppermute | solution.py:18
  24.1 0.8 %collective-permute-start.11 = (bf16[8,64,128]{2,1,0:T(8,128)(2,1)S(1)}, bf16[8,64,128]{2,1,0:T(8,128)(2,1)S(1)}, u32[]{:S(2)}, u32[]{:S(2)}) collective-permute-start(bf16[8,64,128]{2,1,0:T(8,128)(2,1)S(1)} %shard_map.29.own), channel_id=1, source_target_pairs={{0,24},{1,25},{2,26},{3,27},{4,28},{5,29},{6,30},{7,31},{8,0},{9,1... | collective-permute-start | bytes 393224 | tf_op jit(solution)/shard_map/ppermute | solution.py:18
  24.9 0.7 %collective-permute-start.5 = (bf16[8,64,128]{2,1,0:T(8,128)(2,1)S(1)}, bf16[8,64,128]{2,1,0:T(8,128)(2,1)S(1)}, u32[]{:S(2)}, u32[]{:S(2)}) collective-permute-start(bf16[8,64,128]{2,1,0:T(8,128)(2,1)S(1)} %shard_map.29.own), channel_id=1, source_target_pairs={{0,8},{1,9},{2,10},{3,11},{4,12},{5,13},{6,14},{7,15},{8,16},{9,17... | collective-permute-start | bytes 393224 | tf_op jit(solution)/shard_map/ppermute | solution.py:18
  25.6 0.0 collective-permute-done.10.far
  25.6 0.0 collective-permute-done.9.near_swapped
  25.6 0.1 shard_map.31.padded
  25.7 1.0 %shard_map.32.so_far = f32[512,256]{1,0:T(8,128)S(1)} custom-call(bf16[8,64,128]{2,1,0:T(8,128)(2,1)S(1)} %shard_map.29.own, bf16[8,576,128]{2,1,0:T(8,128)(2,1)S(1)} %shard_map.31.padded), custom_call_target="tpu_custom_call" | custom-call | flops 603979776 | bytes 1048576 | tf_op jit(solution)/shard_map/pallas_call | solution.py:166
  26.7 1.1 %collective-permute-done.12.response = bf16[8,64,128]{2,1,0:T(8,128)(2,1)S(1)} collective-permute-done((bf16[8,64,128]{2,1,0:T(8,128)(2,1)S(1)}, bf16[8,64,128]{2,1,0:T(8,128)(2,1)S(1)}, u32[]{:S(2)}, u32[]{:S(2)}) %collective-permute-start.12) | collective-permute-done | bytes 131104 | tf_op jit(solution)/shard_map/ppermute | solution.py:18
  27.8 0.9 %shard_map.33.so_far = f32[512,256]{1,0:T(8,128)S(1)} custom-call(bf16[8,64,128]{2,1,0:T(8,128)(2,1)S(1)} %collective-permute-done.12.response, bf16[8,576,128]{2,1,0:T(8,128)(2,1)S(1)} %shard_map.31.padded, f32[512,256]{1,0:T(8,128)S(1)} %shard_map.32.so_far), custom_call_target="tpu_custom_call" | custom-call | flops 603979776 | bytes 1048576 | tf_op jit(solution)/shard_map/pallas_call | solution.py:166
  28.8 2.2 %collective-permute-done.11.response = bf16[8,64,128]{2,1,0:T(8,128)(2,1)S(1)} collective-permute-done((bf16[8,64,128]{2,1,0:T(8,128)(2,1)S(1)}, bf16[8,64,128]{2,1,0:T(8,128)(2,1)S(1)}, u32[]{:S(2)}, u32[]{:S(2)}) %collective-permute-start.11) | collective-permute-done | bytes 131104 | tf_op jit(solution)/shard_map/ppermute | solution.py:18
  31.0 0.9 %shard_map.34.so_far = f32[512,256]{1,0:T(8,128)S(1)} custom-call(bf16[8,64,128]{2,1,0:T(8,128)(2,1)S(1)} %collective-permute-done.11.response, bf16[8,576,128]{2,1,0:T(8,128)(2,1)S(1)} %shard_map.31.padded, f32[512,256]{1,0:T(8,128)S(1)} %shard_map.33.so_far), custom_call_target="tpu_custom_call" | custom-call | flops 603979776 | bytes 1048576 | tf_op jit(solution)/shard_map/pallas_call | solution.py:166
  32.0 2.0 %shard_map.35 = bf16[32,8,512]{2,1,0:T(8,128)(2,1)} custom-call(bf16[8,64,128]{2,1,0:T(8,128)(2,1)S(1)} %collective-permute-done.5.before, bf16[8,576,128]{2,1,0:T(8,128)(2,1)S(1)} %shard_map.31.padded, f32[512,256]{1,0:T(8,128)S(1)} %shard_map.34.so_far), custom_call_target="tpu_custom_call" | custom-call | flops 603979776 | bytes 1048576 | tf_op jit(solution)/shard_map/pallas_call | solution.py:166
  (2 shorter events, 0.0 us)
Async XLA Ops:
  0.0 4.9 %collective-permute-start.6 = (bf16[16,8,512]{2,1,0:T(8,128)(2,1)}, bf16[16,8,512]{2,1,0:T(8,128)(2,1)S(1)}, u32[]{:S(2)}, u32[]{:S(2)}) collective-permute-start(bf16[16,8,512]{2,1,0:T(8,128)(2,1)} %param.3), channel_id=1, source_target_pairs={{0,0},{32,32},{64,64},{96,96},{128,128},{160,160},{192,192},{224,2... | collective-permute-start | bytes 393224 | tf_op jit(solution)/shard_map/ppermute | solution.py:18
  0.9 4.4 %collective-permute-start.7 = (bf16[16,8,512]{2,1,0:T(8,128)(2,1)}, bf16[16,8,512]{2,1,0:T(8,128)(2,1)S(1)}, u32[]{:S(2)}, u32[]{:S(2)}) collective-permute-start(bf16[16,8,512]{2,1,0:T(8,128)(2,1)} %param.3), channel_id=1, source_target_pairs={{0,32},{32,0},{64,96},{96,64},{128,160},{160,128},{192,224},{224,1... | collective-permute-start | bytes 393224 | tf_op jit(solution)/shard_map/ppermute | solution.py:18
  4.1 3.9 %collective-permute-start = (bf16[128,64]{1,0:T(8,128)(2,1)}, bf16[128,64]{1,0:T(8,128)(2,1)S(1)}, u32[]{:S(2)}, u32[]{:S(2)}) collective-permute-start(bf16[128,64]{1,0:T(8,128)(2,1)} %bitcast.1), channel_id=1, source_target_pairs={{0,0},{32,32},{64,64},{96,96},{128,128},{160,160},{192,192},{224,2... | collective-permute-start | bytes 49160 | tf_op jit(solution)/shard_map/ppermute | solution.py:18
  4.9 3.1 %collective-permute-start.1 = (bf16[128,64]{1,0:T(8,128)(2,1)}, bf16[128,64]{1,0:T(8,128)(2,1)S(1)}, u32[]{:S(2)}, u32[]{:S(2)}) collective-permute-start(bf16[128,64]{1,0:T(8,128)(2,1)} %bitcast.2), channel_id=1, source_target_pairs={{0,1},{1,0},{2,3},{3,2},{4,5},{5,4},{6,7},{7,6},{8,9},{9,8},{10,11... | collective-permute-start | bytes 49160 | tf_op jit(solution)/shard_map/ppermute | solution.py:18
  6.0 12.8 %collective-permute-start.8 = (bf16[2,512,128]{2,1,0:T(8,128)(2,1)S(1)}, bf16[2,512,128]{2,1,0:T(8,128)(2,1)S(1)}, u32[]{:S(2)}, u32[]{:S(2)}) collective-permute-start(bf16[2,512,128]{2,1,0:T(8,128)(2,1)S(1)} %shard_map.30.own), channel_id=1, source_target_pairs={{0,64},{32,224},{64,128},{96,32},{128,192},{160,96},{192,0},{224,1... | collective-permute-start | bytes 786440 | tf_op jit(solution)/shard_map/ppermute | solution.py:18
  8.3 12.8 %collective-permute-start.2 = (bf16[2,64,128]{2,1,0:T(8,128)(2,1)S(1)}, bf16[2,64,128]{2,1,0:T(8,128)(2,1)S(1)}, u32[]{:S(2)}, u32[]{:S(2)}) collective-permute-start(bf16[2,64,128]{2,1,0:T(8,128)(2,1)S(1)} %shard_map.28.blocks_0_), channel_id=1, source_target_pairs={{0,5},{1,4},{2,7},{3,6},{4,1},{5,0},{6,3},{7,2},{8,13},{9,12},{10,... | collective-permute-start | bytes 98312 | tf_op jit(solution)/shard_map/ppermute | solution.py:18
  14.0 7.2 %collective-permute-start.3 = (bf16[2,64,128]{2,1,0:T(8,128)(2,1)S(1)}, bf16[2,64,128]{2,1,0:T(8,128)(2,1)S(1)}, u32[]{:S(2)}, u32[]{:S(2)}) collective-permute-start(bf16[2,64,128]{2,1,0:T(8,128)(2,1)S(1)} %shard_map.28.blocks_0_), channel_id=1, source_target_pairs={{0,6},{1,3},{2,0},{3,5},{4,2},{5,7},{6,4},{7,1},{8,14},{9,11},{10,... | collective-permute-start | bytes 98312 | tf_op jit(solution)/shard_map/ppermute | solution.py:18
  14.0 7.2 %collective-permute-start.4 = (bf16[2,64,128]{2,1,0:T(8,128)(2,1)S(1)}, bf16[2,64,128]{2,1,0:T(8,128)(2,1)S(1)}, u32[]{:S(2)}, u32[]{:S(2)}) collective-permute-start(bf16[2,64,128]{2,1,0:T(8,128)(2,1)S(1)} %shard_map.28.blocks_0_), channel_id=1, source_target_pairs={{0,7},{1,2},{2,1},{3,4},{4,3},{5,6},{6,5},{7,0},{8,15},{9,10},{10,... | collective-permute-start | bytes 98312 | tf_op jit(solution)/shard_map/ppermute | solution.py:18
  17.1 8.5 %collective-permute-start.10 = (bf16[2,512,128]{2,1,0:T(8,128)(2,1)S(1)}, bf16[2,512,128]{2,1,0:T(8,128)(2,1)S(1)}, u32[]{:S(2)}, u32[]{:S(2)}) collective-permute-start(bf16[2,512,128]{2,1,0:T(8,128)(2,1)S(1)} %shard_map.30.own), channel_id=1, source_target_pairs={{0,128},{32,160},{64,192},{96,224},{128,0},{160,32},{192,64},{224,... | collective-permute-start | bytes 786440 | tf_op jit(solution)/shard_map/ppermute | solution.py:18
  18.8 6.8 %collective-permute-start.9 = (bf16[2,512,128]{2,1,0:T(8,128)(2,1)S(1)}, bf16[2,512,128]{2,1,0:T(8,128)(2,1)S(1)}, u32[]{:S(2)}, u32[]{:S(2)}) collective-permute-start(bf16[2,512,128]{2,1,0:T(8,128)(2,1)S(1)} %collective-permute-done.8.near), channel_id=1, source_target_pairs={{0,32},{32,0},{64,96},{96,64},{128,160},{160,128},{192,224},{224,1... | collective-permute-start | bytes 786440 | tf_op jit(solution)/shard_map/ppermute | solution.py:18
  21.1 6.7 %collective-permute-start.12 = (bf16[8,64,128]{2,1,0:T(8,128)(2,1)S(1)}, bf16[8,64,128]{2,1,0:T(8,128)(2,1)S(1)}, u32[]{:S(2)}, u32[]{:S(2)}) collective-permute-start(bf16[8,64,128]{2,1,0:T(8,128)(2,1)S(1)} %shard_map.29.own), channel_id=1, source_target_pairs={{0,16},{1,17},{2,18},{3,19},{4,20},{5,21},{6,22},{7,23},{8,24},{9,... | collective-permute-start | bytes 393224 | tf_op jit(solution)/shard_map/ppermute | solution.py:18
  24.1 6.9 %collective-permute-start.11 = (bf16[8,64,128]{2,1,0:T(8,128)(2,1)S(1)}, bf16[8,64,128]{2,1,0:T(8,128)(2,1)S(1)}, u32[]{:S(2)}, u32[]{:S(2)}) collective-permute-start(bf16[8,64,128]{2,1,0:T(8,128)(2,1)S(1)} %shard_map.29.own), channel_id=1, source_target_pairs={{0,24},{1,25},{2,26},{3,27},{4,28},{5,29},{6,30},{7,31},{8,0},{9,1... | collective-permute-start | bytes 393224 | tf_op jit(solution)/shard_map/ppermute | solution.py:18
  24.9 7.1 %collective-permute-start.5 = (bf16[8,64,128]{2,1,0:T(8,128)(2,1)S(1)}, bf16[8,64,128]{2,1,0:T(8,128)(2,1)S(1)}, u32[]{:S(2)}, u32[]{:S(2)}) collective-permute-start(bf16[8,64,128]{2,1,0:T(8,128)(2,1)S(1)} %shard_map.29.own), channel_id=1, source_target_pairs={{0,8},{1,9},{2,10},{3,11},{4,12},{5,13},{6,14},{7,15},{8,16},{9,17... | collective-permute-start | bytes 393224 | tf_op jit(solution)/shard_map/ppermute | solution.py:18

commit v11 on v9

--- a/solution.py
+++ b/solution.py
@@ -7,7 +7,7 @@
 from jax.experimental.pallas import tpu as pltpu
 from jax.sharding import PartitionSpec as P
 
-RING8 = (0, 1, 2, 3, 7, 6, 5, 4)
+RING8 = (0, 1, 5, 4, 2, 3, 7, 6)
 VMEM = pl.BlockSpec(memory_space=pltpu.VMEM)
 JOIN_COST = 2**33
 PARAMS = pltpu.CompilerParams(vmem_limit_bytes=40 * 2**20)
@@ -206,9 +206,11 @@
         (traces, swap(traces), held),
         [((2, 4, 128, 128), f32), ((2, 512, 128), f32)],
     )
-    for step in (lambda z: z + sign(z), lambda z: z - 2 * sign(z), lambda z: z - sign(z)):
-        arrived = spread(held, "rcv", along_z(step))
-        held = call(join, (2 * held.shape[0], 64, 128), bf16, (held, arrived), [], JOIN_COST)
+    held = call(join, (2, 64, 128), bf16, (held, spread(held, "rcv", along_z(lambda z: z + sign(z)))), [], JOIN_COST)
+    arrived = [
+        spread(held, "rcv", along_z(lambda z, hops=hops: z - hops * sign(z))) for hops in (3, 2, 1)
+    ]
+    held = call(join, (8, 64, 128), bf16, (held, *arrived), [], JOIN_COST)
     before, after, across = [spread(held, "rcv", along_y(offset)) for offset in (1, 3, 2)]
 
     near = spread(both, "shot", along_x)

time: 36.7 us -> 32.7 us (0.89)
  starting transfers between devices: 25.8 us -> 21.6 us
  local copies, waits for them, and re-layouts: 0.76 us -> 1.66 us
  waiting for transfers between devices: 4.16 us -> 3.33 us
    ppermute x10 -> x11, starting transfers between devices: 25.8 us -> 21.6 us  [spread(): return lax.ppermute(value, axis, [(i, partner(i)) for i in range(size)])]
    unnamed x4, local copies, waits for them, and re-layouts: 0.76 us -> 1.66 us
    ppermute x10 -> x11, waiting for transfers between devices: 4.16 us -> 3.33 us  [spread(): return lax.ppermute(value, axis, [(i, partner(i)) for i in range(size)])]
    pallas_call x10 -> x9, Pallas kernels: 5.84 us -> 5.86 us  [call(): pl.pallas_call(body, out_shape=jax.ShapeDtypeStruct(shape, dtype), in_spe...]
  transfers between devices with their start and end apart: 10 -> 11, of which waited for: 4 -> 3; matrix products, arithmetic and copies ran while one was open for 0% -> 0% of each run, Pallas kernels for 10% -> 12%
where the time goes in v11:
time: 32.7 us; the launch traced here: 32.5 us
  starting transfers between devices  21.6 us (66%)
  Pallas kernels  5.86 us (18%)
  waiting for transfers between devices  3.33 us (10%)
  local copies, waits for them, and re-layouts  1.66 us (5%)
    ppermute x11, starting transfers between devices, spread(): return lax.ppermute(value, axis, [(i, partner(i)) for i in range(size)])  21.6 us
    pallas_call x9, Pallas kernels, call(): pl.pallas_call(body, out_shape=jax.ShapeDtypeStruct(shape, dtype), in_spe...  5.86 us
    ppermute x11, waiting for transfers between devices, spread(): return lax.ppermute(value, axis, [(i, partner(i)) for i in range(size)])  3.33 us
    unnamed x4, local copies, waits for them, and re-layouts  1.66 us
  transfers between devices with their start and end apart: 11, of which 3 were waited for; matrix products, arithmetic and copies ran while one was open for 0% of the time, Pallas kernels for 12%

profile of v11, /device:TPU:1, one launch (start us, length us, event | category | flops | bytes accessed | tf_op | source)
XLA Modules:
  0.0 32.5 jit_solution(17308104573303468729)
XLA Ops:
  0.0 3.2 %collective-permute-start.5 = (bf16[16,8,512]{2,1,0:T(8,128)(2,1)}, bf16[16,8,512]{2,1,0:T(8,128)(2,1)S(1)}, u32[]{:S(2)}, u32[]{:S(2)}) collective-permute-start(bf16[16,8,512]{2,1,0:T(8,128)(2,1)} %own.1), channel_id=1, source_target_pairs={{0,32},{32,0},{64,96},{96,64},{128,160},{160,128},{192,224},{224,1... | collective-permute-start | bytes 393224 | tf_op jit(solution)/shard_map/ppermute | solution.py:18
  3.2 0.8 %copy-done.1 = bf16[32,4,64]{2,1,0:T(4,128)(2,1)S(1)} copy-done((bf16[32,4,64]{2,1,0:T(4,128)(2,1)S(1)}, bf16[32,4,64]{2,1,0:T(4,128)(2,1)}, u32[]{:S(2)}) %copy-start.1) | copy-done | bytes 16408
  4.0 0.2 shard_map.28
  4.2 0.1 collective-permute-start
  4.3 0.2 collective-permute-done.5.other
  4.4 0.0 copy-start
  4.4 0.9 %copy-done = bf16[16,8,512]{2,1,0:T(8,128)(2,1)S(1)} copy-done((bf16[16,8,512]{2,1,0:T(8,128)(2,1)S(1)}, bf16[16,8,512]{2,1,0:T(8,128)(2,1)}, u32[]{:S(2)}) %copy-start) | copy-done | bytes 131096
  5.3 0.7 %shard_map.31.own = bf16[2,512,128]{2,1,0:T(8,128)(2,1)S(1)} custom-call(bf16[16,8,512]{2,1,0:T(8,128)(2,1)S(1)} %copy-done, bf16[16,8,512]{2,1,0:T(8,128)(2,1)S(1)} %collective-permute-done.5.other, bf16[1,64,128]{2,1,0:T(8,128)(2,1)S(1)} %bitcast.3), custom_call_target="tpu_custom_call" | custom-call | bytes 1048576 | tf_op jit(solution)/shard_map/pallas_call | solution.py:164
  6.0 2.3 %collective-permute-start.6 = (bf16[2,512,128]{2,1,0:T(8,128)(2,1)S(1)}, bf16[2,512,128]{2,1,0:T(8,128)(2,1)S(1)}, u32[]{:S(2)}, u32[]{:S(2)}) collective-permute-start(bf16[2,512,128]{2,1,0:T(8,128)(2,1)S(1)} %shard_map.31.own), channel_id=1, source_target_pairs={{0,64},{32,224},{64,128},{96,32},{128,192},{160,96},{192,0},{224,1... | collective-permute-start | bytes 786440 | tf_op jit(solution)/shard_map/ppermute | solution.py:18
  8.3 0.0 collective-permute-done.blocks_1_
  8.3 5.6 %collective-permute-start.1 = (bf16[2,64,128]{2,1,0:T(8,128)(2,1)S(1)}, bf16[2,64,128]{2,1,0:T(8,128)(2,1)S(1)}, u32[]{:S(2)}, u32[]{:S(2)}) collective-permute-start(bf16[2,64,128]{2,1,0:T(8,128)(2,1)S(1)} %shard_map.29.blocks_0_), channel_id=1, source_target_pairs={{0,5},{1,4},{2,7},{3,6},{4,1},{5,0},{6,3},{7,2},{8,13},{9,12},{10,... | collective-permute-start | bytes 98312 | tf_op jit(solution)/shard_map/ppermute | solution.py:18
  13.9 0.0 collective-permute-start.2
  13.9 3.1 %collective-permute-start.3 = (bf16[2,64,128]{2,1,0:T(8,128)(2,1)S(1)}, bf16[2,64,128]{2,1,0:T(8,128)(2,1)S(1)}, u32[]{:S(2)}, u32[]{:S(2)}) collective-permute-start(bf16[2,64,128]{2,1,0:T(8,128)(2,1)S(1)} %shard_map.29.blocks_0_), channel_id=1, source_target_pairs={{0,7},{1,2},{2,1},{3,4},{4,3},{5,6},{6,5},{7,0},{8,15},{9,10},{10,... | collective-permute-start | bytes 98312 | tf_op jit(solution)/shard_map/ppermute | solution.py:18
  17.0 0.5 %collective-permute-start.8 = (bf16[2,512,128]{2,1,0:T(8,128)(2,1)S(1)}, bf16[2,512,128]{2,1,0:T(8,128)(2,1)S(1)}, u32[]{:S(2)}, u32[]{:S(2)}) collective-permute-start(bf16[2,512,128]{2,1,0:T(8,128)(2,1)S(1)} %shard_map.31.own), channel_id=1, source_target_pairs={{0,128},{32,160},{64,192},{96,224},{128,0},{160,32},{192,64},{224,... | collective-permute-start | bytes 786440 | tf_op jit(solution)/shard_map/ppermute | solution.py:18
  17.5 0.0 collective-permute-done.6.near
  17.5 2.3 %collective-permute-start.7 = (bf16[2,512,128]{2,1,0:T(8,128)(2,1)S(1)}, bf16[2,512,128]{2,1,0:T(8,128)(2,1)S(1)}, u32[]{:S(2)}, u32[]{:S(2)}) collective-permute-start(bf16[2,512,128]{2,1,0:T(8,128)(2,1)S(1)} %collective-permute-done.6.near), channel_id=1, source_target_pairs={{0,32},{32,0},{64,96},{96,64},{128,160},{160,128},{192,224},{224,1... | collective-permute-start | bytes 786440 | tf_op jit(solution)/shard_map/ppermute | solution.py:18
  19.9 0.0 collective-permute-done.1.blocks_1_
  19.9 0.0 collective-permute-done.2.blocks_2_
  19.9 0.0 collective-permute-done.3.blocks_3_
  19.9 3.0 %collective-permute-start.10 = (bf16[8,64,128]{2,1,0:T(8,128)(2,1)S(1)}, bf16[8,64,128]{2,1,0:T(8,128)(2,1)S(1)}, u32[]{:S(2)}, u32[]{:S(2)}) collective-permute-start(bf16[8,64,128]{2,1,0:T(8,128)(2,1)S(1)} %shard_map.30.own), channel_id=1, source_target_pairs={{0,16},{1,17},{2,18},{3,19},{4,20},{5,21},{6,22},{7,23},{8,24},{9,... | collective-permute-start | bytes 393224 | tf_op jit(solution)/shard_map/ppermute | solution.py:18
  22.9 0.8 %collective-permute-start.9 = (bf16[8,64,128]{2,1,0:T(8,128)(2,1)S(1)}, bf16[8,64,128]{2,1,0:T(8,128)(2,1)S(1)}, u32[]{:S(2)}, u32[]{:S(2)}) collective-permute-start(bf16[8,64,128]{2,1,0:T(8,128)(2,1)S(1)} %shard_map.30.own), channel_id=1, source_target_pairs={{0,24},{1,25},{2,26},{3,27},{4,28},{5,29},{6,30},{7,31},{8,0},{9,1... | collective-permute-start | bytes 393224 | tf_op jit(solution)/shard_map/ppermute | solution.py:18
  23.7 0.7 %collective-permute-start.4 = (bf16[8,64,128]{2,1,0:T(8,128)(2,1)S(1)}, bf16[8,64,128]{2,1,0:T(8,128)(2,1)S(1)}, u32[]{:S(2)}, u32[]{:S(2)}) collective-permute-start(bf16[8,64,128]{2,1,0:T(8,128)(2,1)S(1)} %shard_map.30.own), channel_id=1, source_target_pairs={{0,8},{1,9},{2,10},{3,11},{4,12},{5,13},{6,14},{7,15},{8,16},{9,17... | collective-permute-start | bytes 393224 | tf_op jit(solution)/shard_map/ppermute | solution.py:18
  24.4 1.9 %collective-permute-done.8.far = bf16[2,512,128]{2,1,0:T(8,128)(2,1)S(1)} collective-permute-done((bf16[2,512,128]{2,1,0:T(8,128)(2,1)S(1)}, bf16[2,512,128]{2,1,0:T(8,128)(2,1)S(1)}, u32[]{:S(2)}, u32[]{:S(2)}) %collective-permute-start.8) | collective-permute-done | bytes 262176 | tf_op jit(solution)/shard_map/ppermute | solution.py:18
  26.3 0.0 collective-permute-done.7.near_swapped
  26.3 0.1 shard_map.32.padded
  26.4 1.0 %shard_map.33.so_far = f32[512,256]{1,0:T(8,128)S(1)} custom-call(bf16[8,64,128]{2,1,0:T(8,128)(2,1)S(1)} %shard_map.30.own, bf16[8,576,128]{2,1,0:T(8,128)(2,1)S(1)} %shard_map.32.padded), custom_call_target="tpu_custom_call" | custom-call | flops 603979776 | bytes 1048576 | tf_op jit(solution)/shard_map/pallas_call | solution.py:164
  27.4 0.0 collective-permute-done.10.response
  27.4 1.0 %shard_map.34.so_far = f32[512,256]{1,0:T(8,128)S(1)} custom-call(bf16[8,64,128]{2,1,0:T(8,128)(2,1)S(1)} %collective-permute-done.10.response, bf16[8,576,128]{2,1,0:T(8,128)(2,1)S(1)} %shard_map.32.padded, f32[512,256]{1,0:T(8,128)S(1)} %shard_map.33.so_far), custom_call_target="tpu_custom_call" | custom-call | flops 603979776 | bytes 1048576 | tf_op jit(solution)/shard_map/pallas_call | solution.py:164
  28.4 1.2 %collective-permute-done.9.response = bf16[8,64,128]{2,1,0:T(8,128)(2,1)S(1)} collective-permute-done((bf16[8,64,128]{2,1,0:T(8,128)(2,1)S(1)}, bf16[8,64,128]{2,1,0:T(8,128)(2,1)S(1)}, u32[]{:S(2)}, u32[]{:S(2)}) %collective-permute-start.9) | collective-permute-done | bytes 131104 | tf_op jit(solution)/shard_map/ppermute | solution.py:18
  29.6 0.9 %shard_map.35.so_far = f32[512,256]{1,0:T(8,128)S(1)} custom-call(bf16[8,64,128]{2,1,0:T(8,128)(2,1)S(1)} %collective-permute-done.9.response, bf16[8,576,128]{2,1,0:T(8,128)(2,1)S(1)} %shard_map.32.padded, f32[512,256]{1,0:T(8,128)S(1)} %shard_map.34.so_far), custom_call_target="tpu_custom_call" | custom-call | flops 603979776 | bytes 1048576 | tf_op jit(solution)/shard_map/pallas_call | solution.py:164
  30.5 0.0 collective-permute-done.4.before
  30.6 2.0 %shard_map.36 = bf16[32,8,512]{2,1,0:T(8,128)(2,1)} custom-call(bf16[8,64,128]{2,1,0:T(8,128)(2,1)S(1)} %collective-permute-done.4.before, bf16[8,576,128]{2,1,0:T(8,128)(2,1)S(1)} %shard_map.32.padded, f32[512,256]{1,0:T(8,128)S(1)} %shard_map.35.so_far), custom_call_target="tpu_custom_call" | custom-call | flops 603979776 | bytes 1048576 | tf_op jit(solution)/shard_map/pallas_call | solution.py:164
  (3 shorter events, 0.0 us)
Async XLA Ops:
  0.0 4.4 %collective-permute-start.5 = (bf16[16,8,512]{2,1,0:T(8,128)(2,1)}, bf16[16,8,512]{2,1,0:T(8,128)(2,1)S(1)}, u32[]{:S(2)}, u32[]{:S(2)}) collective-permute-start(bf16[16,8,512]{2,1,0:T(8,128)(2,1)} %own.1), channel_id=1, source_target_pairs={{0,32},{32,0},{64,96},{96,64},{128,160},{160,128},{192,224},{224,1... | collective-permute-start | bytes 393224 | tf_op jit(solution)/shard_map/ppermute | solution.py:18
  3.2 0.8 %copy-start.1 = (bf16[32,4,64]{2,1,0:T(4,128)(2,1)S(1)}, bf16[32,4,64]{2,1,0:T(4,128)(2,1)}, u32[]{:S(2)}) copy-start(bf16[32,4,64]{2,1,0:T(4,128)(2,1)} %param.2) | copy-start | bytes 49156
  4.2 4.1 %collective-permute-start = (bf16[1,64,128]{2,1,0:T(8,128)(2,1)S(1)}, bf16[1,64,128]{2,1,0:T(8,128)(2,1)S(1)}, u32[]{:S(2)}, u32[]{:S(2)}) collective-permute-start(bf16[1,64,128]{2,1,0:T(8,128)(2,1)S(1)} %bitcast.2), channel_id=1, source_target_pairs={{0,1},{1,0},{2,3},{3,2},{4,5},{5,4},{6,7},{7,6},{8,9},{9,8},{10,11... | collective-permute-start | bytes 49160 | tf_op jit(solution)/shard_map/ppermute | solution.py:18
  4.4 0.9 %copy-start = (bf16[16,8,512]{2,1,0:T(8,128)(2,1)S(1)}, bf16[16,8,512]{2,1,0:T(8,128)(2,1)}, u32[]{:S(2)}) copy-start(bf16[16,8,512]{2,1,0:T(8,128)(2,1)} %own.1) | copy-start | bytes 393220
  6.0 11.5 %collective-permute-start.6 = (bf16[2,512,128]{2,1,0:T(8,128)(2,1)S(1)}, bf16[2,512,128]{2,1,0:T(8,128)(2,1)S(1)}, u32[]{:S(2)}, u32[]{:S(2)}) collective-permute-start(bf16[2,512,128]{2,1,0:T(8,128)(2,1)S(1)} %shard_map.31.own), channel_id=1, source_target_pairs={{0,64},{32,224},{64,128},{96,32},{128,192},{160,96},{192,0},{224,1... | collective-permute-start | bytes 786440 | tf_op jit(solution)/shard_map/ppermute | solution.py:18
  8.3 11.6 %collective-permute-start.1 = (bf16[2,64,128]{2,1,0:T(8,128)(2,1)S(1)}, bf16[2,64,128]{2,1,0:T(8,128)(2,1)S(1)}, u32[]{:S(2)}, u32[]{:S(2)}) collective-permute-start(bf16[2,64,128]{2,1,0:T(8,128)(2,1)S(1)} %shard_map.29.blocks_0_), channel_id=1, source_target_pairs={{0,5},{1,4},{2,7},{3,6},{4,1},{5,0},{6,3},{7,2},{8,13},{9,12},{10,... | collective-permute-start | bytes 98312 | tf_op jit(solution)/shard_map/ppermute | solution.py:18
  13.9 6.0 %collective-permute-start.2 = (bf16[2,64,128]{2,1,0:T(8,128)(2,1)S(1)}, bf16[2,64,128]{2,1,0:T(8,128)(2,1)S(1)}, u32[]{:S(2)}, u32[]{:S(2)}) collective-permute-start(bf16[2,64,128]{2,1,0:T(8,128)(2,1)S(1)} %shard_map.29.blocks_0_), channel_id=1, source_target_pairs={{0,6},{1,3},{2,0},{3,5},{4,2},{5,7},{6,4},{7,1},{8,14},{9,11},{10,... | collective-permute-start | bytes 98312 | tf_op jit(solution)/shard_map/ppermute | solution.py:18
  13.9 6.0 %collective-permute-start.3 = (bf16[2,64,128]{2,1,0:T(8,128)(2,1)S(1)}, bf16[2,64,128]{2,1,0:T(8,128)(2,1)S(1)}, u32[]{:S(2)}, u32[]{:S(2)}) collective-permute-start(bf16[2,64,128]{2,1,0:T(8,128)(2,1)S(1)} %shard_map.29.blocks_0_), channel_id=1, source_target_pairs={{0,7},{1,2},{2,1},{3,4},{4,3},{5,6},{6,5},{7,0},{8,15},{9,10},{10,... | collective-permute-start | bytes 98312 | tf_op jit(solution)/shard_map/ppermute | solution.py:18
  17.0 9.3 %collective-permute-start.8 = (bf16[2,512,128]{2,1,0:T(8,128)(2,1)S(1)}, bf16[2,512,128]{2,1,0:T(8,128)(2,1)S(1)}, u32[]{:S(2)}, u32[]{:S(2)}) collective-permute-start(bf16[2,512,128]{2,1,0:T(8,128)(2,1)S(1)} %shard_map.31.own), channel_id=1, source_target_pairs={{0,128},{32,160},{64,192},{96,224},{128,0},{160,32},{192,64},{224,... | collective-permute-start | bytes 786440 | tf_op jit(solution)/shard_map/ppermute | solution.py:18
  17.5 8.8 %collective-permute-start.7 = (bf16[2,512,128]{2,1,0:T(8,128)(2,1)S(1)}, bf16[2,512,128]{2,1,0:T(8,128)(2,1)S(1)}, u32[]{:S(2)}, u32[]{:S(2)}) collective-permute-start(bf16[2,512,128]{2,1,0:T(8,128)(2,1)S(1)} %collective-permute-done.6.near), channel_id=1, source_target_pairs={{0,32},{32,0},{64,96},{96,64},{128,160},{160,128},{192,224},{224,1... | collective-permute-start | bytes 786440 | tf_op jit(solution)/shard_map/ppermute | solution.py:18
  19.9 7.5 %collective-permute-start.10 = (bf16[8,64,128]{2,1,0:T(8,128)(2,1)S(1)}, bf16[8,64,128]{2,1,0:T(8,128)(2,1)S(1)}, u32[]{:S(2)}, u32[]{:S(2)}) collective-permute-start(bf16[8,64,128]{2,1,0:T(8,128)(2,1)S(1)} %shard_map.30.own), channel_id=1, source_target_pairs={{0,16},{1,17},{2,18},{3,19},{4,20},{5,21},{6,22},{7,23},{8,24},{9,... | collective-permute-start | bytes 393224 | tf_op jit(solution)/shard_map/ppermute | solution.py:18
  22.9 6.7 %collective-permute-start.9 = (bf16[8,64,128]{2,1,0:T(8,128)(2,1)S(1)}, bf16[8,64,128]{2,1,0:T(8,128)(2,1)S(1)}, u32[]{:S(2)}, u32[]{:S(2)}) collective-permute-start(bf16[8,64,128]{2,1,0:T(8,128)(2,1)S(1)} %shard_map.30.own), channel_id=1, source_target_pairs={{0,24},{1,25},{2,26},{3,27},{4,28},{5,29},{6,30},{7,31},{8,0},{9,1... | collective-permute-start | bytes 393224 | tf_op jit(solution)/shard_map/ppermute | solution.py:18
  23.7 6.9 %collective-permute-start.4 = (bf16[8,64,128]{2,1,0:T(8,128)(2,1)S(1)}, bf16[8,64,128]{2,1,0:T(8,128)(2,1)S(1)}, u32[]{:S(2)}, u32[]{:S(2)}) collective-permute-start(bf16[8,64,128]{2,1,0:T(8,128)(2,1)S(1)} %shard_map.30.own), channel_id=1, source_target_pairs={{0,8},{1,9},{2,10},{3,11},{4,12},{5,13},{6,14},{7,15},{8,16},{9,17... | collective-permute-start | bytes 393224 | tf_op jit(solution)/shard_map/ppermute | solution.py:18

commit v12 on v11

--- a/solution.py
+++ b/solution.py
@@ -45,12 +45,16 @@
         for part in range(4):
             by_receiver = [rows[side, part, pl.ds(r, 16, stride=8), :] for r in range(8)]
             turned[side, part * 128 : part * 128 + 128, :] = jnp.concatenate(by_receiver, axis=0).T
-        skewed = [pltpu.roll(turned[side, pl.ds(d, 64, stride=8), :], 16 * d, 1) for d in range(8)]
+        skewed = [
+            pltpu.roll(turned[side, pl.ds(d, 64, stride=8), :].astype(jnp.bfloat16), 16 * d, 1)
+            for d in range(8)
+        ]
         for r in range(8):
             mixed = skewed[0]
             for d in range(1, 8):
                 mixed = jnp.where(lane_block == (r + d) % 8, skewed[d], mixed)
-            turned[side, pl.ds(r, 64, stride=8), :] = pltpu.roll(mixed, (128 - 16 * r) % 128, 1)
+            mixed = pltpu.roll(mixed, (128 - 16 * r) % 128, 1)
+            turned[side, pl.ds(r, 64, stride=8), :] = mixed.astype(jnp.float32)
         out[side] = turned[side].astype(jnp.bfloat16)
 
 
@@ -143,8 +147,8 @@
     add_products(offset, response, padded, band, rows, so_far, total)
 
 
-def last_kernel(before, padded, so_far, out, band, rows, total, placed):
-    add_products(1, before, padded, band, rows, so_far, total)
+def last_kernel(after, padded, so_far, out, band, rows, total, placed):
+    add_products(3, after, padded, band, rows, so_far, total)
     turned = total[...].astype(jnp.bfloat16).T
     turned = turned.astype(jnp.bfloat16)
     skewed = [pltpu.roll(turned[u * 32 : u * 32 + 32, :], u, 1) for u in range(8)]
@@ -219,14 +223,14 @@
     padded = call(assemble, (8, 576, 128), bf16, pieces, [])
     work = 2 * 512 * 256 * 9 * 256
     total = call(first_kernel, (512, 256), f32, (held, padded), band, work)
-    for offset, block in ((2, across), (3, after)):
+    for offset, block in ((2, across), (1, before)):
         body = functools.partial(middle_kernel, offset)
         total = call(body, (512, 256), f32, (block, padded, total), band, work)
     return call(
         last_kernel,
         (32, 8, 512),
         bf16,
-        (before, padded, total),
+        (after, padded, total),
         band + [((512, 256), f32), ((4, 256, 128), f32)],
         work,
     )

time: 32.7 us -> 32.5 us (level)
  waiting for transfers between devices: 3.33 us -> 2.02 us
  starting transfers between devices: 21.6 us -> 22.8 us
    ppermute x11, waiting for transfers between devices: 3.33 us -> 2.02 us  [spread(): return lax.ppermute(value, axis, [(i, partner(i)) for i in range(size)])]
    ppermute x11, starting transfers between devices: 21.6 us -> 22.8 us  [spread(): return lax.ppermute(value, axis, [(i, partner(i)) for i in range(size)])]
where the time goes in v12:
time: 32.5 us; the launch traced here: 32.4 us
  starting transfers between devices  22.8 us (70%)
  Pallas kernels  5.8 us (18%)
  waiting for transfers between devices  2.02 us (6%)
  local copies, waits for them, and re-layouts  1.66 us (5%)
    ppermute x11, starting transfers between devices, spread(): return lax.ppermute(value, axis, [(i, partner(i)) for i in range(size)])  22.8 us
    pallas_call x9, Pallas kernels, call(): pl.pallas_call(body, out_shape=jax.ShapeDtypeStruct(shape, dtype), in_spe...  5.8 us
    ppermute x11, waiting for transfers between devices, spread(): return lax.ppermute(value, axis, [(i, partner(i)) for i in range(size)])  2.02 us
    unnamed x4, local copies, waits for them, and re-layouts  1.66 us
  transfers between devices with their start and end apart: 11, of which 3 were waited for; matrix products, arithmetic and copies ran while one was open for 0% of the time, Pallas kernels for 12%

profile of v12, /device:TPU:1, one launch (start us, length us, event | category | flops | bytes accessed | tf_op | source)
XLA Modules:
  0.0 32.4 jit_solution(18289685509959707333)
XLA Ops:
  0.0 3.2 %collective-permute-start.5 = (bf16[16,8,512]{2,1,0:T(8,128)(2,1)}, bf16[16,8,512]{2,1,0:T(8,128)(2,1)S(1)}, u32[]{:S(2)}, u32[]{:S(2)}) collective-permute-start(bf16[16,8,512]{2,1,0:T(8,128)(2,1)} %own.1), channel_id=1, source_target_pairs={{0,32},{32,0},{64,96},{96,64},{128,160},{160,128},{192,224},{224,1... | collective-permute-start | bytes 393224 | tf_op jit(solution)/shard_map/ppermute | solution.py:18
  3.2 0.0 copy-start.1
  3.2 0.8 %copy-done.1 = bf16[32,4,64]{2,1,0:T(4,128)(2,1)S(1)} copy-done((bf16[32,4,64]{2,1,0:T(4,128)(2,1)S(1)}, bf16[32,4,64]{2,1,0:T(4,128)(2,1)}, u32[]{:S(2)}) %copy-start.1) | copy-done | bytes 16408
  4.0 0.2 shard_map.28
  4.2 0.1 collective-permute-start
  4.3 0.2 collective-permute-done.5.other
  4.4 0.9 %copy-done = bf16[16,8,512]{2,1,0:T(8,128)(2,1)S(1)} copy-done((bf16[16,8,512]{2,1,0:T(8,128)(2,1)S(1)}, bf16[16,8,512]{2,1,0:T(8,128)(2,1)}, u32[]{:S(2)}) %copy-start) | copy-done | bytes 131096
  5.3 0.6 %shard_map.31.own = bf16[2,512,128]{2,1,0:T(8,128)(2,1)S(1)} custom-call(bf16[16,8,512]{2,1,0:T(8,128)(2,1)S(1)} %copy-done, bf16[16,8,512]{2,1,0:T(8,128)(2,1)S(1)} %collective-permute-done.5.other, bf16[1,64,128]{2,1,0:T(8,128)(2,1)S(1)} %bitcast.3), custom_call_target="tpu_custom_call" | custom-call | bytes 1048576 | tf_op jit(solution)/shard_map/pallas_call | solution.py:168
  6.0 2.3 %collective-permute-start.6 = (bf16[2,512,128]{2,1,0:T(8,128)(2,1)S(1)}, bf16[2,512,128]{2,1,0:T(8,128)(2,1)S(1)}, u32[]{:S(2)}, u32[]{:S(2)}) collective-permute-start(bf16[2,512,128]{2,1,0:T(8,128)(2,1)S(1)} %shard_map.31.own), channel_id=1, source_target_pairs={{0,64},{32,224},{64,128},{96,32},{128,192},{160,96},{192,0},{224,1... | collective-permute-start | bytes 786440 | tf_op jit(solution)/shard_map/ppermute | solution.py:18
  8.2 0.0 collective-permute-done.blocks_1_
  8.3 5.6 %collective-permute-start.1 = (bf16[2,64,128]{2,1,0:T(8,128)(2,1)S(1)}, bf16[2,64,128]{2,1,0:T(8,128)(2,1)S(1)}, u32[]{:S(2)}, u32[]{:S(2)}) collective-permute-start(bf16[2,64,128]{2,1,0:T(8,128)(2,1)S(1)} %shard_map.29.blocks_0_), channel_id=1, source_target_pairs={{0,5},{1,4},{2,7},{3,6},{4,1},{5,0},{6,3},{7,2},{8,13},{9,12},{10,... | collective-permute-start | bytes 98312 | tf_op jit(solution)/shard_map/ppermute | solution.py:18
  13.8 0.0 collective-permute-start.2
  13.8 3.1 %collective-permute-start.3 = (bf16[2,64,128]{2,1,0:T(8,128)(2,1)S(1)}, bf16[2,64,128]{2,1,0:T(8,128)(2,1)S(1)}, u32[]{:S(2)}, u32[]{:S(2)}) collective-permute-start(bf16[2,64,128]{2,1,0:T(8,128)(2,1)S(1)} %shard_map.29.blocks_0_), channel_id=1, source_target_pairs={{0,7},{1,2},{2,1},{3,4},{4,3},{5,6},{6,5},{7,0},{8,15},{9,10},{10,... | collective-permute-start | bytes 98312 | tf_op jit(solution)/shard_map/ppermute | solution.py:18
  16.9 0.5 %collective-permute-start.8 = (bf16[2,512,128]{2,1,0:T(8,128)(2,1)S(1)}, bf16[2,512,128]{2,1,0:T(8,128)(2,1)S(1)}, u32[]{:S(2)}, u32[]{:S(2)}) collective-permute-start(bf16[2,512,128]{2,1,0:T(8,128)(2,1)S(1)} %shard_map.31.own), channel_id=1, source_target_pairs={{0,128},{32,160},{64,192},{96,224},{128,0},{160,32},{192,64},{224,... | collective-permute-start | bytes 786440 | tf_op jit(solution)/shard_map/ppermute | solution.py:18
  17.5 0.0 collective-permute-done.6.near
  17.5 2.3 %collective-permute-start.7 = (bf16[2,512,128]{2,1,0:T(8,128)(2,1)S(1)}, bf16[2,512,128]{2,1,0:T(8,128)(2,1)S(1)}, u32[]{:S(2)}, u32[]{:S(2)}) collective-permute-start(bf16[2,512,128]{2,1,0:T(8,128)(2,1)S(1)} %collective-permute-done.6.near), channel_id=1, source_target_pairs={{0,32},{32,0},{64,96},{96,64},{128,160},{160,128},{192,224},{224,1... | collective-permute-start | bytes 786440 | tf_op jit(solution)/shard_map/ppermute | solution.py:18
  19.8 0.0 collective-permute-done.1.blocks_1_
  19.8 0.0 collective-permute-done.2.blocks_2_
  19.8 0.0 collective-permute-done.3.blocks_3_
  19.8 3.0 %collective-permute-start.10 = (bf16[8,64,128]{2,1,0:T(8,128)(2,1)S(1)}, bf16[8,64,128]{2,1,0:T(8,128)(2,1)S(1)}, u32[]{:S(2)}, u32[]{:S(2)}) collective-permute-start(bf16[8,64,128]{2,1,0:T(8,128)(2,1)S(1)} %shard_map.30.own), channel_id=1, source_target_pairs={{0,16},{1,17},{2,18},{3,19},{4,20},{5,21},{6,22},{7,23},{8,24},{9,... | collective-permute-start | bytes 393224 | tf_op jit(solution)/shard_map/ppermute | solution.py:18
  22.8 0.4 %collective-permute-start.9 = (bf16[8,64,128]{2,1,0:T(8,128)(2,1)S(1)}, bf16[8,64,128]{2,1,0:T(8,128)(2,1)S(1)}, u32[]{:S(2)}, u32[]{:S(2)}) collective-permute-start(bf16[8,64,128]{2,1,0:T(8,128)(2,1)S(1)} %shard_map.30.own), channel_id=1, source_target_pairs={{0,8},{1,9},{2,10},{3,11},{4,12},{5,13},{6,14},{7,15},{8,16},{9,17... | collective-permute-start | bytes 393224 | tf_op jit(solution)/shard_map/ppermute | solution.py:18
  23.2 2.3 %collective-permute-start.4 = (bf16[8,64,128]{2,1,0:T(8,128)(2,1)S(1)}, bf16[8,64,128]{2,1,0:T(8,128)(2,1)S(1)}, u32[]{:S(2)}, u32[]{:S(2)}) collective-permute-start(bf16[8,64,128]{2,1,0:T(8,128)(2,1)S(1)} %shard_map.30.own), channel_id=1, source_target_pairs={{0,24},{1,25},{2,26},{3,27},{4,28},{5,29},{6,30},{7,31},{8,0},{9,1... | collective-permute-start | bytes 393224 | tf_op jit(solution)/shard_map/ppermute | solution.py:18
  25.5 0.7 %collective-permute-done.8.far = bf16[2,512,128]{2,1,0:T(8,128)(2,1)S(1)} collective-permute-done((bf16[2,512,128]{2,1,0:T(8,128)(2,1)S(1)}, bf16[2,512,128]{2,1,0:T(8,128)(2,1)S(1)}, u32[]{:S(2)}, u32[]{:S(2)}) %collective-permute-start.8) | collective-permute-done | bytes 262176 | tf_op jit(solution)/shard_map/ppermute | solution.py:18
  26.2 0.0 collective-permute-done.7.near_swapped
  26.2 0.1 shard_map.32.padded
  26.4 1.0 %shard_map.33.so_far = f32[512,256]{1,0:T(8,128)S(1)} custom-call(bf16[8,64,128]{2,1,0:T(8,128)(2,1)S(1)} %shard_map.30.own, bf16[8,576,128]{2,1,0:T(8,128)(2,1)S(1)} %shard_map.32.padded), custom_call_target="tpu_custom_call" | custom-call | flops 603979776 | bytes 1048576 | tf_op jit(solution)/shard_map/pallas_call | solution.py:168
  27.3 0.0 collective-permute-done.10.response
  27.3 1.0 %shard_map.34.so_far = f32[512,256]{1,0:T(8,128)S(1)} custom-call(bf16[8,64,128]{2,1,0:T(8,128)(2,1)S(1)} %collective-permute-done.10.response, bf16[8,576,128]{2,1,0:T(8,128)(2,1)S(1)} %shard_map.32.padded, f32[512,256]{1,0:T(8,128)S(1)} %shard_map.33.so_far), custom_call_target="tpu_custom_call" | custom-call | flops 603979776 | bytes 1048576 | tf_op jit(solution)/shard_map/pallas_call | solution.py:168
  28.3 1.2 %collective-permute-done.9.response = bf16[8,64,128]{2,1,0:T(8,128)(2,1)S(1)} collective-permute-done((bf16[8,64,128]{2,1,0:T(8,128)(2,1)S(1)}, bf16[8,64,128]{2,1,0:T(8,128)(2,1)S(1)}, u32[]{:S(2)}, u32[]{:S(2)}) %collective-permute-start.9) | collective-permute-done | bytes 131104 | tf_op jit(solution)/shard_map/ppermute | solution.py:18
  29.4 0.9 %shard_map.35.so_far = f32[512,256]{1,0:T(8,128)S(1)} custom-call(bf16[8,64,128]{2,1,0:T(8,128)(2,1)S(1)} %collective-permute-done.9.response, bf16[8,576,128]{2,1,0:T(8,128)(2,1)S(1)} %shard_map.32.padded, f32[512,256]{1,0:T(8,128)S(1)} %shard_map.34.so_far), custom_call_target="tpu_custom_call" | custom-call | flops 603979776 | bytes 1048576 | tf_op jit(solution)/shard_map/pallas_call | solution.py:168
  30.4 0.0 collective-permute-done.4.after
  30.4 2.0 %shard_map.36 = bf16[32,8,512]{2,1,0:T(8,128)(2,1)} custom-call(bf16[8,64,128]{2,1,0:T(8,128)(2,1)S(1)} %collective-permute-done.4.after, bf16[8,576,128]{2,1,0:T(8,128)(2,1)S(1)} %shard_map.32.padded, f32[512,256]{1,0:T(8,128)S(1)} %shard_map.35.so_far), custom_call_target="tpu_custom_call" | custom-call | flops 603979776 | bytes 1048576 | tf_op jit(solution)/shard_map/pallas_call | solution.py:168
  (3 shorter events, 0.0 us)
Async XLA Ops:
  0.0 4.4 %collective-permute-start.5 = (bf16[16,8,512]{2,1,0:T(8,128)(2,1)}, bf16[16,8,512]{2,1,0:T(8,128)(2,1)S(1)}, u32[]{:S(2)}, u32[]{:S(2)}) collective-permute-start(bf16[16,8,512]{2,1,0:T(8,128)(2,1)} %own.1), channel_id=1, source_target_pairs={{0,32},{32,0},{64,96},{96,64},{128,160},{160,128},{192,224},{224,1... | collective-permute-start | bytes 393224 | tf_op jit(solution)/shard_map/ppermute | solution.py:18
  3.2 0.8 %copy-start.1 = (bf16[32,4,64]{2,1,0:T(4,128)(2,1)S(1)}, bf16[32,4,64]{2,1,0:T(4,128)(2,1)}, u32[]{:S(2)}) copy-start(bf16[32,4,64]{2,1,0:T(4,128)(2,1)} %param.2) | copy-start | bytes 49156
  4.2 4.0 %collective-permute-start = (bf16[1,64,128]{2,1,0:T(8,128)(2,1)S(1)}, bf16[1,64,128]{2,1,0:T(8,128)(2,1)S(1)}, u32[]{:S(2)}, u32[]{:S(2)}) collective-permute-start(bf16[1,64,128]{2,1,0:T(8,128)(2,1)S(1)} %bitcast.2), channel_id=1, source_target_pairs={{0,1},{1,0},{2,3},{3,2},{4,5},{5,4},{6,7},{7,6},{8,9},{9,8},{10,11... | collective-permute-start | bytes 49160 | tf_op jit(solution)/shard_map/ppermute | solution.py:18
  4.4 0.9 %copy-start = (bf16[16,8,512]{2,1,0:T(8,128)(2,1)S(1)}, bf16[16,8,512]{2,1,0:T(8,128)(2,1)}, u32[]{:S(2)}) copy-start(bf16[16,8,512]{2,1,0:T(8,128)(2,1)} %own.1) | copy-start | bytes 393220
  6.0 11.5 %collective-permute-start.6 = (bf16[2,512,128]{2,1,0:T(8,128)(2,1)S(1)}, bf16[2,512,128]{2,1,0:T(8,128)(2,1)S(1)}, u32[]{:S(2)}, u32[]{:S(2)}) collective-permute-start(bf16[2,512,128]{2,1,0:T(8,128)(2,1)S(1)} %shard_map.31.own), channel_id=1, source_target_pairs={{0,64},{32,224},{64,128},{96,32},{128,192},{160,96},{192,0},{224,1... | collective-permute-start | bytes 786440 | tf_op jit(solution)/shard_map/ppermute | solution.py:18
  8.3 11.6 %collective-permute-start.1 = (bf16[2,64,128]{2,1,0:T(8,128)(2,1)S(1)}, bf16[2,64,128]{2,1,0:T(8,128)(2,1)S(1)}, u32[]{:S(2)}, u32[]{:S(2)}) collective-permute-start(bf16[2,64,128]{2,1,0:T(8,128)(2,1)S(1)} %shard_map.29.blocks_0_), channel_id=1, source_target_pairs={{0,5},{1,4},{2,7},{3,6},{4,1},{5,0},{6,3},{7,2},{8,13},{9,12},{10,... | collective-permute-start | bytes 98312 | tf_op jit(solution)/shard_map/ppermute | solution.py:18
  13.8 6.0 %collective-permute-start.2 = (bf16[2,64,128]{2,1,0:T(8,128)(2,1)S(1)}, bf16[2,64,128]{2,1,0:T(8,128)(2,1)S(1)}, u32[]{:S(2)}, u32[]{:S(2)}) collective-permute-start(bf16[2,64,128]{2,1,0:T(8,128)(2,1)S(1)} %shard_map.29.blocks_0_), channel_id=1, source_target_pairs={{0,6},{1,3},{2,0},{3,5},{4,2},{5,7},{6,4},{7,1},{8,14},{9,11},{10,... | collective-permute-start | bytes 98312 | tf_op jit(solution)/shard_map/ppermute | solution.py:18
  13.8 6.0 %collective-permute-start.3 = (bf16[2,64,128]{2,1,0:T(8,128)(2,1)S(1)}, bf16[2,64,128]{2,1,0:T(8,128)(2,1)S(1)}, u32[]{:S(2)}, u32[]{:S(2)}) collective-permute-start(bf16[2,64,128]{2,1,0:T(8,128)(2,1)S(1)} %shard_map.29.blocks_0_), channel_id=1, source_target_pairs={{0,7},{1,2},{2,1},{3,4},{4,3},{5,6},{6,5},{7,0},{8,15},{9,10},{10,... | collective-permute-start | bytes 98312 | tf_op jit(solution)/shard_map/ppermute | solution.py:18
  16.9 9.3 %collective-permute-start.8 = (bf16[2,512,128]{2,1,0:T(8,128)(2,1)S(1)}, bf16[2,512,128]{2,1,0:T(8,128)(2,1)S(1)}, u32[]{:S(2)}, u32[]{:S(2)}) collective-permute-start(bf16[2,512,128]{2,1,0:T(8,128)(2,1)S(1)} %shard_map.31.own), channel_id=1, source_target_pairs={{0,128},{32,160},{64,192},{96,224},{128,0},{160,32},{192,64},{224,... | collective-permute-start | bytes 786440 | tf_op jit(solution)/shard_map/ppermute | solution.py:18
  17.5 8.8 %collective-permute-start.7 = (bf16[2,512,128]{2,1,0:T(8,128)(2,1)S(1)}, bf16[2,512,128]{2,1,0:T(8,128)(2,1)S(1)}, u32[]{:S(2)}, u32[]{:S(2)}) collective-permute-start(bf16[2,512,128]{2,1,0:T(8,128)(2,1)S(1)} %collective-permute-done.6.near), channel_id=1, source_target_pairs={{0,32},{32,0},{64,96},{96,64},{128,160},{160,128},{192,224},{224,1... | collective-permute-start | bytes 786440 | tf_op jit(solution)/shard_map/ppermute | solution.py:18
  19.8 7.5 %collective-permute-start.10 = (bf16[8,64,128]{2,1,0:T(8,128)(2,1)S(1)}, bf16[8,64,128]{2,1,0:T(8,128)(2,1)S(1)}, u32[]{:S(2)}, u32[]{:S(2)}) collective-permute-start(bf16[8,64,128]{2,1,0:T(8,128)(2,1)S(1)} %shard_map.30.own), channel_id=1, source_target_pairs={{0,16},{1,17},{2,18},{3,19},{4,20},{5,21},{6,22},{7,23},{8,24},{9,... | collective-permute-start | bytes 393224 | tf_op jit(solution)/shard_map/ppermute | solution.py:18
  22.8 6.6 %collective-permute-start.9 = (bf16[8,64,128]{2,1,0:T(8,128)(2,1)S(1)}, bf16[8,64,128]{2,1,0:T(8,128)(2,1)S(1)}, u32[]{:S(2)}, u32[]{:S(2)}) collective-permute-start(bf16[8,64,128]{2,1,0:T(8,128)(2,1)S(1)} %shard_map.30.own), channel_id=1, source_target_pairs={{0,8},{1,9},{2,10},{3,11},{4,12},{5,13},{6,14},{7,15},{8,16},{9,17... | collective-permute-start | bytes 393224 | tf_op jit(solution)/shard_map/ppermute | solution.py:18
  23.2 7.1 %collective-permute-start.4 = (bf16[8,64,128]{2,1,0:T(8,128)(2,1)S(1)}, bf16[8,64,128]{2,1,0:T(8,128)(2,1)S(1)}, u32[]{:S(2)}, u32[]{:S(2)}) collective-permute-start(bf16[8,64,128]{2,1,0:T(8,128)(2,1)S(1)} %shard_map.30.own), channel_id=1, source_target_pairs={{0,24},{1,25},{2,26},{3,27},{4,28},{5,29},{6,30},{7,31},{8,0},{9,1... | collective-permute-start | bytes 393224 | tf_op jit(solution)/shard_map/ppermute | solution.py:18

commit v13 on v10

--- a/solution.py
+++ b/solution.py
@@ -47,12 +47,16 @@
         for part in range(4):
             by_receiver = [rows[side, part, pl.ds(r, 16, stride=8), :] for r in range(8)]
             turned[side, part * 128 : part * 128 + 128, :] = jnp.concatenate(by_receiver, axis=0).T
-        skewed = [pltpu.roll(turned[side, pl.ds(d, 64, stride=8), :], 16 * d, 1) for d in range(8)]
+        skewed = [
+            pltpu.roll(turned[side, pl.ds(d, 64, stride=8), :].astype(jnp.bfloat16), 16 * d, 1)
+            for d in range(8)
+        ]
         for r in range(8):
             mixed = skewed[0]
             for d in range(1, 8):
                 mixed = jnp.where(lane_block == (r + d) % 8, skewed[d], mixed)
-            turned[side, pl.ds(r, 64, stride=8), :] = pltpu.roll(mixed, (128 - 16 * r) % 128, 1)
+            mixed = pltpu.roll(mixed, (128 - 16 * r) % 128, 1)
+            turned[side, pl.ds(r, 64, stride=8), :] = mixed.astype(jnp.float32)
         out[side] = turned[side].astype(jnp.bfloat16)
 
 
@@ -198,7 +202,7 @@
         prepare_responses,
         (2, 64, 128),
         bf16,
-        (spread(response, "shot", lambda i: i), spread(response, "rcv", along_z(lambda z: z + sign(z)))),
+        (response, spread(response, "rcv", along_z(lambda z: z + sign(z)))),
         [((2, 128, 128), f32), ((2, 64, 128), f32)],
         JOIN_COST,
     )
@@ -206,7 +210,7 @@
         prepare_traces,
         (2, 512, 128),
         bf16,
-        (spread(traces, "shot", lambda i: i), swap(traces)),
+        (traces, swap(traces)),
         [((2, 4, 128, 128), f32), ((2, 512, 128), f32)],
     )
     arrived = [

time: 34.1 us -> 33.4 us (0.979)
  starting transfers between devices: 24.2 us -> 21.1 us
  local copies, waits for them, and re-layouts: 0 us -> 1.66 us
  waiting for transfers between devices: 3.83 us -> 4.48 us
    ppermute x13 -> x11, starting transfers between devices: 24.2 us -> 21.1 us  [spread(): return lax.ppermute(value, axis, [(i, partner(i)) for i in range(size)])]
    unnamed x0 -> x4, local copies, waits for them, and re-layouts: none -> 1.66 us
    ppermute x13 -> x11, waiting for transfers between devices: 3.83 us -> 4.48 us  [spread(): return lax.ppermute(value, axis, [(i, partner(i)) for i in range(size)])]
  transfers between devices with their start and end apart: 13 -> 11, of which waited for: 3 -> 3; matrix products, arithmetic and copies ran while one was open for 0% -> 0% of each run, Pallas kernels for 11% -> 12%
where the time goes in v13:
time: 33.4 us; the launch traced here: 33.2 us
  starting transfers between devices  21.1 us (63%)
  Pallas kernels  5.82 us (17%)
  waiting for transfers between devices  4.48 us (13%)
  local copies, waits for them, and re-layouts  1.66 us (5%)
    ppermute x11, starting transfers between devices, spread(): return lax.ppermute(value, axis, [(i, partner(i)) for i in range(size)])  21.1 us
    pallas_call x8, Pallas kernels, call(): pl.pallas_call(body, out_shape=jax.ShapeDtypeStruct(shape, dtype), in_spe...  5.82 us
    ppermute x11, waiting for transfers between devices, spread(): return lax.ppermute(value, axis, [(i, partner(i)) for i in range(size)])  4.48 us
    unnamed x4, local copies, waits for them, and re-layouts  1.66 us
  transfers between devices with their start and end apart: 11, of which 3 were waited for; matrix products, arithmetic and copies ran while one was open for 0% of the time, Pallas kernels for 12%

profile of v13, /device:TPU:1, one launch (start us, length us, event | category | flops | bytes accessed | tf_op | source)
XLA Modules:
  0.0 33.2 jit_solution(14003621034848529386)
XLA Ops:
  0.0 3.2 %collective-permute-start.5 = (bf16[16,8,512]{2,1,0:T(8,128)(2,1)}, bf16[16,8,512]{2,1,0:T(8,128)(2,1)S(1)}, u32[]{:S(2)}, u32[]{:S(2)}) collective-permute-start(bf16[16,8,512]{2,1,0:T(8,128)(2,1)} %own.1), channel_id=1, source_target_pairs={{0,32},{32,0},{64,96},{96,64},{128,160},{160,128},{192,224},{224,1... | collective-permute-start | bytes 393224 | tf_op jit(solution)/shard_map/ppermute | solution.py:18
  3.2 0.0 collective-permute-start
  3.2 1.2 %collective-permute-done.5.other = bf16[16,8,512]{2,1,0:T(8,128)(2,1)S(1)} collective-permute-done((bf16[16,8,512]{2,1,0:T(8,128)(2,1)}, bf16[16,8,512]{2,1,0:T(8,128)(2,1)S(1)}, u32[]{:S(2)}, u32[]{:S(2)}) %collective-permute-start.5) | collective-permute-done | bytes 131104 | tf_op jit(solution)/shard_map/ppermute | solution.py:18
  4.4 0.0 copy-start
  4.4 0.9 %copy-done = bf16[16,8,512]{2,1,0:T(8,128)(2,1)S(1)} copy-done((bf16[16,8,512]{2,1,0:T(8,128)(2,1)S(1)}, bf16[16,8,512]{2,1,0:T(8,128)(2,1)}, u32[]{:S(2)}) %copy-start) | copy-done | bytes 131096
  5.3 0.6 %shard_map.30.own = bf16[2,512,128]{2,1,0:T(8,128)(2,1)S(1)} custom-call(bf16[16,8,512]{2,1,0:T(8,128)(2,1)S(1)} %copy-done, bf16[16,8,512]{2,1,0:T(8,128)(2,1)S(1)} %collective-permute-done.5.other), custom_call_target="tpu_custom_call" | custom-call | bytes 1048576 | tf_op jit(solution)/shard_map/pallas_call | solution.py:170
  6.0 1.3 %collective-permute-start.6 = (bf16[2,512,128]{2,1,0:T(8,128)(2,1)S(1)}, bf16[2,512,128]{2,1,0:T(8,128)(2,1)S(1)}, u32[]{:S(2)}, u32[]{:S(2)}) collective-permute-start(bf16[2,512,128]{2,1,0:T(8,128)(2,1)S(1)} %shard_map.30.own), channel_id=1, source_target_pairs={{0,64},{32,224},{64,128},{96,32},{128,192},{160,96},{192,0},{224,1... | collective-permute-start | bytes 786440 | tf_op jit(solution)/shard_map/ppermute | solution.py:18
  7.2 0.0 collective-permute-done.neighbour
  7.2 0.8 %copy-done.1 = bf16[32,4,64]{2,1,0:T(4,128)(2,1)S(1)} copy-done((bf16[32,4,64]{2,1,0:T(4,128)(2,1)S(1)}, bf16[32,4,64]{2,1,0:T(4,128)(2,1)}, u32[]{:S(2)}) %copy-start.1) | copy-done | bytes 16408
  8.0 0.3 shard_map.28.blocks_0_
  8.2 6.1 %collective-permute-start.1 = (bf16[2,64,128]{2,1,0:T(8,128)(2,1)S(1)}, bf16[2,64,128]{2,1,0:T(8,128)(2,1)S(1)}, u32[]{:S(2)}, u32[]{:S(2)}) collective-permute-start(bf16[2,64,128]{2,1,0:T(8,128)(2,1)S(1)} %shard_map.28.blocks_0_), channel_id=1, source_target_pairs={{0,5},{1,4},{2,7},{3,6},{4,1},{5,0},{6,3},{7,2},{8,13},{9,12},{10,... | collective-permute-start | bytes 98312 | tf_op jit(solution)/shard_map/ppermute | solution.py:18
  14.4 0.3 collective-permute-start.2
  14.6 2.9 %collective-permute-start.3 = (bf16[2,64,128]{2,1,0:T(8,128)(2,1)S(1)}, bf16[2,64,128]{2,1,0:T(8,128)(2,1)S(1)}, u32[]{:S(2)}, u32[]{:S(2)}) collective-permute-start(bf16[2,64,128]{2,1,0:T(8,128)(2,1)S(1)} %shard_map.28.blocks_0_), channel_id=1, source_target_pairs={{0,7},{1,2},{2,1},{3,4},{4,3},{5,6},{6,5},{7,0},{8,15},{9,10},{10,... | collective-permute-start | bytes 98312 | tf_op jit(solution)/shard_map/ppermute | solution.py:18
  17.5 0.5 %collective-permute-start.8 = (bf16[2,512,128]{2,1,0:T(8,128)(2,1)S(1)}, bf16[2,512,128]{2,1,0:T(8,128)(2,1)S(1)}, u32[]{:S(2)}, u32[]{:S(2)}) collective-permute-start(bf16[2,512,128]{2,1,0:T(8,128)(2,1)S(1)} %shard_map.30.own), channel_id=1, source_target_pairs={{0,128},{32,160},{64,192},{96,224},{128,0},{160,32},{192,64},{224,... | collective-permute-start | bytes 786440 | tf_op jit(solution)/shard_map/ppermute | solution.py:18
  18.0 0.0 collective-permute-done.6.near
  18.0 2.4 %collective-permute-start.7 = (bf16[2,512,128]{2,1,0:T(8,128)(2,1)S(1)}, bf16[2,512,128]{2,1,0:T(8,128)(2,1)S(1)}, u32[]{:S(2)}, u32[]{:S(2)}) collective-permute-start(bf16[2,512,128]{2,1,0:T(8,128)(2,1)S(1)} %collective-permute-done.6.near), channel_id=1, source_target_pairs={{0,32},{32,0},{64,96},{96,64},{128,160},{160,128},{192,224},{224,1... | collective-permute-start | bytes 786440 | tf_op jit(solution)/shard_map/ppermute | solution.py:18
  20.4 0.0 collective-permute-done.1.blocks_1_
  20.4 0.0 collective-permute-done.2.blocks_2_
  20.4 0.0 collective-permute-done.3.blocks_3_
  20.5 3.0 %collective-permute-start.10 = (bf16[8,64,128]{2,1,0:T(8,128)(2,1)S(1)}, bf16[8,64,128]{2,1,0:T(8,128)(2,1)S(1)}, u32[]{:S(2)}, u32[]{:S(2)}) collective-permute-start(bf16[8,64,128]{2,1,0:T(8,128)(2,1)S(1)} %shard_map.29.own), channel_id=1, source_target_pairs={{0,16},{1,17},{2,18},{3,19},{4,20},{5,21},{6,22},{7,23},{8,24},{9,... | collective-permute-start | bytes 393224 | tf_op jit(solution)/shard_map/ppermute | solution.py:18
  23.5 0.8 %collective-permute-start.9 = (bf16[8,64,128]{2,1,0:T(8,128)(2,1)S(1)}, bf16[8,64,128]{2,1,0:T(8,128)(2,1)S(1)}, u32[]{:S(2)}, u32[]{:S(2)}) collective-permute-start(bf16[8,64,128]{2,1,0:T(8,128)(2,1)S(1)} %shard_map.29.own), channel_id=1, source_target_pairs={{0,24},{1,25},{2,26},{3,27},{4,28},{5,29},{6,30},{7,31},{8,0},{9,1... | collective-permute-start | bytes 393224 | tf_op jit(solution)/shard_map/ppermute | solution.py:18
  24.2 0.7 %collective-permute-start.4 = (bf16[8,64,128]{2,1,0:T(8,128)(2,1)S(1)}, bf16[8,64,128]{2,1,0:T(8,128)(2,1)S(1)}, u32[]{:S(2)}, u32[]{:S(2)}) collective-permute-start(bf16[8,64,128]{2,1,0:T(8,128)(2,1)S(1)} %shard_map.29.own), channel_id=1, source_target_pairs={{0,8},{1,9},{2,10},{3,11},{4,12},{5,13},{6,14},{7,15},{8,16},{9,17... | collective-permute-start | bytes 393224 | tf_op jit(solution)/shard_map/ppermute | solution.py:18
  24.9 1.8 %collective-permute-done.8.far = bf16[2,512,128]{2,1,0:T(8,128)(2,1)S(1)} collective-permute-done((bf16[2,512,128]{2,1,0:T(8,128)(2,1)S(1)}, bf16[2,512,128]{2,1,0:T(8,128)(2,1)S(1)}, u32[]{:S(2)}, u32[]{:S(2)}) %collective-permute-start.8) | collective-permute-done | bytes 262176 | tf_op jit(solution)/shard_map/ppermute | solution.py:18
  26.7 0.0 collective-permute-done.7.near_swapped
  26.7 0.1 shard_map.31.padded
  26.8 1.0 %shard_map.32.so_far = f32[512,256]{1,0:T(8,128)S(1)} custom-call(bf16[8,64,128]{2,1,0:T(8,128)(2,1)S(1)} %shard_map.29.own, bf16[8,576,128]{2,1,0:T(8,128)(2,1)S(1)} %shard_map.31.padded), custom_call_target="tpu_custom_call" | custom-call | flops 603979776 | bytes 1048576 | tf_op jit(solution)/shard_map/pallas_call | solution.py:170
  27.8 0.0 collective-permute-done.10.response
  27.8 1.0 %shard_map.33.so_far = f32[512,256]{1,0:T(8,128)S(1)} custom-call(bf16[8,64,128]{2,1,0:T(8,128)(2,1)S(1)} %collective-permute-done.10.response, bf16[8,576,128]{2,1,0:T(8,128)(2,1)S(1)} %shard_map.31.padded, f32[512,256]{1,0:T(8,128)S(1)} %shard_map.32.so_far), custom_call_target="tpu_custom_call" | custom-call | flops 603979776 | bytes 1048576 | tf_op jit(solution)/shard_map/pallas_call | solution.py:170
  28.8 1.5 %collective-permute-done.9.response = bf16[8,64,128]{2,1,0:T(8,128)(2,1)S(1)} collective-permute-done((bf16[8,64,128]{2,1,0:T(8,128)(2,1)S(1)}, bf16[8,64,128]{2,1,0:T(8,128)(2,1)S(1)}, u32[]{:S(2)}, u32[]{:S(2)}) %collective-permute-start.9) | collective-permute-done | bytes 131104 | tf_op jit(solution)/shard_map/ppermute | solution.py:18
  30.3 0.9 %shard_map.34.so_far = f32[512,256]{1,0:T(8,128)S(1)} custom-call(bf16[8,64,128]{2,1,0:T(8,128)(2,1)S(1)} %collective-permute-done.9.response, bf16[8,576,128]{2,1,0:T(8,128)(2,1)S(1)} %shard_map.31.padded, f32[512,256]{1,0:T(8,128)S(1)} %shard_map.33.so_far), custom_call_target="tpu_custom_call" | custom-call | flops 603979776 | bytes 1048576 | tf_op jit(solution)/shard_map/pallas_call | solution.py:170
  31.2 0.0 collective-permute-done.4.before
  31.2 2.0 %shard_map.35 = bf16[32,8,512]{2,1,0:T(8,128)(2,1)} custom-call(bf16[8,64,128]{2,1,0:T(8,128)(2,1)S(1)} %collective-permute-done.4.before, bf16[8,576,128]{2,1,0:T(8,128)(2,1)S(1)} %shard_map.31.padded, f32[512,256]{1,0:T(8,128)S(1)} %shard_map.34.so_far), custom_call_target="tpu_custom_call" | custom-call | flops 603979776 | bytes 1048576 | tf_op jit(solution)/shard_map/pallas_call | solution.py:170
  (2 shorter events, 0.0 us)
Async XLA Ops:
  0.0 4.4 %collective-permute-start.5 = (bf16[16,8,512]{2,1,0:T(8,128)(2,1)}, bf16[16,8,512]{2,1,0:T(8,128)(2,1)S(1)}, u32[]{:S(2)}, u32[]{:S(2)}) collective-permute-start(bf16[16,8,512]{2,1,0:T(8,128)(2,1)} %own.1), channel_id=1, source_target_pairs={{0,32},{32,0},{64,96},{96,64},{128,160},{160,128},{192,224},{224,1... | collective-permute-start | bytes 393224 | tf_op jit(solution)/shard_map/ppermute | solution.py:18
  3.2 4.0 %collective-permute-start = (bf16[128,64]{1,0:T(8,128)(2,1)}, bf16[128,64]{1,0:T(8,128)(2,1)S(1)}, u32[]{:S(2)}, u32[]{:S(2)}) collective-permute-start(bf16[128,64]{1,0:T(8,128)(2,1)} %bitcast.1), channel_id=1, source_target_pairs={{0,1},{1,0},{2,3},{3,2},{4,5},{5,4},{6,7},{7,6},{8,9},{9,8},{10,11... | collective-permute-start | bytes 49160 | tf_op jit(solution)/shard_map/ppermute | solution.py:18
  4.4 0.9 %copy-start = (bf16[16,8,512]{2,1,0:T(8,128)(2,1)S(1)}, bf16[16,8,512]{2,1,0:T(8,128)(2,1)}, u32[]{:S(2)}) copy-start(bf16[16,8,512]{2,1,0:T(8,128)(2,1)} %own.1) | copy-start | bytes 393220
  6.0 12.0 %collective-permute-start.6 = (bf16[2,512,128]{2,1,0:T(8,128)(2,1)S(1)}, bf16[2,512,128]{2,1,0:T(8,128)(2,1)S(1)}, u32[]{:S(2)}, u32[]{:S(2)}) collective-permute-start(bf16[2,512,128]{2,1,0:T(8,128)(2,1)S(1)} %shard_map.30.own), channel_id=1, source_target_pairs={{0,64},{32,224},{64,128},{96,32},{128,192},{160,96},{192,0},{224,1... | collective-permute-start | bytes 786440 | tf_op jit(solution)/shard_map/ppermute | solution.py:18
  7.2 0.8 %copy-start.1 = (bf16[32,4,64]{2,1,0:T(4,128)(2,1)S(1)}, bf16[32,4,64]{2,1,0:T(4,128)(2,1)}, u32[]{:S(2)}) copy-start(bf16[32,4,64]{2,1,0:T(4,128)(2,1)} %param.2) | copy-start | bytes 49156
  8.2 12.2 %collective-permute-start.1 = (bf16[2,64,128]{2,1,0:T(8,128)(2,1)S(1)}, bf16[2,64,128]{2,1,0:T(8,128)(2,1)S(1)}, u32[]{:S(2)}, u32[]{:S(2)}) collective-permute-start(bf16[2,64,128]{2,1,0:T(8,128)(2,1)S(1)} %shard_map.28.blocks_0_), channel_id=1, source_target_pairs={{0,5},{1,4},{2,7},{3,6},{4,1},{5,0},{6,3},{7,2},{8,13},{9,12},{10,... | collective-permute-start | bytes 98312 | tf_op jit(solution)/shard_map/ppermute | solution.py:18
  14.4 6.1 %collective-permute-start.2 = (bf16[2,64,128]{2,1,0:T(8,128)(2,1)S(1)}, bf16[2,64,128]{2,1,0:T(8,128)(2,1)S(1)}, u32[]{:S(2)}, u32[]{:S(2)}) collective-permute-start(bf16[2,64,128]{2,1,0:T(8,128)(2,1)S(1)} %shard_map.28.blocks_0_), channel_id=1, source_target_pairs={{0,6},{1,3},{2,0},{3,5},{4,2},{5,7},{6,4},{7,1},{8,14},{9,11},{10,... | collective-permute-start | bytes 98312 | tf_op jit(solution)/shard_map/ppermute | solution.py:18
  14.6 5.8 %collective-permute-start.3 = (bf16[2,64,128]{2,1,0:T(8,128)(2,1)S(1)}, bf16[2,64,128]{2,1,0:T(8,128)(2,1)S(1)}, u32[]{:S(2)}, u32[]{:S(2)}) collective-permute-start(bf16[2,64,128]{2,1,0:T(8,128)(2,1)S(1)} %shard_map.28.blocks_0_), channel_id=1, source_target_pairs={{0,7},{1,2},{2,1},{3,4},{4,3},{5,6},{6,5},{7,0},{8,15},{9,10},{10,... | collective-permute-start | bytes 98312 | tf_op jit(solution)/shard_map/ppermute | solution.py:18
  17.5 9.2 %collective-permute-start.8 = (bf16[2,512,128]{2,1,0:T(8,128)(2,1)S(1)}, bf16[2,512,128]{2,1,0:T(8,128)(2,1)S(1)}, u32[]{:S(2)}, u32[]{:S(2)}) collective-permute-start(bf16[2,512,128]{2,1,0:T(8,128)(2,1)S(1)} %shard_map.30.own), channel_id=1, source_target_pairs={{0,128},{32,160},{64,192},{96,224},{128,0},{160,32},{192,64},{224,... | collective-permute-start | bytes 786440 | tf_op jit(solution)/shard_map/ppermute | solution.py:18
  18.0 8.7 %collective-permute-start.7 = (bf16[2,512,128]{2,1,0:T(8,128)(2,1)S(1)}, bf16[2,512,128]{2,1,0:T(8,128)(2,1)S(1)}, u32[]{:S(2)}, u32[]{:S(2)}) collective-permute-start(bf16[2,512,128]{2,1,0:T(8,128)(2,1)S(1)} %collective-permute-done.6.near), channel_id=1, source_target_pairs={{0,32},{32,0},{64,96},{96,64},{128,160},{160,128},{192,224},{224,1... | collective-permute-start | bytes 786440 | tf_op jit(solution)/shard_map/ppermute | solution.py:18
  20.5 7.3 %collective-permute-start.10 = (bf16[8,64,128]{2,1,0:T(8,128)(2,1)S(1)}, bf16[8,64,128]{2,1,0:T(8,128)(2,1)S(1)}, u32[]{:S(2)}, u32[]{:S(2)}) collective-permute-start(bf16[8,64,128]{2,1,0:T(8,128)(2,1)S(1)} %shard_map.29.own), channel_id=1, source_target_pairs={{0,16},{1,17},{2,18},{3,19},{4,20},{5,21},{6,22},{7,23},{8,24},{9,... | collective-permute-start | bytes 393224 | tf_op jit(solution)/shard_map/ppermute | solution.py:18
  23.5 6.8 %collective-permute-start.9 = (bf16[8,64,128]{2,1,0:T(8,128)(2,1)S(1)}, bf16[8,64,128]{2,1,0:T(8,128)(2,1)S(1)}, u32[]{:S(2)}, u32[]{:S(2)}) collective-permute-start(bf16[8,64,128]{2,1,0:T(8,128)(2,1)S(1)} %shard_map.29.own), channel_id=1, source_target_pairs={{0,24},{1,25},{2,26},{3,27},{4,28},{5,29},{6,30},{7,31},{8,0},{9,1... | collective-permute-start | bytes 393224 | tf_op jit(solution)/shard_map/ppermute | solution.py:18
  24.2 7.0 %collective-permute-start.4 = (bf16[8,64,128]{2,1,0:T(8,128)(2,1)S(1)}, bf16[8,64,128]{2,1,0:T(8,128)(2,1)S(1)}, u32[]{:S(2)}, u32[]{:S(2)}) collective-permute-start(bf16[8,64,128]{2,1,0:T(8,128)(2,1)S(1)} %shard_map.29.own), channel_id=1, source_target_pairs={{0,8},{1,9},{2,10},{3,11},{4,12},{5,13},{6,14},{7,15},{8,16},{9,17... | collective-permute-start | bytes 393224 | tf_op jit(solution)/shard_map/ppermute | solution.py:18

commit v14 on v12

--- a/solution.py
+++ b/solution.py
@@ -109,6 +109,8 @@
             band[half, shift * 16 : shift * 16 + 16, :] = pltpu.roll(
                 wide, 128 + 32 * shift, 1
             ).astype(jnp.bfloat16)
+    if offset % 2:
+        offset = offset * sign(lax.axis_index("shot") % 2)
     place = ((y + 4 - offset) % 4) * 2
     even_rows, odd_rows, sides = [], [], []
     for group in range(5):
@@ -147,8 +149,8 @@
     add_products(offset, response, padded, band, rows, so_far, total)
 
 
-def last_kernel(after, padded, so_far, out, band, rows, total, placed):
-    add_products(3, after, padded, band, rows, so_far, total)
+def last_kernel(outward, padded, so_far, out, band, rows, total, placed):
+    add_products(1, outward, padded, band, rows, so_far, total)
     turned = total[...].astype(jnp.bfloat16).T
     turned = turned.astype(jnp.bfloat16)
     skewed = [pltpu.roll(turned[u * 32 : u * 32 + 32, :], u, 1) for u in range(8)]
@@ -186,6 +188,13 @@
     def along_y(offset):
         return lambda i: (i // 8 + offset) % 4 * 8 + i % 8
 
+    def by_core(value, way):
+        pairs = []
+        for i in range(lax.axis_size("shot")):
+            step = along_y(way * sign(i))
+            pairs += [(i * 32 + j, i * 32 + step(j)) for j in range(lax.axis_size("rcv"))]
+        return lax.ppermute(value, ("shot", "rcv"), pairs)
+
     def along_x(i):
         return ((i // 2 + sign(i)) % 4) * 2 + i % 2
 
@@ -215,7 +224,8 @@
         spread(held, "rcv", along_z(lambda z, hops=hops: z - hops * sign(z))) for hops in (3, 2, 1)
     ]
     held = call(join, (8, 64, 128), bf16, (held, *arrived), [], JOIN_COST)
-    before, after, across = [spread(held, "rcv", along_y(offset)) for offset in (1, 3, 2)]
+    across = spread(held, "rcv", along_y(2))
+    outward, inward = by_core(held, 1), by_core(held, -1)
 
     near = spread(both, "shot", along_x)
     far = spread(both, "shot", across_x)
@@ -223,14 +233,14 @@
     padded = call(assemble, (8, 576, 128), bf16, pieces, [])
     work = 2 * 512 * 256 * 9 * 256
     total = call(first_kernel, (512, 256), f32, (held, padded), band, work)
-    for offset, block in ((2, across), (1, before)):
+    for offset, block in ((2, across), (-1, inward)):
         body = functools.partial(middle_kernel, offset)
         total = call(body, (512, 256), f32, (block, padded, total), band, work)
     return call(
         last_kernel,
         (32, 8, 512),
         bf16,
-        (after, padded, total),
+        (outward, padded, total),
         band + [((512, 256), f32), ((4, 256, 128), f32)],
         work,
     )

time: 32.5 us -> 31.8 us (0.978)
  waiting for transfers between devices: 2.02 us -> 1.15 us
    ppermute x0 -> x2, starting transfers between devices: none -> 2.68 us  [by_core(): return lax.ppermute(value, ('shot', 'rcv'), pairs)]
    ppermute x11 -> x9, starting transfers between devices: 22.8 us -> 20.1 us  [spread(): return lax.ppermute(value, axis, [(i, partner(i)) for i in range(size)])]
    ppermute x11 -> x9, waiting for transfers between devices: 2.02 us -> 0.86 us  [spread(): return lax.ppermute(value, axis, [(i, partner(i)) for i in range(size)])]
  transfers between devices with their start and end apart: 11 -> 11, of which waited for: 3 -> 4; matrix products, arithmetic and copies ran while one was open for 0% -> 0% of each run, Pallas kernels for 12% -> 12%
where the time goes in v14:
time: 31.8 us; the launch traced here: 31.5 us
  starting transfers between devices  22.8 us (72%)
  Pallas kernels  5.78 us (18%)
  local copies, waits for them, and re-layouts  1.66 us (5%)
  waiting for transfers between devices  1.15 us (4%)
    ppermute x9, starting transfers between devices, spread(): return lax.ppermute(value, axis, [(i, partner(i)) for i in range(size)])  20.1 us
    pallas_call x9, Pallas kernels, call(): pl.pallas_call(body, out_shape=jax.ShapeDtypeStruct(shape, dtype), in_spe...  5.78 us
    ppermute x2, starting transfers between devices, by_core(): return lax.ppermute(value, ('shot', 'rcv'), pairs)  2.68 us
    unnamed x4, local copies, waits for them, and re-layouts  1.66 us
    ppermute x9, waiting for transfers between devices, spread(): return lax.ppermute(value, axis, [(i, partner(i)) for i in range(size)])  0.86 us
  transfers between devices with their start and end apart: 11, of which 4 were waited for; matrix products, arithmetic and copies ran while one was open for 0% of the time, Pallas kernels for 12%

profile of v14, /device:TPU:1, one launch (start us, length us, event | category | flops | bytes accessed | tf_op | source)
XLA Modules:
  0.0 31.5 jit_solution(15928837100446530366)
XLA Ops:
  0.0 3.2 %collective-permute-start.5 = (bf16[16,8,512]{2,1,0:T(8,128)(2,1)}, bf16[16,8,512]{2,1,0:T(8,128)(2,1)S(1)}, u32[]{:S(2)}, u32[]{:S(2)}) collective-permute-start(bf16[16,8,512]{2,1,0:T(8,128)(2,1)} %own.1), channel_id=1, source_target_pairs={{0,32},{32,0},{64,96},{96,64},{128,160},{160,128},{192,224},{224,1... | collective-permute-start | bytes 393224 | tf_op jit(solution)/shard_map/ppermute | solution.py:18
  3.2 0.0 copy-start.1
  3.2 0.8 %copy-done.1 = bf16[32,4,64]{2,1,0:T(4,128)(2,1)S(1)} copy-done((bf16[32,4,64]{2,1,0:T(4,128)(2,1)S(1)}, bf16[32,4,64]{2,1,0:T(4,128)(2,1)}, u32[]{:S(2)}) %copy-start.1) | copy-done | bytes 16408
  4.0 0.2 shard_map.28
  4.2 0.1 collective-permute-start
  4.3 0.2 collective-permute-done.5.other
  4.4 0.9 %copy-done = bf16[16,8,512]{2,1,0:T(8,128)(2,1)S(1)} copy-done((bf16[16,8,512]{2,1,0:T(8,128)(2,1)S(1)}, bf16[16,8,512]{2,1,0:T(8,128)(2,1)}, u32[]{:S(2)}) %copy-start) | copy-done | bytes 131096
  5.3 0.6 %shard_map.31.own = bf16[2,512,128]{2,1,0:T(8,128)(2,1)S(1)} custom-call(bf16[16,8,512]{2,1,0:T(8,128)(2,1)S(1)} %copy-done, bf16[16,8,512]{2,1,0:T(8,128)(2,1)S(1)} %collective-permute-done.5.other, bf16[1,64,128]{2,1,0:T(8,128)(2,1)S(1)} %bitcast.3), custom_call_target="tpu_custom_call" | custom-call | bytes 1048576 | tf_op jit(solution)/shard_map/pallas_call | solution.py:170
  6.0 2.3 %collective-permute-start.6 = (bf16[2,512,128]{2,1,0:T(8,128)(2,1)S(1)}, bf16[2,512,128]{2,1,0:T(8,128)(2,1)S(1)}, u32[]{:S(2)}, u32[]{:S(2)}) collective-permute-start(bf16[2,512,128]{2,1,0:T(8,128)(2,1)S(1)} %shard_map.31.own), channel_id=1, source_target_pairs={{0,64},{32,224},{64,128},{96,32},{128,192},{160,96},{192,0},{224,1... | collective-permute-start | bytes 786440 | tf_op jit(solution)/shard_map/ppermute | solution.py:18
  8.2 0.0 collective-permute-done.blocks_1_
  8.3 5.6 %collective-permute-start.1 = (bf16[2,64,128]{2,1,0:T(8,128)(2,1)S(1)}, bf16[2,64,128]{2,1,0:T(8,128)(2,1)S(1)}, u32[]{:S(2)}, u32[]{:S(2)}) collective-permute-start(bf16[2,64,128]{2,1,0:T(8,128)(2,1)S(1)} %shard_map.29.blocks_0_), channel_id=1, source_target_pairs={{0,5},{1,4},{2,7},{3,6},{4,1},{5,0},{6,3},{7,2},{8,13},{9,12},{10,... | collective-permute-start | bytes 98312 | tf_op jit(solution)/shard_map/ppermute | solution.py:18
  13.8 0.0 collective-permute-start.2
  13.8 3.1 %collective-permute-start.3 = (bf16[2,64,128]{2,1,0:T(8,128)(2,1)S(1)}, bf16[2,64,128]{2,1,0:T(8,128)(2,1)S(1)}, u32[]{:S(2)}, u32[]{:S(2)}) collective-permute-start(bf16[2,64,128]{2,1,0:T(8,128)(2,1)S(1)} %shard_map.29.blocks_0_), channel_id=1, source_target_pairs={{0,7},{1,2},{2,1},{3,4},{4,3},{5,6},{6,5},{7,0},{8,15},{9,10},{10,... | collective-permute-start | bytes 98312 | tf_op jit(solution)/shard_map/ppermute | solution.py:18
  16.9 0.5 %collective-permute-start.8 = (bf16[2,512,128]{2,1,0:T(8,128)(2,1)S(1)}, bf16[2,512,128]{2,1,0:T(8,128)(2,1)S(1)}, u32[]{:S(2)}, u32[]{:S(2)}) collective-permute-start(bf16[2,512,128]{2,1,0:T(8,128)(2,1)S(1)} %shard_map.31.own), channel_id=1, source_target_pairs={{0,128},{32,160},{64,192},{96,224},{128,0},{160,32},{192,64},{224,... | collective-permute-start | bytes 786440 | tf_op jit(solution)/shard_map/ppermute | solution.py:18
  17.5 0.0 collective-permute-done.6.near
  17.5 2.3 %collective-permute-start.7 = (bf16[2,512,128]{2,1,0:T(8,128)(2,1)S(1)}, bf16[2,512,128]{2,1,0:T(8,128)(2,1)S(1)}, u32[]{:S(2)}, u32[]{:S(2)}) collective-permute-start(bf16[2,512,128]{2,1,0:T(8,128)(2,1)S(1)} %collective-permute-done.6.near), channel_id=1, source_target_pairs={{0,32},{32,0},{64,96},{96,64},{128,160},{160,128},{192,224},{224,1... | collective-permute-start | bytes 786440 | tf_op jit(solution)/shard_map/ppermute | solution.py:18
  19.8 0.0 collective-permute-done.1.blocks_1_
  19.8 0.0 collective-permute-done.2.blocks_2_
  19.8 0.0 collective-permute-done.3.blocks_3_
  19.8 3.0 %collective-permute-start.10 = (bf16[8,64,128]{2,1,0:T(8,128)(2,1)S(1)}, bf16[8,64,128]{2,1,0:T(8,128)(2,1)S(1)}, u32[]{:S(2)}, u32[]{:S(2)}) collective-permute-start(bf16[8,64,128]{2,1,0:T(8,128)(2,1)S(1)} %shard_map.30.own), channel_id=1, source_target_pairs={{0,16},{1,17},{2,18},{3,19},{4,20},{5,21},{6,22},{7,23},{8,24},{9,... | collective-permute-start | bytes 393224 | tf_op jit(solution)/shard_map/ppermute | solution.py:18
  22.8 0.4 %collective-permute-start.9 = (bf16[8,64,128]{2,1,0:T(8,128)(2,1)S(1)}, bf16[8,64,128]{2,1,0:T(8,128)(2,1)S(1)}, u32[]{:S(2)}, u32[]{:S(2)}) collective-permute-start(bf16[8,64,128]{2,1,0:T(8,128)(2,1)S(1)} %shard_map.30.own), channel_id=1, source_target_pairs={{0,24},{1,25},{2,26},{3,27},{4,28},{5,29},{6,30},{7,31},{8,0},{9,1... | collective-permute-start | bytes 393224 | tf_op jit(solution)/shard_map/ppermute | solution.py:196
  23.2 2.3 %collective-permute-start.4 = (bf16[8,64,128]{2,1,0:T(8,128)(2,1)S(1)}, bf16[8,64,128]{2,1,0:T(8,128)(2,1)S(1)}, u32[]{:S(2)}, u32[]{:S(2)}) collective-permute-start(bf16[8,64,128]{2,1,0:T(8,128)(2,1)S(1)} %shard_map.30.own), channel_id=1, source_target_pairs={{0,8},{1,9},{2,10},{3,11},{4,12},{5,13},{6,14},{7,15},{8,16},{9,17... | collective-permute-start | bytes 393224 | tf_op jit(solution)/shard_map/ppermute | solution.py:196
  25.5 0.7 %collective-permute-done.8.far = bf16[2,512,128]{2,1,0:T(8,128)(2,1)S(1)} collective-permute-done((bf16[2,512,128]{2,1,0:T(8,128)(2,1)S(1)}, bf16[2,512,128]{2,1,0:T(8,128)(2,1)S(1)}, u32[]{:S(2)}, u32[]{:S(2)}) %collective-permute-start.8) | collective-permute-done | bytes 262176 | tf_op jit(solution)/shard_map/ppermute | solution.py:18
  26.2 0.0 collective-permute-done.7.near_swapped
  26.2 0.1 shard_map.32.padded
  26.4 1.0 %shard_map.33.so_far = f32[512,256]{1,0:T(8,128)S(1)} custom-call(bf16[8,64,128]{2,1,0:T(8,128)(2,1)S(1)} %shard_map.30.own, bf16[8,576,128]{2,1,0:T(8,128)(2,1)S(1)} %shard_map.32.padded), custom_call_target="tpu_custom_call" | custom-call | flops 603979776 | bytes 1048576 | tf_op jit(solution)/shard_map/pallas_call | solution.py:170
  27.3 0.0 collective-permute-done.10.response
  27.3 1.0 %shard_map.34.so_far = f32[512,256]{1,0:T(8,128)S(1)} custom-call(bf16[8,64,128]{2,1,0:T(8,128)(2,1)S(1)} %collective-permute-done.10.response, bf16[8,576,128]{2,1,0:T(8,128)(2,1)S(1)} %shard_map.32.padded, f32[512,256]{1,0:T(8,128)S(1)} %shard_map.33.so_far), custom_call_target="tpu_custom_call" | custom-call | flops 603979776 | bytes 1048576 | tf_op jit(solution)/shard_map/pallas_call | solution.py:170
  28.3 0.2 collective-permute-done.9.response
  28.4 0.9 %shard_map.35.so_far = f32[512,256]{1,0:T(8,128)S(1)} custom-call(bf16[8,64,128]{2,1,0:T(8,128)(2,1)S(1)} %collective-permute-done.9.response, bf16[8,576,128]{2,1,0:T(8,128)(2,1)S(1)} %shard_map.32.padded, f32[512,256]{1,0:T(8,128)S(1)} %shard_map.34.so_far), custom_call_target="tpu_custom_call" | custom-call | flops 603979776 | bytes 1048576 | tf_op jit(solution)/shard_map/pallas_call | solution.py:170
  29.4 0.1 collective-permute-done.4.outward
  29.5 2.0 %shard_map.36 = bf16[32,8,512]{2,1,0:T(8,128)(2,1)} custom-call(bf16[8,64,128]{2,1,0:T(8,128)(2,1)S(1)} %collective-permute-done.4.outward, bf16[8,576,128]{2,1,0:T(8,128)(2,1)S(1)} %shard_map.32.padded, f32[512,256]{1,0:T(8,128)S(1)} %shard_map.35.so_far), custom_call_target="tpu_custom_call" | custom-call | flops 603979776 | bytes 1048576 | tf_op jit(solution)/shard_map/pallas_call | solution.py:170
  (3 shorter events, 0.0 us)
Async XLA Ops:
  0.0 4.4 %collective-permute-start.5 = (bf16[16,8,512]{2,1,0:T(8,128)(2,1)}, bf16[16,8,512]{2,1,0:T(8,128)(2,1)S(1)}, u32[]{:S(2)}, u32[]{:S(2)}) collective-permute-start(bf16[16,8,512]{2,1,0:T(8,128)(2,1)} %own.1), channel_id=1, source_target_pairs={{0,32},{32,0},{64,96},{96,64},{128,160},{160,128},{192,224},{224,1... | collective-permute-start | bytes 393224 | tf_op jit(solution)/shard_map/ppermute | solution.py:18
  3.2 0.8 %copy-start.1 = (bf16[32,4,64]{2,1,0:T(4,128)(2,1)S(1)}, bf16[32,4,64]{2,1,0:T(4,128)(2,1)}, u32[]{:S(2)}) copy-start(bf16[32,4,64]{2,1,0:T(4,128)(2,1)} %param.2) | copy-start | bytes 49156
  4.2 4.0 %collective-permute-start = (bf16[1,64,128]{2,1,0:T(8,128)(2,1)S(1)}, bf16[1,64,128]{2,1,0:T(8,128)(2,1)S(1)}, u32[]{:S(2)}, u32[]{:S(2)}) collective-permute-start(bf16[1,64,128]{2,1,0:T(8,128)(2,1)S(1)} %bitcast.2), channel_id=1, source_target_pairs={{0,1},{1,0},{2,3},{3,2},{4,5},{5,4},{6,7},{7,6},{8,9},{9,8},{10,11... | collective-permute-start | bytes 49160 | tf_op jit(solution)/shard_map/ppermute | solution.py:18
  4.4 0.9 %copy-start = (bf16[16,8,512]{2,1,0:T(8,128)(2,1)S(1)}, bf16[16,8,512]{2,1,0:T(8,128)(2,1)}, u32[]{:S(2)}) copy-start(bf16[16,8,512]{2,1,0:T(8,128)(2,1)} %own.1) | copy-start | bytes 393220
  6.0 11.5 %collective-permute-start.6 = (bf16[2,512,128]{2,1,0:T(8,128)(2,1)S(1)}, bf16[2,512,128]{2,1,0:T(8,128)(2,1)S(1)}, u32[]{:S(2)}, u32[]{:S(2)}) collective-permute-start(bf16[2,512,128]{2,1,0:T(8,128)(2,1)S(1)} %shard_map.31.own), channel_id=1, source_target_pairs={{0,64},{32,224},{64,128},{96,32},{128,192},{160,96},{192,0},{224,1... | collective-permute-start | bytes 786440 | tf_op jit(solution)/shard_map/ppermute | solution.py:18
  8.3 11.6 %collective-permute-start.1 = (bf16[2,64,128]{2,1,0:T(8,128)(2,1)S(1)}, bf16[2,64,128]{2,1,0:T(8,128)(2,1)S(1)}, u32[]{:S(2)}, u32[]{:S(2)}) collective-permute-start(bf16[2,64,128]{2,1,0:T(8,128)(2,1)S(1)} %shard_map.29.blocks_0_), channel_id=1, source_target_pairs={{0,5},{1,4},{2,7},{3,6},{4,1},{5,0},{6,3},{7,2},{8,13},{9,12},{10,... | collective-permute-start | bytes 98312 | tf_op jit(solution)/shard_map/ppermute | solution.py:18
  13.8 6.0 %collective-permute-start.2 = (bf16[2,64,128]{2,1,0:T(8,128)(2,1)S(1)}, bf16[2,64,128]{2,1,0:T(8,128)(2,1)S(1)}, u32[]{:S(2)}, u32[]{:S(2)}) collective-permute-start(bf16[2,64,128]{2,1,0:T(8,128)(2,1)S(1)} %shard_map.29.blocks_0_), channel_id=1, source_target_pairs={{0,6},{1,3},{2,0},{3,5},{4,2},{5,7},{6,4},{7,1},{8,14},{9,11},{10,... | collective-permute-start | bytes 98312 | tf_op jit(solution)/shard_map/ppermute | solution.py:18
  13.8 6.0 %collective-permute-start.3 = (bf16[2,64,128]{2,1,0:T(8,128)(2,1)S(1)}, bf16[2,64,128]{2,1,0:T(8,128)(2,1)S(1)}, u32[]{:S(2)}, u32[]{:S(2)}) collective-permute-start(bf16[2,64,128]{2,1,0:T(8,128)(2,1)S(1)} %shard_map.29.blocks_0_), channel_id=1, source_target_pairs={{0,7},{1,2},{2,1},{3,4},{4,3},{5,6},{6,5},{7,0},{8,15},{9,10},{10,... | collective-permute-start | bytes 98312 | tf_op jit(solution)/shard_map/ppermute | solution.py:18
  16.9 9.3 %collective-permute-start.8 = (bf16[2,512,128]{2,1,0:T(8,128)(2,1)S(1)}, bf16[2,512,128]{2,1,0:T(8,128)(2,1)S(1)}, u32[]{:S(2)}, u32[]{:S(2)}) collective-permute-start(bf16[2,512,128]{2,1,0:T(8,128)(2,1)S(1)} %shard_map.31.own), channel_id=1, source_target_pairs={{0,128},{32,160},{64,192},{96,224},{128,0},{160,32},{192,64},{224,... | collective-permute-start | bytes 786440 | tf_op jit(solution)/shard_map/ppermute | solution.py:18
  17.5 8.8 %collective-permute-start.7 = (bf16[2,512,128]{2,1,0:T(8,128)(2,1)S(1)}, bf16[2,512,128]{2,1,0:T(8,128)(2,1)S(1)}, u32[]{:S(2)}, u32[]{:S(2)}) collective-permute-start(bf16[2,512,128]{2,1,0:T(8,128)(2,1)S(1)} %collective-permute-done.6.near), channel_id=1, source_target_pairs={{0,32},{32,0},{64,96},{96,64},{128,160},{160,128},{192,224},{224,1... | collective-permute-start | bytes 786440 | tf_op jit(solution)/shard_map/ppermute | solution.py:18
  19.8 7.5 %collective-permute-start.10 = (bf16[8,64,128]{2,1,0:T(8,128)(2,1)S(1)}, bf16[8,64,128]{2,1,0:T(8,128)(2,1)S(1)}, u32[]{:S(2)}, u32[]{:S(2)}) collective-permute-start(bf16[8,64,128]{2,1,0:T(8,128)(2,1)S(1)} %shard_map.30.own), channel_id=1, source_target_pairs={{0,16},{1,17},{2,18},{3,19},{4,20},{5,21},{6,22},{7,23},{8,24},{9,... | collective-permute-start | bytes 393224 | tf_op jit(solution)/shard_map/ppermute | solution.py:18
  22.8 5.6 %collective-permute-start.9 = (bf16[8,64,128]{2,1,0:T(8,128)(2,1)S(1)}, bf16[8,64,128]{2,1,0:T(8,128)(2,1)S(1)}, u32[]{:S(2)}, u32[]{:S(2)}) collective-permute-start(bf16[8,64,128]{2,1,0:T(8,128)(2,1)S(1)} %shard_map.30.own), channel_id=1, source_target_pairs={{0,24},{1,25},{2,26},{3,27},{4,28},{5,29},{6,30},{7,31},{8,0},{9,1... | collective-permute-start | bytes 393224 | tf_op jit(solution)/shard_map/ppermute | solution.py:196
  23.2 6.3 %collective-permute-start.4 = (bf16[8,64,128]{2,1,0:T(8,128)(2,1)S(1)}, bf16[8,64,128]{2,1,0:T(8,128)(2,1)S(1)}, u32[]{:S(2)}, u32[]{:S(2)}) collective-permute-start(bf16[8,64,128]{2,1,0:T(8,128)(2,1)S(1)} %shard_map.30.own), channel_id=1, source_target_pairs={{0,8},{1,9},{2,10},{3,11},{4,12},{5,13},{6,14},{7,15},{8,16},{9,17... | collective-permute-start | bytes 393224 | tf_op jit(solution)/shard_map/ppermute | solution.py:196

commit v15 on v14

--- a/solution.py
+++ b/solution.py
@@ -92,7 +92,7 @@
     return slot
 
 
-def add_products(offset, response, padded, band, rows_f32, so_far, total):
+def operands(offset, response, padded, band, rows_f32):
     rcv = lax.axis_index("rcv")
     y, z = rcv // 8, rcv % 8
     slots = [position_of((sign(z) * (wanted - z) + 64) % 8) for wanted in range(8)]
@@ -123,16 +123,16 @@
                     for late in range(2):
                         first = (2 * step - late + 1) * 128
                         rows.append(band[half, :, first : first + 256])
-    even = jnp.dot(
-        jnp.concatenate(sides, axis=1),
-        jnp.concatenate(even_rows, axis=0),
-        preferred_element_type=jnp.float32,
-    )
-    odd = jnp.dot(
-        jnp.concatenate(sides[:8], axis=1),
-        jnp.concatenate(odd_rows, axis=0),
-        preferred_element_type=jnp.float32,
-    )
+    return jnp.concatenate(sides, axis=1), jnp.concatenate(even_rows, axis=0), jnp.concatenate(odd_rows, axis=0)
+
+
+def dot(left, right):
+    return jnp.dot(left, right, preferred_element_type=jnp.float32)
+
+
+def add_products(offset, response, padded, band, rows, so_far, total):
+    sides, even_rows, odd_rows = operands(offset, response, padded, band, rows)
+    even, odd = dot(sides, even_rows), dot(sides[:, :1024], odd_rows)
     if so_far is None:
         total[:8, :] = even[:8, :]
         total[8:, :] = even[8:, :] + odd[:504, :]
@@ -149,21 +149,29 @@
     add_products(offset, response, padded, band, rows, so_far, total)
 
 
-def last_kernel(outward, padded, so_far, out, band, rows, total, placed):
-    add_products(1, outward, padded, band, rows, so_far, total)
-    turned = total[...].astype(jnp.bfloat16).T
-    turned = turned.astype(jnp.bfloat16)
-    skewed = [pltpu.roll(turned[u * 32 : u * 32 + 32, :], u, 1) for u in range(8)]
-    lane = lax.broadcasted_iota(jnp.int32, (32, 512), 1)
-    for r in range(8):
-        mixed = skewed[0]
-        for u in range(1, 8):
-            mixed = jnp.where(lane % 8 == (r + u) % 8, skewed[u], mixed)
-        mixed = pltpu.roll(mixed, (512 - r) % 512, 1)
-        for part in range(4):
-            placed[part, pl.ds(r, 32, stride=8), :] = mixed[:, part * 128 : part * 128 + 128].astype(jnp.float32)
-    for part in range(4):
-        out[:, :, part * 128 : part * 128 + 128] = placed[part].reshape(32, 8, 128).astype(jnp.bfloat16)
+def last_kernel(outward, padded, so_far, out, band, rows, placed):
+    sides, even_rows, odd_rows = operands(1, outward, padded, band, rows)
+    lane = lax.broadcasted_iota(jnp.int32, (32, 256), 1)
+    carried = jnp.zeros((8, 256), jnp.float32)
+    for half in range(2):
+        left = sides[half * 256 : half * 256 + 256, :]
+        even, odd = dot(left, even_rows), dot(left[:, :1024], odd_rows)
+        shifted = jnp.concatenate([carried, odd[:248, :]], axis=0)
+        carried = odd[248:, :]
+        total = so_far[half * 256 : half * 256 + 256, :] + even + shifted
+        turned = total.astype(jnp.bfloat16).T
+        skewed = [pltpu.roll(turned[u * 32 : u * 32 + 32, :], u, 1) for u in range(8)]
+        for r in range(8):
+            mixed = skewed[0]
+            for u in range(1, 8):
+                mixed = jnp.where(lane % 8 == (r + u) % 8, skewed[u], mixed)
+            mixed = pltpu.roll(mixed, (256 - r) % 256, 1)
+            for part in range(2):
+                lanes = mixed[:, part * 128 : part * 128 + 128].astype(jnp.float32)
+                placed[half * 2 + part, pl.ds(r, 32, stride=8), :] = lanes
+        for part in range(half * 2, half * 2 + 2):
+            block = placed[part].reshape(32, 8, 128).astype(jnp.bfloat16)
+            out[:, :, part * 128 : part * 128 + 128] = block
 
 
 def call(body, shape, dtype, operands, scratch, flops=0):
@@ -233,7 +241,7 @@
     padded = call(assemble, (8, 576, 128), bf16, pieces, [])
     work = 2 * 512 * 256 * 9 * 256
     total = call(first_kernel, (512, 256), f32, (held, padded), band, work)
-    for offset, block in ((2, across), (-1, inward)):
+    for offset, block in ((-1, inward), (2, across)):
         body = functools.partial(middle_kernel, offset)
         total = call(body, (512, 256), f32, (block, padded, total), band, work)
     return call(
@@ -241,7 +249,7 @@
         (32, 8, 512),
         bf16,
         (outward, padded, total),
-        band + [((512, 256), f32), ((4, 256, 128), f32)],
+        band + [((4, 256, 128), f32)],
         work,
     )
 

time: 31.8 us -> 32.8 us (1.031)
  the two profiles are of different devices: /device:TPU:1 before, /device:TPU:24 now
where the time goes in v15:
time: 32.8 us; the launch traced here: 32.6 us
  starting transfers between devices  19.7 us (60%)
  Pallas kernels  5.8 us (18%)
  waiting for transfers between devices  5.35 us (16%)
  local copies, waits for them, and re-layouts  1.66 us (5%)
    ppermute x9, starting transfers between devices, spread(): return lax.ppermute(value, axis, [(i, partner(i)) for i in range(size)])  16.7 us
    pallas_call x9, Pallas kernels, call(): pl.pallas_call(body, out_shape=jax.ShapeDtypeStruct(shape, dtype), in_spe...  5.8 us
    ppermute x9, waiting for transfers between devices, spread(): return lax.ppermute(value, axis, [(i, partner(i)) for i in range(size)])  3.4 us
    ppermute x2, starting transfers between devices, by_core(): return lax.ppermute(value, ('shot', 'rcv'), pairs)  3 us
    ppermute x2, waiting for transfers between devices, by_core(): return lax.ppermute(value, ('shot', 'rcv'), pairs)  1.96 us
    unnamed x4, local copies, waits for them, and re-layouts  1.66 us
  transfers between devices with their start and end apart: 11, of which 3 were waited for; matrix products, arithmetic and copies ran while one was open for 0% of the time, Pallas kernels for 12%

profile of v15, /device:TPU:24, one launch (start us, length us, event | category | flops | bytes accessed | tf_op | source)
XLA Modules:
  0.0 32.6 jit_solution(13909419854053117137)
XLA Ops:
  0.0 0.0 collective-permute-start.5
  0.0 0.0 copy-start.1
  0.0 0.8 %copy-done.1 = bf16[32,4,64]{2,1,0:T(4,128)(2,1)S(1)} copy-done((bf16[32,4,64]{2,1,0:T(4,128)(2,1)S(1)}, bf16[32,4,64]{2,1,0:T(4,128)(2,1)}, u32[]{:S(2)}) %copy-start.1) | copy-done | bytes 16408
  0.8 0.2 shard_map.28
  1.0 2.0 %collective-permute-start = (bf16[1,64,128]{2,1,0:T(8,128)(2,1)S(1)}, bf16[1,64,128]{2,1,0:T(8,128)(2,1)S(1)}, u32[]{:S(2)}, u32[]{:S(2)}) collective-permute-start(bf16[1,64,128]{2,1,0:T(8,128)(2,1)S(1)} %bitcast.2), channel_id=1, source_target_pairs={{0,1},{1,0},{2,3},{3,2},{4,5},{5,4},{6,7},{7,6},{8,9},{9,8},{10,11... | collective-permute-start | bytes 49160 | tf_op jit(solution)/shard_map/ppermute | solution.py:18
  3.0 0.0 collective-permute-done.5.other
  3.0 0.9 %copy-done = bf16[16,8,512]{2,1,0:T(8,128)(2,1)S(1)} copy-done((bf16[16,8,512]{2,1,0:T(8,128)(2,1)S(1)}, bf16[16,8,512]{2,1,0:T(8,128)(2,1)}, u32[]{:S(2)}) %copy-start) | copy-done | bytes 131096
  3.9 0.6 %shard_map.31.own = bf16[2,512,128]{2,1,0:T(8,128)(2,1)S(1)} custom-call(bf16[16,8,512]{2,1,0:T(8,128)(2,1)S(1)} %copy-done, bf16[16,8,512]{2,1,0:T(8,128)(2,1)S(1)} %collective-permute-done.5.other, bf16[1,64,128]{2,1,0:T(8,128)(2,1)S(1)} %bitcast.3), custom_call_target="tpu_custom_call" | custom-call | bytes 1048576 | tf_op jit(solution)/shard_map/pallas_call | solution.py:178
  4.5 1.6 %collective-permute-start.6 = (bf16[2,512,128]{2,1,0:T(8,128)(2,1)S(1)}, bf16[2,512,128]{2,1,0:T(8,128)(2,1)S(1)}, u32[]{:S(2)}, u32[]{:S(2)}) collective-permute-start(bf16[2,512,128]{2,1,0:T(8,128)(2,1)S(1)} %shard_map.31.own), channel_id=1, source_target_pairs={{0,64},{32,224},{64,128},{96,32},{128,192},{160,96},{192,0},{224,1... | collective-permute-start | bytes 786440 | tf_op jit(solution)/shard_map/ppermute | solution.py:18
  6.0 0.0 collective-permute-done.blocks_1_
  6.0 5.8 %collective-permute-start.1 = (bf16[2,64,128]{2,1,0:T(8,128)(2,1)S(1)}, bf16[2,64,128]{2,1,0:T(8,128)(2,1)S(1)}, u32[]{:S(2)}, u32[]{:S(2)}) collective-permute-start(bf16[2,64,128]{2,1,0:T(8,128)(2,1)S(1)} %shard_map.29.blocks_0_), channel_id=1, source_target_pairs={{0,5},{1,4},{2,7},{3,6},{4,1},{5,0},{6,3},{7,2},{8,13},{9,12},{10,... | collective-permute-start | bytes 98312 | tf_op jit(solution)/shard_map/ppermute | solution.py:18
  11.9 0.2 collective-permute-start.2
  12.1 3.5 %collective-permute-start.3 = (bf16[2,64,128]{2,1,0:T(8,128)(2,1)S(1)}, bf16[2,64,128]{2,1,0:T(8,128)(2,1)S(1)}, u32[]{:S(2)}, u32[]{:S(2)}) collective-permute-start(bf16[2,64,128]{2,1,0:T(8,128)(2,1)S(1)} %shard_map.29.blocks_0_), channel_id=1, source_target_pairs={{0,7},{1,2},{2,1},{3,4},{4,3},{5,6},{6,5},{7,0},{8,15},{9,10},{10,... | collective-permute-start | bytes 98312 | tf_op jit(solution)/shard_map/ppermute | solution.py:18
  15.6 2.7 %collective-permute-start.8 = (bf16[2,512,128]{2,1,0:T(8,128)(2,1)S(1)}, bf16[2,512,128]{2,1,0:T(8,128)(2,1)S(1)}, u32[]{:S(2)}, u32[]{:S(2)}) collective-permute-start(bf16[2,512,128]{2,1,0:T(8,128)(2,1)S(1)} %shard_map.31.own), channel_id=1, source_target_pairs={{0,128},{32,160},{64,192},{96,224},{128,0},{160,32},{192,64},{224,... | collective-permute-start | bytes 786440 | tf_op jit(solution)/shard_map/ppermute | solution.py:18
  18.3 0.0 collective-permute-done.6.near
  18.3 0.0 collective-permute-start.7
  18.3 0.0 collective-permute-done.1.blocks_1_
  18.3 0.0 collective-permute-done.2.blocks_2_
  18.3 0.2 collective-permute-done.3.blocks_3_
  18.5 0.8 %collective-permute-start.10 = (bf16[8,64,128]{2,1,0:T(8,128)(2,1)S(1)}, bf16[8,64,128]{2,1,0:T(8,128)(2,1)S(1)}, u32[]{:S(2)}, u32[]{:S(2)}) collective-permute-start(bf16[8,64,128]{2,1,0:T(8,128)(2,1)S(1)} %shard_map.30.own), channel_id=1, source_target_pairs={{0,24},{1,25},{2,26},{3,27},{4,28},{5,29},{6,30},{7,31},{8,0},{9,1... | collective-permute-start | bytes 393224 | tf_op jit(solution)/shard_map/ppermute | solution.py:204
  19.3 0.9 %collective-permute-start.9 = (bf16[8,64,128]{2,1,0:T(8,128)(2,1)S(1)}, bf16[8,64,128]{2,1,0:T(8,128)(2,1)S(1)}, u32[]{:S(2)}, u32[]{:S(2)}) collective-permute-start(bf16[8,64,128]{2,1,0:T(8,128)(2,1)S(1)} %shard_map.30.own), channel_id=1, source_target_pairs={{0,16},{1,17},{2,18},{3,19},{4,20},{5,21},{6,22},{7,23},{8,24},{9,... | collective-permute-start | bytes 393224 | tf_op jit(solution)/shard_map/ppermute | solution.py:18
  20.3 2.2 %collective-permute-start.4 = (bf16[8,64,128]{2,1,0:T(8,128)(2,1)S(1)}, bf16[8,64,128]{2,1,0:T(8,128)(2,1)S(1)}, u32[]{:S(2)}, u32[]{:S(2)}) collective-permute-start(bf16[8,64,128]{2,1,0:T(8,128)(2,1)S(1)} %shard_map.30.own), channel_id=1, source_target_pairs={{0,8},{1,9},{2,10},{3,11},{4,12},{5,13},{6,14},{7,15},{8,16},{9,17... | collective-permute-start | bytes 393224 | tf_op jit(solution)/shard_map/ppermute | solution.py:204
  22.4 3.2 %collective-permute-done.8.far = bf16[2,512,128]{2,1,0:T(8,128)(2,1)S(1)} collective-permute-done((bf16[2,512,128]{2,1,0:T(8,128)(2,1)S(1)}, bf16[2,512,128]{2,1,0:T(8,128)(2,1)S(1)}, u32[]{:S(2)}, u32[]{:S(2)}) %collective-permute-start.8) | collective-permute-done | bytes 262176 | tf_op jit(solution)/shard_map/ppermute | solution.py:18
  25.7 0.0 collective-permute-done.7.near_swapped
  25.7 0.1 shard_map.32.padded
  25.8 1.0 %shard_map.33.so_far = f32[512,256]{1,0:T(8,128)S(1)} custom-call(bf16[8,64,128]{2,1,0:T(8,128)(2,1)S(1)} %shard_map.30.own, bf16[8,576,128]{2,1,0:T(8,128)(2,1)S(1)} %shard_map.32.padded), custom_call_target="tpu_custom_call" | custom-call | flops 603979776 | bytes 1048576 | tf_op jit(solution)/shard_map/pallas_call | solution.py:178
  26.8 2.0 %collective-permute-done.10.response = bf16[8,64,128]{2,1,0:T(8,128)(2,1)S(1)} collective-permute-done((bf16[8,64,128]{2,1,0:T(8,128)(2,1)S(1)}, bf16[8,64,128]{2,1,0:T(8,128)(2,1)S(1)}, u32[]{:S(2)}, u32[]{:S(2)}) %collective-permute-start.10) | collective-permute-done | bytes 131104 | tf_op jit(solution)/shard_map/ppermute | solution.py:204
  28.7 0.9 %shard_map.34.so_far = f32[512,256]{1,0:T(8,128)S(1)} custom-call(bf16[8,64,128]{2,1,0:T(8,128)(2,1)S(1)} %collective-permute-done.10.response, bf16[8,576,128]{2,1,0:T(8,128)(2,1)S(1)} %shard_map.32.padded, f32[512,256]{1,0:T(8,128)S(1)} %shard_map.33.so_far), custom_call_target="tpu_custom_call" | custom-call | flops 603979776 | bytes 1048576 | tf_op jit(solution)/shard_map/pallas_call | solution.py:178
  29.7 0.0 collective-permute-done.9.response
  29.7 1.0 %shard_map.35.so_far = f32[512,256]{1,0:T(8,128)S(1)} custom-call(bf16[8,64,128]{2,1,0:T(8,128)(2,1)S(1)} %collective-permute-done.9.response, bf16[8,576,128]{2,1,0:T(8,128)(2,1)S(1)} %shard_map.32.padded, f32[512,256]{1,0:T(8,128)S(1)} %shard_map.34.so_far), custom_call_target="tpu_custom_call" | custom-call | flops 603979776 | bytes 1048576 | tf_op jit(solution)/shard_map/pallas_call | solution.py:178
  30.6 0.0 collective-permute-done.4.outward
  30.6 2.0 %shard_map.36 = bf16[32,8,512]{2,1,0:T(8,128)(2,1)} custom-call(bf16[8,64,128]{2,1,0:T(8,128)(2,1)S(1)} %collective-permute-done.4.outward, bf16[8,576,128]{2,1,0:T(8,128)(2,1)S(1)} %shard_map.32.padded, f32[512,256]{1,0:T(8,128)S(1)} %shard_map.35.so_far), custom_call_target="tpu_custom_call" | custom-call | flops 603979776 | bytes 1048576 | tf_op jit(solution)/shard_map/pallas_call | solution.py:178
  (3 shorter events, 0.0 us)
Async XLA Ops:
  0.0 3.0 %collective-permute-start.5 = (bf16[16,8,512]{2,1,0:T(8,128)(2,1)}, bf16[16,8,512]{2,1,0:T(8,128)(2,1)S(1)}, u32[]{:S(2)}, u32[]{:S(2)}) collective-permute-start(bf16[16,8,512]{2,1,0:T(8,128)(2,1)} %own.1), channel_id=1, source_target_pairs={{0,32},{32,0},{64,96},{96,64},{128,160},{160,128},{192,224},{224,1... | collective-permute-start | bytes 393224 | tf_op jit(solution)/shard_map/ppermute | solution.py:18
  0.0 0.8 %copy-start.1 = (bf16[32,4,64]{2,1,0:T(4,128)(2,1)S(1)}, bf16[32,4,64]{2,1,0:T(4,128)(2,1)}, u32[]{:S(2)}) copy-start(bf16[32,4,64]{2,1,0:T(4,128)(2,1)} %param.2) | copy-start | bytes 49156
  1.0 5.1 %collective-permute-start = (bf16[1,64,128]{2,1,0:T(8,128)(2,1)S(1)}, bf16[1,64,128]{2,1,0:T(8,128)(2,1)S(1)}, u32[]{:S(2)}, u32[]{:S(2)}) collective-permute-start(bf16[1,64,128]{2,1,0:T(8,128)(2,1)S(1)} %bitcast.2), channel_id=1, source_target_pairs={{0,1},{1,0},{2,3},{3,2},{4,5},{5,4},{6,7},{7,6},{8,9},{9,8},{10,11... | collective-permute-start | bytes 49160 | tf_op jit(solution)/shard_map/ppermute | solution.py:18
  3.0 0.9 %copy-start = (bf16[16,8,512]{2,1,0:T(8,128)(2,1)S(1)}, bf16[16,8,512]{2,1,0:T(8,128)(2,1)}, u32[]{:S(2)}) copy-start(bf16[16,8,512]{2,1,0:T(8,128)(2,1)} %own.1) | copy-start | bytes 393220
  4.5 13.8 %collective-permute-start.6 = (bf16[2,512,128]{2,1,0:T(8,128)(2,1)S(1)}, bf16[2,512,128]{2,1,0:T(8,128)(2,1)S(1)}, u32[]{:S(2)}, u32[]{:S(2)}) collective-permute-start(bf16[2,512,128]{2,1,0:T(8,128)(2,1)S(1)} %shard_map.31.own), channel_id=1, source_target_pairs={{0,64},{32,224},{64,128},{96,32},{128,192},{160,96},{192,0},{224,1... | collective-permute-start | bytes 786440 | tf_op jit(solution)/shard_map/ppermute | solution.py:18
  6.0 12.3 %collective-permute-start.1 = (bf16[2,64,128]{2,1,0:T(8,128)(2,1)S(1)}, bf16[2,64,128]{2,1,0:T(8,128)(2,1)S(1)}, u32[]{:S(2)}, u32[]{:S(2)}) collective-permute-start(bf16[2,64,128]{2,1,0:T(8,128)(2,1)S(1)} %shard_map.29.blocks_0_), channel_id=1, source_target_pairs={{0,5},{1,4},{2,7},{3,6},{4,1},{5,0},{6,3},{7,2},{8,13},{9,12},{10,... | collective-permute-start | bytes 98312 | tf_op jit(solution)/shard_map/ppermute | solution.py:18
  11.9 6.4 %collective-permute-start.2 = (bf16[2,64,128]{2,1,0:T(8,128)(2,1)S(1)}, bf16[2,64,128]{2,1,0:T(8,128)(2,1)S(1)}, u32[]{:S(2)}, u32[]{:S(2)}) collective-permute-start(bf16[2,64,128]{2,1,0:T(8,128)(2,1)S(1)} %shard_map.29.blocks_0_), channel_id=1, source_target_pairs={{0,6},{1,3},{2,0},{3,5},{4,2},{5,7},{6,4},{7,1},{8,14},{9,11},{10,... | collective-permute-start | bytes 98312 | tf_op jit(solution)/shard_map/ppermute | solution.py:18
  12.1 6.4 %collective-permute-start.3 = (bf16[2,64,128]{2,1,0:T(8,128)(2,1)S(1)}, bf16[2,64,128]{2,1,0:T(8,128)(2,1)S(1)}, u32[]{:S(2)}, u32[]{:S(2)}) collective-permute-start(bf16[2,64,128]{2,1,0:T(8,128)(2,1)S(1)} %shard_map.29.blocks_0_), channel_id=1, source_target_pairs={{0,7},{1,2},{2,1},{3,4},{4,3},{5,6},{6,5},{7,0},{8,15},{9,10},{10,... | collective-permute-start | bytes 98312 | tf_op jit(solution)/shard_map/ppermute | solution.py:18
  15.6 10.1 %collective-permute-start.8 = (bf16[2,512,128]{2,1,0:T(8,128)(2,1)S(1)}, bf16[2,512,128]{2,1,0:T(8,128)(2,1)S(1)}, u32[]{:S(2)}, u32[]{:S(2)}) collective-permute-start(bf16[2,512,128]{2,1,0:T(8,128)(2,1)S(1)} %shard_map.31.own), channel_id=1, source_target_pairs={{0,128},{32,160},{64,192},{96,224},{128,0},{160,32},{192,64},{224,... | collective-permute-start | bytes 786440 | tf_op jit(solution)/shard_map/ppermute | solution.py:18
  18.3 7.4 %collective-permute-start.7 = (bf16[2,512,128]{2,1,0:T(8,128)(2,1)S(1)}, bf16[2,512,128]{2,1,0:T(8,128)(2,1)S(1)}, u32[]{:S(2)}, u32[]{:S(2)}) collective-permute-start(bf16[2,512,128]{2,1,0:T(8,128)(2,1)S(1)} %collective-permute-done.6.near), channel_id=1, source_target_pairs={{0,32},{32,0},{64,96},{96,64},{128,160},{160,128},{192,224},{224,1... | collective-permute-start | bytes 786440 | tf_op jit(solution)/shard_map/ppermute | solution.py:18
  18.5 10.2 %collective-permute-start.10 = (bf16[8,64,128]{2,1,0:T(8,128)(2,1)S(1)}, bf16[8,64,128]{2,1,0:T(8,128)(2,1)S(1)}, u32[]{:S(2)}, u32[]{:S(2)}) collective-permute-start(bf16[8,64,128]{2,1,0:T(8,128)(2,1)S(1)} %shard_map.30.own), channel_id=1, source_target_pairs={{0,24},{1,25},{2,26},{3,27},{4,28},{5,29},{6,30},{7,31},{8,0},{9,1... | collective-permute-start | bytes 393224 | tf_op jit(solution)/shard_map/ppermute | solution.py:204
  19.3 10.4 %collective-permute-start.9 = (bf16[8,64,128]{2,1,0:T(8,128)(2,1)S(1)}, bf16[8,64,128]{2,1,0:T(8,128)(2,1)S(1)}, u32[]{:S(2)}, u32[]{:S(2)}) collective-permute-start(bf16[8,64,128]{2,1,0:T(8,128)(2,1)S(1)} %shard_map.30.own), channel_id=1, source_target_pairs={{0,16},{1,17},{2,18},{3,19},{4,20},{5,21},{6,22},{7,23},{8,24},{9,... | collective-permute-start | bytes 393224 | tf_op jit(solution)/shard_map/ppermute | solution.py:18
  20.3 10.4 %collective-permute-start.4 = (bf16[8,64,128]{2,1,0:T(8,128)(2,1)S(1)}, bf16[8,64,128]{2,1,0:T(8,128)(2,1)S(1)}, u32[]{:S(2)}, u32[]{:S(2)}) collective-permute-start(bf16[8,64,128]{2,1,0:T(8,128)(2,1)S(1)} %shard_map.30.own), channel_id=1, source_target_pairs={{0,8},{1,9},{2,10},{3,11},{4,12},{5,13},{6,14},{7,15},{8,16},{9,17... | collective-permute-start | bytes 393224 | tf_op jit(solution)/shard_map/ppermute | solution.py:204

commit v16 on v15

--- a/solution.py
+++ b/solution.py
@@ -149,8 +149,8 @@
     add_products(offset, response, padded, band, rows, so_far, total)
 
 
-def last_kernel(outward, padded, so_far, out, band, rows, placed):
-    sides, even_rows, odd_rows = operands(1, outward, padded, band, rows)
+def last_kernel(second, padded, so_far, out, band, rows, placed):
+    sides, even_rows, odd_rows = operands(-1, second, padded, band, rows)
     lane = lax.broadcasted_iota(jnp.int32, (32, 256), 1)
     carried = jnp.zeros((8, 256), jnp.float32)
     for half in range(2):
@@ -233,7 +233,7 @@
     ]
     held = call(join, (8, 64, 128), bf16, (held, *arrived), [], JOIN_COST)
     across = spread(held, "rcv", along_y(2))
-    outward, inward = by_core(held, 1), by_core(held, -1)
+    second, first = by_core(held, -1), by_core(held, 1)
 
     near = spread(both, "shot", along_x)
     far = spread(both, "shot", across_x)
@@ -241,14 +241,14 @@
     padded = call(assemble, (8, 576, 128), bf16, pieces, [])
     work = 2 * 512 * 256 * 9 * 256
     total = call(first_kernel, (512, 256), f32, (held, padded), band, work)
-    for offset, block in ((-1, inward), (2, across)):
+    for offset, block in ((2, across), (1, first)):
         body = functools.partial(middle_kernel, offset)
         total = call(body, (512, 256), f32, (block, padded, total), band, work)
     return call(
         last_kernel,
         (32, 8, 512),
         bf16,
-        (outward, padded, total),
+        (second, padded, total),
         band + [((4, 256, 128), f32)],
         work,
     )

time: 32.8 us -> 32.6 us (level)
  the two profiles are of different devices: /device:TPU:24 before, /device:TPU:1 now
where the time goes in v16:
time: 32.6 us; the launch traced here: 32.5 us
  starting transfers between devices  21.6 us (66%)
  Pallas kernels  5.8 us (18%)
  waiting for transfers between devices  3.32 us (10%)
  local copies, waits for them, and re-layouts  1.66 us (5%)
    ppermute x9, starting transfers between devices, spread(): return lax.ppermute(value, axis, [(i, partner(i)) for i in range(size)])  20.1 us
    pallas_call x9, Pallas kernels, call(): pl.pallas_call(body, out_shape=jax.ShapeDtypeStruct(shape, dtype), in_spe...  5.8 us
    ppermute x9, waiting for transfers between devices, spread(): return lax.ppermute(value, axis, [(i, partner(i)) for i in range(size)])  2.07 us
    unnamed x4, local copies, waits for them, and re-layouts  1.66 us
    ppermute x2, starting transfers between devices, by_core(): return lax.ppermute(value, ('shot', 'rcv'), pairs)  1.47 us
    ppermute x2, waiting for transfers between devices, by_core(): return lax.ppermute(value, ('shot', 'rcv'), pairs)  1.25 us
  transfers between devices with their start and end apart: 11, of which 3 were waited for; matrix products, arithmetic and copies ran while one was open for 0% of the time, Pallas kernels for 12%

profile of v16, /device:TPU:1, one launch (start us, length us, event | category | flops | bytes accessed | tf_op | source)
XLA Modules:
  0.0 32.5 jit_solution(8098581375484976947)
XLA Ops:
  0.0 3.2 %collective-permute-start.5 = (bf16[16,8,512]{2,1,0:T(8,128)(2,1)}, bf16[16,8,512]{2,1,0:T(8,128)(2,1)S(1)}, u32[]{:S(2)}, u32[]{:S(2)}) collective-permute-start(bf16[16,8,512]{2,1,0:T(8,128)(2,1)} %own.1), channel_id=1, source_target_pairs={{0,32},{32,0},{64,96},{96,64},{128,160},{160,128},{192,224},{224,1... | collective-permute-start | bytes 393224 | tf_op jit(solution)/shard_map/ppermute | solution.py:18
  3.2 0.0 copy-start.1
  3.2 0.8 %copy-done.1 = bf16[32,4,64]{2,1,0:T(4,128)(2,1)S(1)} copy-done((bf16[32,4,64]{2,1,0:T(4,128)(2,1)S(1)}, bf16[32,4,64]{2,1,0:T(4,128)(2,1)}, u32[]{:S(2)}) %copy-start.1) | copy-done | bytes 16408
  4.0 0.2 shard_map.28
  4.2 0.1 collective-permute-start
  4.3 0.2 collective-permute-done.5.other
  4.4 0.9 %copy-done = bf16[16,8,512]{2,1,0:T(8,128)(2,1)S(1)} copy-done((bf16[16,8,512]{2,1,0:T(8,128)(2,1)S(1)}, bf16[16,8,512]{2,1,0:T(8,128)(2,1)}, u32[]{:S(2)}) %copy-start) | copy-done | bytes 131096
  5.3 0.6 %shard_map.31.own = bf16[2,512,128]{2,1,0:T(8,128)(2,1)S(1)} custom-call(bf16[16,8,512]{2,1,0:T(8,128)(2,1)S(1)} %copy-done, bf16[16,8,512]{2,1,0:T(8,128)(2,1)S(1)} %collective-permute-done.5.other, bf16[1,64,128]{2,1,0:T(8,128)(2,1)S(1)} %bitcast.3), custom_call_target="tpu_custom_call" | custom-call | bytes 1048576 | tf_op jit(solution)/shard_map/pallas_call | solution.py:178
  6.0 2.3 %collective-permute-start.6 = (bf16[2,512,128]{2,1,0:T(8,128)(2,1)S(1)}, bf16[2,512,128]{2,1,0:T(8,128)(2,1)S(1)}, u32[]{:S(2)}, u32[]{:S(2)}) collective-permute-start(bf16[2,512,128]{2,1,0:T(8,128)(2,1)S(1)} %shard_map.31.own), channel_id=1, source_target_pairs={{0,64},{32,224},{64,128},{96,32},{128,192},{160,96},{192,0},{224,1... | collective-permute-start | bytes 786440 | tf_op jit(solution)/shard_map/ppermute | solution.py:18
  8.2 0.0 collective-permute-done.blocks_1_
  8.3 5.6 %collective-permute-start.1 = (bf16[2,64,128]{2,1,0:T(8,128)(2,1)S(1)}, bf16[2,64,128]{2,1,0:T(8,128)(2,1)S(1)}, u32[]{:S(2)}, u32[]{:S(2)}) collective-permute-start(bf16[2,64,128]{2,1,0:T(8,128)(2,1)S(1)} %shard_map.29.blocks_0_), channel_id=1, source_target_pairs={{0,5},{1,4},{2,7},{3,6},{4,1},{5,0},{6,3},{7,2},{8,13},{9,12},{10,... | collective-permute-start | bytes 98312 | tf_op jit(solution)/shard_map/ppermute | solution.py:18
  13.8 0.0 collective-permute-start.2
  13.8 3.1 %collective-permute-start.3 = (bf16[2,64,128]{2,1,0:T(8,128)(2,1)S(1)}, bf16[2,64,128]{2,1,0:T(8,128)(2,1)S(1)}, u32[]{:S(2)}, u32[]{:S(2)}) collective-permute-start(bf16[2,64,128]{2,1,0:T(8,128)(2,1)S(1)} %shard_map.29.blocks_0_), channel_id=1, source_target_pairs={{0,7},{1,2},{2,1},{3,4},{4,3},{5,6},{6,5},{7,0},{8,15},{9,10},{10,... | collective-permute-start | bytes 98312 | tf_op jit(solution)/shard_map/ppermute | solution.py:18
  16.9 0.5 %collective-permute-start.8 = (bf16[2,512,128]{2,1,0:T(8,128)(2,1)S(1)}, bf16[2,512,128]{2,1,0:T(8,128)(2,1)S(1)}, u32[]{:S(2)}, u32[]{:S(2)}) collective-permute-start(bf16[2,512,128]{2,1,0:T(8,128)(2,1)S(1)} %shard_map.31.own), channel_id=1, source_target_pairs={{0,128},{32,160},{64,192},{96,224},{128,0},{160,32},{192,64},{224,... | collective-permute-start | bytes 786440 | tf_op jit(solution)/shard_map/ppermute | solution.py:18
  17.5 0.0 collective-permute-done.6.near
  17.5 2.3 %collective-permute-start.7 = (bf16[2,512,128]{2,1,0:T(8,128)(2,1)S(1)}, bf16[2,512,128]{2,1,0:T(8,128)(2,1)S(1)}, u32[]{:S(2)}, u32[]{:S(2)}) collective-permute-start(bf16[2,512,128]{2,1,0:T(8,128)(2,1)S(1)} %collective-permute-done.6.near), channel_id=1, source_target_pairs={{0,32},{32,0},{64,96},{96,64},{128,160},{160,128},{192,224},{224,1... | collective-permute-start | bytes 786440 | tf_op jit(solution)/shard_map/ppermute | solution.py:18
  19.8 0.0 collective-permute-done.1.blocks_1_
  19.8 0.0 collective-permute-done.2.blocks_2_
  19.8 0.0 collective-permute-done.3.blocks_3_
  19.8 3.0 %collective-permute-start.10 = (bf16[8,64,128]{2,1,0:T(8,128)(2,1)S(1)}, bf16[8,64,128]{2,1,0:T(8,128)(2,1)S(1)}, u32[]{:S(2)}, u32[]{:S(2)}) collective-permute-start(bf16[8,64,128]{2,1,0:T(8,128)(2,1)S(1)} %shard_map.30.own), channel_id=1, source_target_pairs={{0,16},{1,17},{2,18},{3,19},{4,20},{5,21},{6,22},{7,23},{8,24},{9,... | collective-permute-start | bytes 393224 | tf_op jit(solution)/shard_map/ppermute | solution.py:18
  22.8 0.8 %collective-permute-start.9 = (bf16[8,64,128]{2,1,0:T(8,128)(2,1)S(1)}, bf16[8,64,128]{2,1,0:T(8,128)(2,1)S(1)}, u32[]{:S(2)}, u32[]{:S(2)}) collective-permute-start(bf16[8,64,128]{2,1,0:T(8,128)(2,1)S(1)} %shard_map.30.own), channel_id=1, source_target_pairs={{0,8},{1,9},{2,10},{3,11},{4,12},{5,13},{6,14},{7,15},{8,16},{9,17... | collective-permute-start | bytes 393224 | tf_op jit(solution)/shard_map/ppermute | solution.py:204
  23.6 0.7 %collective-permute-start.4 = (bf16[8,64,128]{2,1,0:T(8,128)(2,1)S(1)}, bf16[8,64,128]{2,1,0:T(8,128)(2,1)S(1)}, u32[]{:S(2)}, u32[]{:S(2)}) collective-permute-start(bf16[8,64,128]{2,1,0:T(8,128)(2,1)S(1)} %shard_map.30.own), channel_id=1, source_target_pairs={{0,24},{1,25},{2,26},{3,27},{4,28},{5,29},{6,30},{7,31},{8,0},{9,1... | collective-permute-start | bytes 393224 | tf_op jit(solution)/shard_map/ppermute | solution.py:204
  24.3 1.9 %collective-permute-done.8.far = bf16[2,512,128]{2,1,0:T(8,128)(2,1)S(1)} collective-permute-done((bf16[2,512,128]{2,1,0:T(8,128)(2,1)S(1)}, bf16[2,512,128]{2,1,0:T(8,128)(2,1)S(1)}, u32[]{:S(2)}, u32[]{:S(2)}) %collective-permute-start.8) | collective-permute-done | bytes 262176 | tf_op jit(solution)/shard_map/ppermute | solution.py:18
  26.2 0.0 collective-permute-done.7.near_swapped
  26.2 0.1 shard_map.32.padded
  26.4 1.0 %shard_map.33.so_far = f32[512,256]{1,0:T(8,128)S(1)} custom-call(bf16[8,64,128]{2,1,0:T(8,128)(2,1)S(1)} %shard_map.30.own, bf16[8,576,128]{2,1,0:T(8,128)(2,1)S(1)} %shard_map.32.padded), custom_call_target="tpu_custom_call" | custom-call | flops 603979776 | bytes 1048576 | tf_op jit(solution)/shard_map/pallas_call | solution.py:178
  27.3 0.0 collective-permute-done.10.response
  27.3 1.0 %shard_map.34.so_far = f32[512,256]{1,0:T(8,128)S(1)} custom-call(bf16[8,64,128]{2,1,0:T(8,128)(2,1)S(1)} %collective-permute-done.10.response, bf16[8,576,128]{2,1,0:T(8,128)(2,1)S(1)} %shard_map.32.padded, f32[512,256]{1,0:T(8,128)S(1)} %shard_map.33.so_far), custom_call_target="tpu_custom_call" | custom-call | flops 603979776 | bytes 1048576 | tf_op jit(solution)/shard_map/pallas_call | solution.py:178
  28.3 1.2 %collective-permute-done.9.response = bf16[8,64,128]{2,1,0:T(8,128)(2,1)S(1)} collective-permute-done((bf16[8,64,128]{2,1,0:T(8,128)(2,1)S(1)}, bf16[8,64,128]{2,1,0:T(8,128)(2,1)S(1)}, u32[]{:S(2)}, u32[]{:S(2)}) %collective-permute-start.9) | collective-permute-done | bytes 131104 | tf_op jit(solution)/shard_map/ppermute | solution.py:204
  29.5 0.9 %shard_map.35.so_far = f32[512,256]{1,0:T(8,128)S(1)} custom-call(bf16[8,64,128]{2,1,0:T(8,128)(2,1)S(1)} %collective-permute-done.9.response, bf16[8,576,128]{2,1,0:T(8,128)(2,1)S(1)} %shard_map.32.padded, f32[512,256]{1,0:T(8,128)S(1)} %shard_map.34.so_far), custom_call_target="tpu_custom_call" | custom-call | flops 603979776 | bytes 1048576 | tf_op jit(solution)/shard_map/pallas_call | solution.py:178
  30.5 0.0 collective-permute-done.4.second
  30.5 2.0 %shard_map.36 = bf16[32,8,512]{2,1,0:T(8,128)(2,1)} custom-call(bf16[8,64,128]{2,1,0:T(8,128)(2,1)S(1)} %collective-permute-done.4.second, bf16[8,576,128]{2,1,0:T(8,128)(2,1)S(1)} %shard_map.32.padded, f32[512,256]{1,0:T(8,128)S(1)} %shard_map.35.so_far), custom_call_target="tpu_custom_call" | custom-call | flops 603979776 | bytes 1048576 | tf_op jit(solution)/shard_map/pallas_call | solution.py:178
  (3 shorter events, 0.0 us)
Async XLA Ops:
  0.0 4.4 %collective-permute-start.5 = (bf16[16,8,512]{2,1,0:T(8,128)(2,1)}, bf16[16,8,512]{2,1,0:T(8,128)(2,1)S(1)}, u32[]{:S(2)}, u32[]{:S(2)}) collective-permute-start(bf16[16,8,512]{2,1,0:T(8,128)(2,1)} %own.1), channel_id=1, source_target_pairs={{0,32},{32,0},{64,96},{96,64},{128,160},{160,128},{192,224},{224,1... | collective-permute-start | bytes 393224 | tf_op jit(solution)/shard_map/ppermute | solution.py:18
  3.2 0.8 %copy-start.1 = (bf16[32,4,64]{2,1,0:T(4,128)(2,1)S(1)}, bf16[32,4,64]{2,1,0:T(4,128)(2,1)}, u32[]{:S(2)}) copy-start(bf16[32,4,64]{2,1,0:T(4,128)(2,1)} %param.2) | copy-start | bytes 49156
  4.2 4.0 %collective-permute-start = (bf16[1,64,128]{2,1,0:T(8,128)(2,1)S(1)}, bf16[1,64,128]{2,1,0:T(8,128)(2,1)S(1)}, u32[]{:S(2)}, u32[]{:S(2)}) collective-permute-start(bf16[1,64,128]{2,1,0:T(8,128)(2,1)S(1)} %bitcast.2), channel_id=1, source_target_pairs={{0,1},{1,0},{2,3},{3,2},{4,5},{5,4},{6,7},{7,6},{8,9},{9,8},{10,11... | collective-permute-start | bytes 49160 | tf_op jit(solution)/shard_map/ppermute | solution.py:18
  4.4 0.9 %copy-start = (bf16[16,8,512]{2,1,0:T(8,128)(2,1)S(1)}, bf16[16,8,512]{2,1,0:T(8,128)(2,1)}, u32[]{:S(2)}) copy-start(bf16[16,8,512]{2,1,0:T(8,128)(2,1)} %own.1) | copy-start | bytes 393220
  6.0 11.5 %collective-permute-start.6 = (bf16[2,512,128]{2,1,0:T(8,128)(2,1)S(1)}, bf16[2,512,128]{2,1,0:T(8,128)(2,1)S(1)}, u32[]{:S(2)}, u32[]{:S(2)}) collective-permute-start(bf16[2,512,128]{2,1,0:T(8,128)(2,1)S(1)} %shard_map.31.own), channel_id=1, source_target_pairs={{0,64},{32,224},{64,128},{96,32},{128,192},{160,96},{192,0},{224,1... | collective-permute-start | bytes 786440 | tf_op jit(solution)/shard_map/ppermute | solution.py:18
  8.3 11.6 %collective-permute-start.1 = (bf16[2,64,128]{2,1,0:T(8,128)(2,1)S(1)}, bf16[2,64,128]{2,1,0:T(8,128)(2,1)S(1)}, u32[]{:S(2)}, u32[]{:S(2)}) collective-permute-start(bf16[2,64,128]{2,1,0:T(8,128)(2,1)S(1)} %shard_map.29.blocks_0_), channel_id=1, source_target_pairs={{0,5},{1,4},{2,7},{3,6},{4,1},{5,0},{6,3},{7,2},{8,13},{9,12},{10,... | collective-permute-start | bytes 98312 | tf_op jit(solution)/shard_map/ppermute | solution.py:18
  13.8 6.0 %collective-permute-start.2 = (bf16[2,64,128]{2,1,0:T(8,128)(2,1)S(1)}, bf16[2,64,128]{2,1,0:T(8,128)(2,1)S(1)}, u32[]{:S(2)}, u32[]{:S(2)}) collective-permute-start(bf16[2,64,128]{2,1,0:T(8,128)(2,1)S(1)} %shard_map.29.blocks_0_), channel_id=1, source_target_pairs={{0,6},{1,3},{2,0},{3,5},{4,2},{5,7},{6,4},{7,1},{8,14},{9,11},{10,... | collective-permute-start | bytes 98312 | tf_op jit(solution)/shard_map/ppermute | solution.py:18
  13.8 6.0 %collective-permute-start.3 = (bf16[2,64,128]{2,1,0:T(8,128)(2,1)S(1)}, bf16[2,64,128]{2,1,0:T(8,128)(2,1)S(1)}, u32[]{:S(2)}, u32[]{:S(2)}) collective-permute-start(bf16[2,64,128]{2,1,0:T(8,128)(2,1)S(1)} %shard_map.29.blocks_0_), channel_id=1, source_target_pairs={{0,7},{1,2},{2,1},{3,4},{4,3},{5,6},{6,5},{7,0},{8,15},{9,10},{10,... | collective-permute-start | bytes 98312 | tf_op jit(solution)/shard_map/ppermute | solution.py:18
  16.9 9.3 %collective-permute-start.8 = (bf16[2,512,128]{2,1,0:T(8,128)(2,1)S(1)}, bf16[2,512,128]{2,1,0:T(8,128)(2,1)S(1)}, u32[]{:S(2)}, u32[]{:S(2)}) collective-permute-start(bf16[2,512,128]{2,1,0:T(8,128)(2,1)S(1)} %shard_map.31.own), channel_id=1, source_target_pairs={{0,128},{32,160},{64,192},{96,224},{128,0},{160,32},{192,64},{224,... | collective-permute-start | bytes 786440 | tf_op jit(solution)/shard_map/ppermute | solution.py:18
  17.5 8.8 %collective-permute-start.7 = (bf16[2,512,128]{2,1,0:T(8,128)(2,1)S(1)}, bf16[2,512,128]{2,1,0:T(8,128)(2,1)S(1)}, u32[]{:S(2)}, u32[]{:S(2)}) collective-permute-start(bf16[2,512,128]{2,1,0:T(8,128)(2,1)S(1)} %collective-permute-done.6.near), channel_id=1, source_target_pairs={{0,32},{32,0},{64,96},{96,64},{128,160},{160,128},{192,224},{224,1... | collective-permute-start | bytes 786440 | tf_op jit(solution)/shard_map/ppermute | solution.py:18
  19.8 7.5 %collective-permute-start.10 = (bf16[8,64,128]{2,1,0:T(8,128)(2,1)S(1)}, bf16[8,64,128]{2,1,0:T(8,128)(2,1)S(1)}, u32[]{:S(2)}, u32[]{:S(2)}) collective-permute-start(bf16[8,64,128]{2,1,0:T(8,128)(2,1)S(1)} %shard_map.30.own), channel_id=1, source_target_pairs={{0,16},{1,17},{2,18},{3,19},{4,20},{5,21},{6,22},{7,23},{8,24},{9,... | collective-permute-start | bytes 393224 | tf_op jit(solution)/shard_map/ppermute | solution.py:18
  22.8 6.7 %collective-permute-start.9 = (bf16[8,64,128]{2,1,0:T(8,128)(2,1)S(1)}, bf16[8,64,128]{2,1,0:T(8,128)(2,1)S(1)}, u32[]{:S(2)}, u32[]{:S(2)}) collective-permute-start(bf16[8,64,128]{2,1,0:T(8,128)(2,1)S(1)} %shard_map.30.own), channel_id=1, source_target_pairs={{0,8},{1,9},{2,10},{3,11},{4,12},{5,13},{6,14},{7,15},{8,16},{9,17... | collective-permute-start | bytes 393224 | tf_op jit(solution)/shard_map/ppermute | solution.py:204
  23.6 6.9 %collective-permute-start.4 = (bf16[8,64,128]{2,1,0:T(8,128)(2,1)S(1)}, bf16[8,64,128]{2,1,0:T(8,128)(2,1)S(1)}, u32[]{:S(2)}, u32[]{:S(2)}) collective-permute-start(bf16[8,64,128]{2,1,0:T(8,128)(2,1)S(1)} %shard_map.30.own), channel_id=1, source_target_pairs={{0,24},{1,25},{2,26},{3,27},{4,28},{5,29},{6,30},{7,31},{8,0},{9,1... | collective-permute-start | bytes 393224 | tf_op jit(solution)/shard_map/ppermute | solution.py:204
